TPU v7x, 1024 devices: a whole 4x8x16 slice. The times are simulated.
1024 devices in a mesh: row: 128 (over z, x, core), col: 8 (over y).
Axes of the slice: x: 4, y: 8, z: 16, core: 2. Of those that a mesh axis runs over, the one named last changes fastest.
Arguments:
- features: bfloat16 [131072, 256], P(('row', 'col')), may hold values from -6 to 6
- self_weight: bfloat16 [256, 256], replicated, may hold values from -0.375 to 0.375
- neigh_weight: bfloat16 [256, 256], replicated, may hold values from -0.375 to 0.375
- tiles: bfloat16 [128, 8, 16, 128, 128], P('row', 'col'), may hold values from 0 to 1
- tile_rows: int32 [128, 8, 16], P('row', 'col'), may hold values from 0 to 7
- tile_bands: int32 [128, 8, 16], P('row', 'col'), may hold values from 0 to 4
- tile_count: int32 [128, 8], P('row', 'col'), may hold values from 1 to 16, as said below
- degree: int32 [131072], P(('row', 'col')), may hold values from 16 to 96
- cotangent: bfloat16 [131072, 256], P(('row', 'col')), may hold values from -6 to 6
Outputs:
- output: bfloat16 [131072, 256], P(('row', 'col'))
- feature_grad: bfloat16 [131072, 256], P(('row', 'col'))
- self_grad: float32 [256, 256], replicated
- neigh_grad: float32 [256, 256], replicated
Inputs may be any that keep to these rules, and one draw needn't show every extreme that they name: `tile_count`: some device uses all 16 slots.
All inputs are finite; a program needn't handle non-finite values.
Results may differ from a plain program's by a relative error of at most 0.017.
Values may be sent and summed in bfloat16 or wider, within the bound.
No kernel may reach another device: no remote copies, remote signals or barrier semaphores. Data moves between devices by JAX's collectives and lax.ppermute only.
A program may use at most 32 MiB of HBM per device.

v0:
```python
import math

import jax
import jax.numpy as jnp
from jax import lax
from jax.sharding import PartitionSpec as P

HALO = 2


def passed_along(value, axis, steps):
    count = lax.axis_size(axis)
    leading, last = (max(0, -steps), min(count, count - steps))
    return lax.ppermute(value, axis, [(source, source + steps) for source in range(leading, last)])


def fetch_block(features, offset):
    return passed_along(features, "row", -offset)


def relay_far(piece, offset):
    return passed_along(piece, "row", offset)


def fold_split(form, picker, values):
    upper = values.astype(jnp.bfloat16)
    lower = (values - upper.astype(jnp.float32)).astype(jnp.bfloat16)
    return jnp.einsum(form, picker, upper, preferred_element_type=jnp.float32) + jnp.einsum(
        form, picker, lower, preferred_element_type=jnp.float32
    )


def run_slots(work, slots):
    return work(0, slots)


def local(
    features, self_weight, neigh_weight, tiles, tile_rows, tile_bands, tile_count, degree, cotangent
):
    ncol = lax.axis_size("col")
    wide = 2 * HALO + 1
    blk, width = features.shape
    slots = tiles.shape[2]
    tile_set = tiles[0, 0]
    rows_all = tile_rows[0, 0]
    bands_all = tile_bands[0, 0]
    count = tile_count[0, 0]
    live_all = jnp.arange(slots, dtype=jnp.int32) < count
    column_ids = jnp.arange(ncol, dtype=jnp.int32)
    offset_ids = jnp.arange(wide, dtype=jnp.int32)
    pieces = []
    for offset in range(-HALO, HALO + 1):
        pieces.append(features if offset == 0 else fetch_block(features, offset))
    window = jnp.stack(pieces, 0)

    def take():
        band_pick = (bands_all[:, None] == offset_ids[None, :]) & live_all[:, None]
        row_pick = (rows_all[:, None] == column_ids[None, :]) & live_all[:, None]
        return (tile_set, band_pick, row_pick)

    def forward_work(start, amount):
        tile_part, band_pick, row_pick = take()
        source = jnp.einsum(
            "tw,wbf->tbf",
            band_pick.astype(jnp.bfloat16),
            window,
            preferred_element_type=jnp.float32,
        ).astype(jnp.bfloat16)
        product = jnp.einsum("tab,tbf->taf", tile_part, source, preferred_element_type=jnp.float32)
        return fold_split("ti,taf->iaf", row_pick.astype(jnp.bfloat16), product)

    partial_sums = run_slots(forward_work, slots)
    sums = lax.psum_scatter(
        partial_sums.reshape(ncol * blk, width).astype(jnp.bfloat16),
        "col",
        scatter_dimension=0,
        tiled=True,
    ).astype(jnp.float32)
    norm = degree.astype(jnp.float32)[:, None]
    aggregate = (sums / norm).astype(jnp.bfloat16)
    output = (
        jnp.dot(features, self_weight, preferred_element_type=jnp.float32)
        + jnp.dot(aggregate, neigh_weight, preferred_element_type=jnp.float32)
    ).astype(jnp.bfloat16)
    scaled = (jnp.dot(cotangent, neigh_weight.T, preferred_element_type=jnp.float32) / norm).astype(
        jnp.bfloat16
    )
    band_scaled = lax.all_gather(scaled, "col", axis=0, tiled=True).reshape(ncol, blk, width)

    def backward_work(start, amount):
        tile_part, band_pick, row_pick = take()
        chosen = jnp.einsum(
            "ti,iaf->taf",
            row_pick.astype(jnp.bfloat16),
            band_scaled,
            preferred_element_type=jnp.float32,
        ).astype(jnp.bfloat16)
        contrib = jnp.einsum("tab,taf->tbf", tile_part, chosen, preferred_element_type=jnp.float32)
        return fold_split("tw,tbf->wbf", band_pick.astype(jnp.bfloat16), contrib)

    landed = run_slots(backward_work, slots)
    landed_half = landed.astype(jnp.bfloat16)
    spread = landed_half[HALO].astype(jnp.float32)
    for offset in range(-HALO, HALO + 1):
        if offset != 0:
            spread = spread + relay_far(landed_half[HALO + offset], offset).astype(jnp.float32)
    feature_grad = (
        jnp.dot(cotangent, self_weight.T, preferred_element_type=jnp.float32) + spread
    ).astype(jnp.bfloat16)
    local_self = lax.dot_general(
        features, cotangent, (((0,), (0,)), ((), ())), preferred_element_type=jnp.float32
    )
    local_neigh = lax.dot_general(
        aggregate, cotangent, (((0,), (0,)), ((), ())), preferred_element_type=jnp.float32
    )
    self_sum, neigh_sum = lax.psum((local_self, local_neigh), ("row", "col"))
    factor = 1.0 / math.sqrt(lax.axis_size("row") * ncol * blk)
    return (output, feature_grad, self_sum * factor, neigh_sum * factor)


def solution(mesh):
    in_specs = (
        P(("row", "col"), None),
        P(),
        P(),
        P("row", "col", None, None, None),
        P("row", "col", None),
        P("row", "col", None),
        P("row", "col"),
        P(("row", "col")),
        P(("row", "col"), None),
    )
    out_specs = (P(("row", "col"), None), P(("row", "col"), None), P(), P())
    return jax.shard_map(local, mesh=mesh, in_specs=in_specs, out_specs=out_specs, check_vma=False)
```

profile of v0, /device:TPU:1, one launch (start us, length us, event | category | flops | bytes accessed | tf_op | source)
XLA Modules:
  0.0 614.0 jit_solution(13235259324775860247)
XLA Ops:
  7.2 0.0 copy-start
  7.2 0.0 reduce-scatter.2.cloned.1.call-start
  7.2 4.1 collective-permute-start
  11.3 4.0 collective-permute-start.1
  15.3 10.7 %collective-permute-start.2 = (bf16[128,256]{1,0:T(8,128)(2,1)}, bf16[128,256]{1,0:T(8,128)(2,1)S(1)}, u32[]{:S(2)}, u32[]{:S(2)}) collective-permute-start(bf16[128,256]{1,0:T(8,128)(2,1)} %param.9), channel_id=1, source_target_pairs={{8,0},{16,8},{24,16},{32,24},{40,32},{48,40},{56,48},{64,56},{72,6... | collective-permute-start | bytes 196616 | tf_op jit(solution)/shard_map/ppermute | solution.py:14
  26.0 1.3 collective-permute-start.3
  28.0 0.7 convert_element_type.80
  28.7 1.1 fusion.4
  29.8 19.7 %all_gather.3 = bf16[1024,256]{1,0:T(8,128)(2,1)S(1)} all-gather(bf16[128,256]{1,0:T(8,128)(2,1)S(1)} %fusion.4), channel_id=1, replica_groups=mesh['row'=128,'col'=8] {'col'}, dimensions={0}, use_global_device_ids=true | all-gather | bytes 589824 | tf_op jit(solution)/shard_map/all_gather | solution.py:88
  49.5 0.5 fusion.12
  50.1 1.0 copy.29
  51.1 1.4 fusion
  52.5 1.9 copy.23
  54.4 1.3 fusion.25
  55.7 1.7 copy.22
  57.4 0.0 collective-permute-done
  57.4 0.0 collective-permute-done.1
  57.5 0.5 fusion.14
  58.0 1.0 copy.27
  59.0 1.4 fusion.1
  60.4 1.9 copy.19
  62.3 1.3 fusion.32
  63.6 0.9 copy.20
  64.5 1.5 fusion.2
  66.0 0.9 copy.21
  66.9 0.0 reduce-scatter.2.cloned.1.call-update
  67.0 0.0 all-reduce.3.cloned.1.call-start
  67.0 0.4 copy-done.2
  67.4 0.3 fusion.27
  67.7 0.5 copy-done.1
  68.3 0.4 fusion.9
  68.7 1.3 collective-permute-start.4
  70.0 7.1 %collective-permute-start.5 = (bf16[128,256]{1,0:T(8,128)(2,1)S(1)}, bf16[128,256]{1,0:T(8,128)(2,1)S(1)}, u32[]{:S(2)}, u32[]{:S(2)}) collective-permute-start(bf16[128,256]{1,0:T(8,128)(2,1)S(1)} %get-tuple-element.13), channel_id=1, source_target_pairs={{8,0},{16,8},{24,16},{32,24},{40,32},{48,40},{56,48},{64,56},{72,6... | collective-permute-start | bytes 196616 | tf_op jit(solution)/shard_map/ppermute | solution.py:14
  77.1 4.9 collective-permute-start.6
  82.0 3.6 collective-permute-start.7
  85.6 0.2 fusion.47
  85.8 0.0 copy-start.8
  85.8 0.9 fusion.48
  86.7 27.7 %reduce-scatter.2.cloned.1.call-done = bf16[128,256]{1,0:T(8,128)(2,1)} async-done(((bf16[1024,256]{1,0:T(8,128)(2,1)}), bf16[128,256]{1,0:T(8,128)(2,1)}) %reduce-scatter.2.cloned.1.call-update) | async-done | bytes 65552 | tf_op jit(solution)/shard_map/reduce_scatter | solution.py:73
  114.4 1.9 fusion.46
  116.3 0.0 all-reduce.3.cloned.1.call-update
  116.3 0.0 collective-permute-done.4
  116.3 0.0 collective-permute-done.5
  116.4 0.0 collective-permute-done.7
  116.4 0.8 fusion.20
  117.2 0.9 fusion.3
  118.1 487.2 %all-reduce.3.cloned.1.call-done = (f32[256,256]{1,0:T(8,128)}, f32[256,256]{1,0:T(8,128)}) async-done(((f32[256,256]{1,0:T(8,128)}, f32[256,256]{1,0:T(8,128)}), (f32[256,256]{1,0:T(8,128)}, f32[256,256]{1,0:T(8,128)})) %all-reduce.3.cloned.1.call-update) | async-done | bytes 524304 | tf_op jit(solution)/shard_map/psum | solution.py:116
  605.3 1.9 broadcast_multiply_fusion
  (26 shorter events, 0.1 us)
Async XLA Ops:
  7.2 43.9 %copy-start = (bf16[1,1,16,128,128]{4,3,2,1,0:T(8,128)(2,1)S(1)}, bf16[1,1,16,128,128]{4,3,2,1,0:T(8,128)(2,1)}, u32[]{:S(2)}) copy-start(bf16[1,1,16,128,128]{4,3,2,1,0:T(8,128)(2,1)} %param.12) | copy-start | bytes 1572868
  7.2 42.4 %copy-start.6 = (s32[1,1,16]{2,1,0:T(1,128)S(1)}, s32[1,1,16]{2,1,0:T(1,128)}, u32[]{:S(2)}) copy-start(s32[1,1,16]{2,1,0:T(1,128)} %param.13) | copy-start | bytes 196
  7.2 107.2 %reduce-scatter.2.cloned.1.call-start = ((), (), s32[]{:S(2)}) async-start(), calls=%async_computation.1 | async-start | bytes 589824 | tf_op jit(solution)/shard_map/reduce_scatter | solution.py:73
  7.2 50.1 %collective-permute-start = (bf16[128,256]{1,0:T(8,128)(2,1)}, bf16[128,256]{1,0:T(8,128)(2,1)S(1)}, u32[]{:S(2)}, u32[]{:S(2)}) collective-permute-start(bf16[128,256]{1,0:T(8,128)(2,1)} %param.9), channel_id=1, source_target_pairs={{0,16},{8,24},{16,32},{24,40},{32,48},{40,56},{48,64},{56,72},{64,... | collective-permute-start | bytes 196616 | tf_op jit(solution)/shard_map/ppermute | solution.py:14
  11.3 46.0 %collective-permute-start.1 = (bf16[128,256]{1,0:T(8,128)(2,1)}, bf16[128,256]{1,0:T(8,128)(2,1)S(1)}, u32[]{:S(2)}, u32[]{:S(2)}) collective-permute-start(bf16[128,256]{1,0:T(8,128)(2,1)} %param.9), channel_id=1, source_target_pairs={{0,8},{8,16},{16,24},{24,32},{32,40},{40,48},{48,56},{56,64},{64,7... | collective-permute-start | bytes 196616 | tf_op jit(solution)/shard_map/ppermute | solution.py:14
  15.3 42.1 %collective-permute-start.2 = (bf16[128,256]{1,0:T(8,128)(2,1)}, bf16[128,256]{1,0:T(8,128)(2,1)S(1)}, u32[]{:S(2)}, u32[]{:S(2)}) collective-permute-start(bf16[128,256]{1,0:T(8,128)(2,1)} %param.9), channel_id=1, source_target_pairs={{8,0},{16,8},{24,16},{32,24},{40,32},{48,40},{56,48},{64,56},{72,6... | collective-permute-start | bytes 196616 | tf_op jit(solution)/shard_map/ppermute | solution.py:14
  26.0 31.4 %collective-permute-start.3 = (bf16[128,256]{1,0:T(8,128)(2,1)}, bf16[128,256]{1,0:T(8,128)(2,1)S(1)}, u32[]{:S(2)}, u32[]{:S(2)}) collective-permute-start(bf16[128,256]{1,0:T(8,128)(2,1)} %param.9), channel_id=1, source_target_pairs={{16,0},{24,8},{32,16},{40,24},{48,32},{56,40},{64,48},{72,56},{80,... | collective-permute-start | bytes 196616 | tf_op jit(solution)/shard_map/ppermute | solution.py:14
  52.5 1.9 copy-start.7
  55.7 1.7 copy-start.3
  66.0 1.4 copy-start.2
  67.0 1.3 copy-start.1
  67.0 538.3 %all-reduce.3.cloned.1.call-start = ((), (), s32[]{:S(2)}) async-start(), calls=%async_computation.2 | async-start | bytes 1048576 | tf_op jit(solution)/shard_map/psum | solution.py:116
  68.3 17.4 %copy-start.4 = (bf16[256,256]{1,0:T(8,128)(2,1)S(1)}, bf16[256,256]{1,0:T(8,128)(2,1)}, u32[]{:S(2)}) copy-start(bf16[256,256]{1,0:T(8,128)(2,1)} %param.10) | copy-start | bytes 393220
  68.3 17.5 %copy-start.5 = (bf16[128,256]{1,0:T(8,128)(2,1)S(1)}, bf16[128,256]{1,0:T(8,128)(2,1)}, u32[]{:S(2)}) copy-start(bf16[128,256]{1,0:T(8,128)(2,1)} %param.17) | copy-start | bytes 196612
  68.7 47.6 %collective-permute-start.4 = (bf16[128,256]{1,0:T(8,128)(2,1)S(1)}, bf16[128,256]{1,0:T(8,128)(2,1)S(1)}, u32[]{:S(2)}, u32[]{:S(2)}) collective-permute-start(bf16[128,256]{1,0:T(8,128)(2,1)S(1)} %get-tuple-element.10), channel_id=1, source_target_pairs={{16,0},{24,8},{32,16},{40,24},{48,32},{56,40},{64,48},{72,56},{80,... | collective-permute-start | bytes 196616 | tf_op jit(solution)/shard_map/ppermute | solution.py:14
  70.0 46.4 %collective-permute-start.5 = (bf16[128,256]{1,0:T(8,128)(2,1)S(1)}, bf16[128,256]{1,0:T(8,128)(2,1)S(1)}, u32[]{:S(2)}, u32[]{:S(2)}) collective-permute-start(bf16[128,256]{1,0:T(8,128)(2,1)S(1)} %get-tuple-element.13), channel_id=1, source_target_pairs={{8,0},{16,8},{24,16},{32,24},{40,32},{48,40},{56,48},{64,56},{72,6... | collective-permute-start | bytes 196616 | tf_op jit(solution)/shard_map/ppermute | solution.py:14
  77.1 39.2 %collective-permute-start.6 = (bf16[128,256]{1,0:T(8,128)(2,1)S(1)}, bf16[128,256]{1,0:T(8,128)(2,1)S(1)}, u32[]{:S(2)}, u32[]{:S(2)}) collective-permute-start(bf16[128,256]{1,0:T(8,128)(2,1)S(1)} %get-tuple-element.12), channel_id=1, source_target_pairs={{0,8},{8,16},{16,24},{24,32},{32,40},{40,48},{48,56},{56,64},{64,7... | collective-permute-start | bytes 196616 | tf_op jit(solution)/shard_map/ppermute | solution.py:14
  82.0 34.4 %collective-permute-start.7 = (bf16[128,256]{1,0:T(8,128)(2,1)S(1)}, bf16[128,256]{1,0:T(8,128)(2,1)S(1)}, u32[]{:S(2)}, u32[]{:S(2)}) collective-permute-start(bf16[128,256]{1,0:T(8,128)(2,1)S(1)} %get-tuple-element.11), channel_id=1, source_target_pairs={{0,16},{8,24},{16,32},{24,40},{32,48},{40,56},{48,64},{56,72},{64,... | collective-permute-start | bytes 196616 | tf_op jit(solution)/shard_map/ppermute | solution.py:14
  85.8 31.4 %copy-start.8 = (bf16[256,256]{1,0:T(8,128)(2,1)S(1)}, bf16[256,256]{1,0:T(8,128)(2,1)}, u32[]{:S(2)}) copy-start(bf16[256,256]{1,0:T(8,128)(2,1)} %param.11) | copy-start | bytes 393220
  114.4 2.8 copy-start.9
Sparse Core Ops, SparseCore 0:
  67.1 47.2 reduce-scatter.1
  121.5 483.7 all-reduce.2
where the time goes:
time: 616 us; the launch traced here: 614 us
  waiting for transfers between devices  515 us (84%)
  starting transfers between devices  37.1 us (6%)
  blocking collectives  19.7 us (3%)
  between operations  15 us (2%)
  matrix products  14.1 us (2%)
  local copies, waits for them, and re-layouts  10.2 us (2%)
    psum x1, waiting for transfers between devices, local(): self_sum, neigh_sum = lax.psum((local_self, local_neigh), ('row', 'col'))  487 us
    ppermute x8, starting transfers between devices, passed_along(): lax.ppermute(value, axis, [(source, source + steps) for source in range(l...  37 us
    reduce_scatter x1, waiting for transfers between devices, local(): lax.psum_scatter(partial_sums.reshape(ncol * blk, width).astype(jnp.bfloa...  27.7 us
    all_gather x1, blocking collectives, local(): lax.all_gather(scaled, 'col', axis=0, tiled=True).reshape(ncol, blk, width)  19.7 us
  transfers between devices with their start and end apart: 10, of which 2 were waited for; matrix products, arithmetic and copies ran while one was open for 2% of the time, Pallas kernels for 0%

commit v1 on v0

v1 whole, which is shorter than its diff:
```python
import functools
import math

import jax
import jax.numpy as jnp
import numpy as np
from jax import lax
from jax.experimental import pallas as pl
from jax.experimental.pallas import tpu as pltpu
from jax.sharding import Mesh
from jax.sharding import PartitionSpec as P

HALO = 2
WIDE = 2 * HALO + 1
ROW = ("z", "x", "core")
NEAR = ("x", "core", "y")
LIMIT = 48 * 1024 * 1024

VM = pl.BlockSpec(memory_space=pltpu.VMEM)
SM = pl.BlockSpec(memory_space=pltpu.SMEM)
HB = pl.BlockSpec(memory_space=pl.ANY)


def call(body, outs, in_specs, out_specs=None, scratch=(), aliases=None, cost=None):
    return pl.pallas_call(
        body,
        out_shape=outs,
        in_specs=in_specs,
        out_specs=out_specs if out_specs is not None else jax.tree.map(lambda _: VM, outs),
        scratch_shapes=list(scratch),
        input_output_aliases=aliases or {},
        cost_estimate=cost,
        compiler_params=pltpu.CompilerParams(vmem_limit_bytes=LIMIT),
    )


def half(*shape):
    return jax.ShapeDtypeStruct(shape, jnp.bfloat16)


def full(*shape):
    return jax.ShapeDtypeStruct(shape, jnp.float32)


def dot(a, b, ca, cb):
    return lax.dot_general(a, b, (((ca,), (cb,)), ((), ())), preferred_element_type=jnp.float32)


def cost(flops, moved):
    return pl.CostEstimate(flops=flops, bytes_accessed=moved, transcendentals=0)


def pair_body(spot, own, below, above, out):
    blk = own.shape[0]
    out[:blk, :] = own[...]
    out[blk:, :] = jnp.where(spot[0] == 0, above[...], below[...])


def forward_body(rows, bands, count, spot, tiles, f0, near, f4, own, out, sent, kept, window, total):
    slots, blk = tiles.shape[0], tiles.shape[1]
    ncol = total.shape[0] - 1
    core = spot[0]
    window[0] = f0[...]
    window[1] = near[pl.ds(pl.multiple_of((1 - core) * blk, blk), blk), :]
    window[2] = own[...]
    window[3] = near[pl.ds(pl.multiple_of(core * blk, blk), blk), :]
    window[4] = f4[...]
    total[...] = jnp.zeros_like(total)
    for slot in range(slots):
        place = jnp.where(slot < count[0], rows[slot], ncol)
        total[place] += dot(tiles[slot], window[bands[slot]], 1, 0)
    for at in range(ncol):
        out[at * blk : (at + 1) * blk, :] = total[at].astype(jnp.bfloat16)
    bit = spot[1]
    for at in range(ncol // 2):
        sent[at * blk : (at + 1) * blk, :] = total[2 * at + 1 - bit].astype(jnp.bfloat16)
        kept[at * blk : (at + 1) * blk, :] = total[2 * at + bit].astype(jnp.bfloat16)


def halve_body(blk, which):
    def body(spot, came, held, sent, kept):
        bit = spot[which]
        for at in range(sent.shape[0] // blk):
            for out, side in ((sent, 1 - bit), (kept, bit)):
                start = pl.multiple_of((2 * at + side) * blk, blk)
                rows = pl.ds(start, blk)
                total = came[rows, :].astype(jnp.float32) + held[rows, :].astype(jnp.float32)
                out[at * blk : (at + 1) * blk, :] = total.astype(out.dtype)

    return body


def column(degree, width):
    blk = degree.shape[1]
    tall = jnp.broadcast_to(degree[...].astype(jnp.float32), (blk, blk)).T
    return jnp.concatenate([tall] * (width // blk), axis=1)


def share_body(degree, cotangent, out):
    blk, width = cotangent.shape
    share = (cotangent[...].astype(jnp.float32) / column(degree, width)).astype(jnp.bfloat16)
    for at in range(out.shape[0] // blk):
        out[at * blk : (at + 1) * blk, :] = share


def grads_body(features, cotangent, partial, shares, sent, out, passed):
    own = dot(features[...], cotangent[...], 0, 0).astype(jnp.bfloat16)
    neigh = dot(partial[...], shares[...], 0, 0).astype(jnp.bfloat16)
    height, lanes = own.shape[0], out.shape[1]
    for at in range(2):
        out[at * height : (at + 1) * height, :] = own[:, at * lanes : (at + 1) * lanes]
        out[(at + 2) * height : (at + 3) * height, :] = neigh[:, at * lanes : (at + 1) * lanes]


def backward_body(rows, bands, count, tiles, shares, weight, after, far0, near, own, far1, total):
    slots, blk = tiles.shape[0], tiles.shape[1]
    total[...] = jnp.zeros_like(total)
    for slot in range(slots):
        place = jnp.where(slot < count[0], bands[slot], WIDE)
        start = pl.multiple_of(rows[slot] * blk, blk)
        total[place] += dot(tiles[slot], shares[pl.ds(start, blk), :], 0, 0)
    landed = [
        dot(total[at].astype(jnp.bfloat16), weight[...], 1, 1).astype(jnp.bfloat16)
        for at in range(WIDE)
    ]
    far0[...], own[...], far1[...] = landed[0], landed[2], landed[4]
    near[:blk, :], near[blk:, :] = landed[1], landed[3]


def merge_body(spot, came, far0, far1, own, low, high, mid):
    blk = own.shape[0]
    core = spot[0]
    lower = came[:blk, :].astype(jnp.float32)
    upper = came[blk:, :].astype(jnp.float32)
    low[...] = jnp.where(core == 1, far0[...].astype(jnp.float32) + lower, far0[...].astype(jnp.float32)).astype(low.dtype)
    high[...] = jnp.where(core == 0, far1[...].astype(jnp.float32) + upper, far1[...].astype(jnp.float32)).astype(high.dtype)
    mid[...] = own[...].astype(jnp.float32) + jnp.where(core == 0, lower, upper)


def fold(source, members):
    rows = source.shape[0] // members
    total = source[:rows, :].astype(jnp.float32)
    for at in range(1, members):
        total = total + source[at * rows : (at + 1) * rows, :].astype(jnp.float32)
    return total


def fold_spread(value, members, copies, after=()):
    rows, lanes = value.shape[0] // members, value.shape[1]

    def body(*refs):
        total = fold(refs[0], members).astype(jnp.bfloat16)
        for at in range(copies):
            refs[-1][at * rows : (at + 1) * rows, :] = total

    return call(body, half(copies * rows, lanes), [VM] + [HB] * len(after))(value, *after)


def finish_body(factor, source, own, neigh):
    height, lanes = own.shape[0], source.shape[1]
    for at in range(2):
        for first, grad in ((at, own), (at + 2, neigh)):
            grad[:, at * lanes : (at + 1) * lanes] = (
                source[first * height : (first + 1) * height, :].astype(jnp.float32) * factor
            )


def output_body(came, held, degree, features, self_weight, neigh_weight, out):
    sums = came[...].astype(jnp.float32) + held[...]
    aggregate = (sums / column(degree, out.shape[1])).astype(jnp.bfloat16)
    out[...] = (
        dot(features[...], self_weight[...], 1, 0) + dot(aggregate, neigh_weight[...], 1, 0)
    ).astype(jnp.bfloat16)


def feature_body(low, high, mid, cotangent, self_weight, out):
    spread = mid[...] + low[...].astype(jnp.float32) + high[...].astype(jnp.float32)
    out[...] = (dot(cotangent[...], self_weight[...], 1, 1) + spread).astype(jnp.bfloat16)


def passed_along(value, steps):
    count = lax.axis_size(ROW)
    leading, last = max(0, -steps), min(count, count - steps)
    return lax.ppermute(value, ROW, [(source, source + steps) for source in range(leading, last)])


def crossed(value, axis, flip):
    return lax.ppermute(value, axis, [(at, at ^ flip) for at in range(lax.axis_size(axis))])


def exchange(value, axes):
    return lax.all_to_all(value, axes, 0, 0, tiled=True)


def local(
    features, self_weight, neigh_weight, tiles, tile_rows, tile_bands, tile_count, degree, cotangent
):
    ncol = lax.axis_size("y")
    near, far = lax.axis_size(NEAR), lax.axis_size("z")
    blk, width = features.shape
    lanes = width // 2
    slots = tiles.shape[2]
    tile_set = tiles[0, 0]
    rows, bands, count = tile_rows[0, 0], tile_bands[0, 0], tile_count[0]
    core, at_col = lax.axis_index("core"), lax.axis_index("y")
    spot = jnp.stack([core, at_col % 2, at_col // 2 % 2, at_col // 4]).astype(jnp.int32)
    degree = degree[None, :]
    work = 2 * slots * blk * blk * width
    factor = 1.0 / math.sqrt(lax.axis_size(ROW) * ncol * blk)

    copies = call(share_body, half(ncol * blk, width), [VM] * 2)(degree, cotangent)
    shares = exchange(copies, "y")
    below, above = passed_along(features, 2), passed_along(features, -2)
    pair = call(pair_body, half(2 * blk, width), [SM] + [VM] * 3)(spot, features, below, above)
    near_blocks = crossed(pair, "core", 1)
    partial, sent, kept = call(
        forward_body,
        [half(ncol * blk, width)] + [half(ncol // 2 * blk, width)] * 2,
        [SM] * 4 + [VM] * 5,
        scratch=[
            pltpu.VMEM((WIDE, blk, width), jnp.bfloat16),
            pltpu.VMEM((ncol + 1, blk, width), jnp.float32),
        ],
        cost=cost(work, tile_set.size * 2 + 21 * features.size * 2),
    )(rows, bands, count, spot, tile_set, below, near_blocks, above, features)

    grads, sent = call(
        grads_body,
        [half(4 * width, lanes), half(*sent.shape)],
        [VM] * 4 + [HB],
        [VM, HB],
        aliases={4: 1},
        cost=cost(2 * (ncol + 1) * blk * width * width, 18 * features.size * 2),
    )(features, cotangent, partial, shares, sent)
    scattered = exchange(grads, NEAR)

    far0, near_landed, own, far1 = call(
        backward_body,
        [half(blk, width), half(2 * blk, width), half(blk, width), half(blk, width)],
        [SM] * 3 + [VM] * 3 + [HB],
        scratch=[pltpu.VMEM((WIDE + 1, blk, width), jnp.float32)],
        cost=cost(work, tile_set.size * 2 + 13 * features.size * 2),
    )(rows, bands, count, tile_set, shares, neigh_weight, grads)
    near_landed = crossed(near_landed, "core", 1)
    came = crossed(sent, "y", 1)

    joined = fold_spread(scattered, near, far, after=[near_landed, came])
    joined = exchange(joined, "z")

    low, high, mid = call(
        merge_body, [half(blk, width)] * 2 + [full(blk, width)], [SM] + [VM] * 4
    )(spot, near_landed, far0, far1, own)
    low, high = passed_along(low, -2), passed_along(high, 2)
    sent, kept = call(
        halve_body(blk, 2),
        [half(ncol // 4 * blk, width), full(ncol // 4 * blk, width)],
        [SM] + [VM] * 2,
    )(spot, came, kept)
    came = crossed(sent, "y", 2)

    grads = fold_spread(joined, far, near, after=[low, high, came])
    gathered = exchange(grads, NEAR)

    feature_grad = call(feature_body, half(blk, width), [VM] * 5)(
        low, high, mid, cotangent, self_weight
    )
    sent, kept = call(halve_body(blk, 3), [half(blk, width), full(blk, width)], [SM] + [VM] * 2)(
        spot, came, kept
    )
    came = crossed(sent, "y", 4)
    output = call(output_body, half(blk, width), [VM] * 6)(
        came, kept, degree, features, self_weight, neigh_weight
    )
    self_grad, neigh_grad = call(
        functools.partial(finish_body, factor), [full(width, width)] * 2, [VM]
    )(gathered)
    return (output, feature_grad, self_grad, neigh_grad)


def solution(mesh):
    fine = Mesh(
        np.array(mesh.devices).reshape(mesh.shape["row"] // 8, 4, 2, mesh.shape["col"]),
        ROW + ("y",),
    )
    nodes = ROW + ("y",)
    in_specs = (
        P(nodes, None),
        P(),
        P(),
        P(ROW, "y", None, None, None),
        P(ROW, "y", None),
        P(ROW, "y", None),
        P(ROW, "y"),
        P(nodes),
        P(nodes, None),
    )
    out_specs = (P(nodes, None), P(nodes, None), P(), P())
    return jax.shard_map(local, mesh=fine, in_specs=in_specs, out_specs=out_specs, check_vma=False)
```

time: 616 us -> 114 us (0.19)
  waiting for transfers between devices: 515 us -> 14.7 us
  starting transfers between devices: 37.1 us -> 84.2 us
  blocking collectives: 19.7 us -> 0 us
  matrix products: 14.1 us -> 0 us
  between operations: 15 us -> 1.53 us
  Pallas kernels: 0 us -> 10.8 us
  local copies, waits for them, and re-layouts: 10.2 us -> 2.18 us
    psum x1 -> x0, waiting for transfers between devices: 487 us -> none  [local(): self_sum, neigh_sum = lax.psum((local_self, local_neigh), ('row', 'col'))]
    all_to_all x0 -> x4, starting transfers between devices: none -> 43.5 us  [exchange(): return lax.all_to_all(value, axes, 0, 0, tiled=True)]
    reduce_scatter x1 -> x0, waiting for transfers between devices: 27.7 us -> none  [local(): lax.psum_scatter(partial_sums.reshape(ncol * blk, width).astype(jnp.bfloa...]
    all_gather x1 -> x0, blocking collectives: 19.7 us -> none  [local(): lax.all_gather(scaled, 'col', axis=0, tiled=True).reshape(ncol, blk, width)]
    ppermute x8 -> x9, waiting for transfers between devices: 0.02 us -> 14.6 us  [the longest x5 12.1 us: crossed(): lax.ppermute(value, axis, [(at, at ^ flip) for at in range(lax.axis_size(...]
    dot_general x14 -> x0, matrix products: 14.1 us -> none  [the longest x2 2.8 us: fold_split(): jnp.einsum(form, picker, lower, preferred_element_type=jnp.float32)]
    pallas_call x0 -> x13, Pallas kernels: none -> 10.8 us  [the longest x2 1.44 us: fold_spread(): call(body, half(copies * rows, lanes), [VM] + [HB] * len(after))]
    convert_element_type x5 -> x0, local copies, waits for them, and re-layouts: 7.22 us -> none  [the longest x2 3.55 us: fold_split(): upper = values.astype(jnp.bfloat16)]
  transfers between devices with their start and end apart: 10 -> 13, of which waited for: 2 -> 6; matrix products, arithmetic and copies ran while one was open for 2% -> 0% of each run, Pallas kernels for 0% -> 6%
where the time goes in v1:
time: 114 us; the launch traced here: 113 us
  starting transfers between devices  84.2 us (74%)
  waiting for transfers between devices  14.7 us (13%)
  Pallas kernels  10.8 us (9%)
  local copies, waits for them, and re-layouts  2.18 us (2%)
  between operations  1.53 us (1%)
    all_to_all x4, starting transfers between devices, exchange(): return lax.all_to_all(value, axes, 0, 0, tiled=True)  43.5 us
    ppermute x5, starting transfers between devices, crossed(): lax.ppermute(value, axis, [(at, at ^ flip) for at in range(lax.axis_size(...  30.1 us
    ppermute x5, waiting for transfers between devices, crossed(): lax.ppermute(value, axis, [(at, at ^ flip) for at in range(lax.axis_size(...  12.1 us
    ppermute x4, starting transfers between devices, passed_along(): lax.ppermute(value, ROW, [(source, source + steps) for source in range(le...  10.6 us
    ppermute x4, waiting for transfers between devices, passed_along(): lax.ppermute(value, ROW, [(source, source + steps) for source in range(le...  2.5 us
  transfers between devices with their start and end apart: 13, of which 6 were waited for; matrix products, arithmetic and copies ran while one was open for 0% of the time, Pallas kernels for 6%

profile of v1, /device:TPU:1, one launch (start us, length us, event | category | flops | bytes accessed | tf_op | source)
XLA Modules:
  0.0 113.4 jit_solution(1769257290075162319)
XLA Ops:
  0.6 0.0 copy-start.8
  0.6 0.6 copy-done.8
  1.3 0.8 copy-done.2
  2.1 0.9 shard_map.122
  3.1 7.8 %all-to-all-start = ((bf16[8,128,256]{2,1,0:T(8,128)(2,1)}), bf16[8,128,256]{2,1,0:T(8,128)(2,1)S(1)}, u32[]{:S(2)}, u32[]{:S(2)}) async-start(bf16[8,128,256]{2,1,0:T(8,128)(2,1)} %bitcast.9), calls=%async_computation | async-start | bytes 1048576 | tf_op jit(solution)/shard_map/all_to_all | solution.py:192
  10.8 0.0 copy-done.1
  10.8 1.3 %collective-permute-start.1 = (bf16[128,256]{1,0:T(8,128)(2,1)S(1)}, bf16[128,256]{1,0:T(8,128)(2,1)S(1)}, u32[]{:S(2)}, u32[]{:S(2)}) collective-permute-start(bf16[128,256]{1,0:T(8,128)(2,1)S(1)} %copy-done.1), channel_id=1, source_target_pairs={{16,0},{24,8},{32,16},{40,24},{48,32},{56,40},{64,48},{72,56},{80,... | collective-permute-start | bytes 196616 | tf_op jit(solution)/shard_map/ppermute | solution.py:184
  12.1 4.0 %collective-permute-start = (bf16[128,256]{1,0:T(8,128)(2,1)S(1)}, bf16[128,256]{1,0:T(8,128)(2,1)S(1)}, u32[]{:S(2)}, u32[]{:S(2)}) collective-permute-start(bf16[128,256]{1,0:T(8,128)(2,1)S(1)} %copy-done.1), channel_id=1, source_target_pairs={{0,16},{8,24},{16,32},{24,40},{32,48},{40,56},{48,64},{56,72},{64,... | collective-permute-start | bytes 196616 | tf_op jit(solution)/shard_map/ppermute | solution.py:184
  16.2 0.1 pad_add_fusion.spot
  16.3 0.0 collective-permute-done.1.above.f4
  16.3 1.2 %collective-permute-done.below.f0 = bf16[128,256]{1,0:T(8,128)(2,1)S(1)} collective-permute-done((bf16[128,256]{1,0:T(8,128)(2,1)S(1)}, bf16[128,256]{1,0:T(8,128)(2,1)S(1)}, u32[]{:S(2)}, u32[]{:S(2)}) %collective-permute-start) | collective-permute-done | bytes 65568 | tf_op jit(solution)/shard_map/ppermute | solution.py:184
  17.4 0.6 shard_map.120
  18.0 13.0 %collective-permute-start.2 = (bf16[256,256]{1,0:T(8,128)(2,1)S(1)}, bf16[256,256]{1,0:T(8,128)(2,1)S(1)}, u32[]{:S(2)}, u32[]{:S(2)}) collective-permute-start(bf16[256,256]{1,0:T(8,128)(2,1)S(1)} %shard_map.120), channel_id=1, source_target_pairs={{0,8},{8,0},{1,9},{9,1},{2,10},{10,2},{3,11},{11,3},{4,12},{12,4},... | collective-permute-start | bytes 393224 | tf_op jit(solution)/shard_map/ppermute | solution.py:188
  31.7 0.3 collective-permute-done.2.near
  32.0 0.0 copy-done
  32.0 0.6 copy-done.6
  32.7 0.0 copy-done.7
  32.7 1.1 shard_map.121
  33.8 0.0 all-to-all-done
  33.8 1.1 shard_map.123
  34.9 10.0 %all-to-all-start.1 = ((bf16[64,16,128]{2,1,0:T(8,128)(2,1)}), bf16[64,16,128]{2,1,0:T(8,128)(2,1)S(1)}, u32[]{:S(2)}, u32[]{:S(2)}) async-start(bf16[64,16,128]{2,1,0:T(8,128)(2,1)} %bitcast.11), calls=%async_computation.1 | async-start | bytes 524288 | tf_op jit(solution)/shard_map/all_to_all | solution.py:192
  44.9 3.3 %collective-permute-start.3 = (bf16[512,256]{1,0:T(8,128)(2,1)S(1)}, bf16[512,256]{1,0:T(8,128)(2,1)S(1)}, u32[]{:S(2)}, u32[]{:S(2)}) collective-permute-start(bf16[512,256]{1,0:T(8,128)(2,1)S(1)} %get-tuple-element.24), channel_id=1, source_target_pairs={{0,1},{1,0},{2,3},{3,2},{4,5},{5,4},{6,7},{7,6},{8,9},{9,8},{10,11... | collective-permute-start | bytes 786440 | tf_op jit(solution)/shard_map/ppermute | solution.py:188
  48.3 1.4 %shard_map.127 = (bf16[128,256]{1,0:T(8,128)(2,1)S(1)}, bf16[256,256]{1,0:T(8,128)(2,1)S(1)}, bf16[128,256]{1,0:T(8,128)(2,1)S(1)}, bf16[128,256]{1,0:T(8,128)(2,1)S(1)}) custom-call(s32[16]{0:T(128)S(1)} %bitcast.27, s32[16]{0:T(128)S(1)} %bitcast.29, s32[1]{0:T(128)} %bitcast.18.count, bf16[16,128,128]{2,1,0:T(8,128)(2,1)S(1)} %bitcast.22, ...), custom_call_target="tpu_custom_call" | custom-call | flops 134217728 | bytes 1376256 | tf_op jit(solution)/shard_map/pallas_call | solution.py:237
  49.6 2.5 %collective-permute-start.6 = (bf16[256,256]{1,0:T(8,128)(2,1)S(1)}, bf16[256,256]{1,0:T(8,128)(2,1)S(1)}, u32[]{:S(2)}, u32[]{:S(2)}) collective-permute-start(bf16[256,256]{1,0:T(8,128)(2,1)S(1)} %get-tuple-element.31), channel_id=1, source_target_pairs={{0,8},{8,0},{1,9},{9,1},{2,10},{10,2},{3,11},{11,3},{4,12},{12,4},... | collective-permute-start | bytes 393224 | tf_op jit(solution)/shard_map/ppermute | solution.py:188
  52.2 1.0 collective-permute-done.6.came.refs_1_
  53.1 5.0 %collective-permute-done.3.came.refs_2_ = bf16[512,256]{1,0:T(8,128)(2,1)S(1)} collective-permute-done((bf16[512,256]{1,0:T(8,128)(2,1)S(1)}, bf16[512,256]{1,0:T(8,128)(2,1)S(1)}, u32[]{:S(2)}, u32[]{:S(2)}) %collective-permute-start.3) | collective-permute-done | bytes 262176 | tf_op jit(solution)/shard_map/ppermute | solution.py:188
  58.2 0.0 all-to-all-done.1
  58.2 0.7 shard_map.130
  58.9 14.2 %all-to-all-start.2 = ((bf16[16,16,128]{2,1,0:T(8,128)(2,1)}), bf16[16,16,128]{2,1,0:T(8,128)(2,1)S(1)}, u32[]{:S(2)}, u32[]{:S(2)}) async-start(bf16[16,16,128]{2,1,0:T(8,128)(2,1)} %bitcast.13), calls=%async_computation.2 | async-start | bytes 131072 | tf_op jit(solution)/shard_map/all_to_all | solution.py:192
  73.1 0.6 shard_map.124
  73.7 4.0 %collective-permute-start.4 = (bf16[256,256]{1,0:T(8,128)(2,1)S(1)}, bf16[256,256]{1,0:T(8,128)(2,1)S(1)}, u32[]{:S(2)}, u32[]{:S(2)}) collective-permute-start(bf16[256,256]{1,0:T(8,128)(2,1)S(1)} %get-tuple-element.26), channel_id=1, source_target_pairs={{0,2},{1,3},{2,0},{3,1},{4,6},{5,7},{6,4},{7,5},{8,10},{9,11},{10,... | collective-permute-start | bytes 393224 | tf_op jit(solution)/shard_map/ppermute | solution.py:188
  77.7 0.6 shard_map.128
  78.3 1.3 %collective-permute-start.7 = (bf16[128,256]{1,0:T(8,128)(2,1)S(1)}, bf16[128,256]{1,0:T(8,128)(2,1)S(1)}, u32[]{:S(2)}, u32[]{:S(2)}) collective-permute-start(bf16[128,256]{1,0:T(8,128)(2,1)S(1)} %get-tuple-element.35), channel_id=1, source_target_pairs={{16,0},{24,8},{32,16},{40,24},{48,32},{56,40},{64,48},{72,56},{80,... | collective-permute-start | bytes 196616 | tf_op jit(solution)/shard_map/ppermute | solution.py:184
  79.6 4.0 %collective-permute-start.8 = (bf16[128,256]{1,0:T(8,128)(2,1)S(1)}, bf16[128,256]{1,0:T(8,128)(2,1)S(1)}, u32[]{:S(2)}, u32[]{:S(2)}) collective-permute-start(bf16[128,256]{1,0:T(8,128)(2,1)S(1)} %get-tuple-element.36), channel_id=1, source_target_pairs={{0,16},{8,24},{16,32},{24,40},{32,48},{40,56},{48,64},{56,72},{64,... | collective-permute-start | bytes 196616 | tf_op jit(solution)/shard_map/ppermute | solution.py:184
  83.6 0.0 collective-permute-done.7.low.refs_1_
  83.6 1.3 %collective-permute-done.8.high.refs_2_ = bf16[128,256]{1,0:T(8,128)(2,1)S(1)} collective-permute-done((bf16[128,256]{1,0:T(8,128)(2,1)S(1)}, bf16[128,256]{1,0:T(8,128)(2,1)S(1)}, u32[]{:S(2)}, u32[]{:S(2)}) %collective-permute-start.8) | collective-permute-done | bytes 65568 | tf_op jit(solution)/shard_map/ppermute | solution.py:184
  84.9 0.0 collective-permute-done.4.came.refs_3_
  84.9 0.0 all-to-all-done.2
  84.9 0.7 shard_map.131
  85.6 11.6 %all-to-all-start.3 = ((bf16[64,16,128]{2,1,0:T(8,128)(2,1)}), bf16[64,16,128]{2,1,0:T(8,128)(2,1)S(1)}, u32[]{:S(2)}, u32[]{:S(2)}) async-start(bf16[64,16,128]{2,1,0:T(8,128)(2,1)} %bitcast.15), calls=%async_computation.3 | async-start | bytes 524288 | tf_op jit(solution)/shard_map/all_to_all | solution.py:192
  97.2 0.0 copy-start.5
  97.2 0.6 shard_map.125
  97.8 7.2 %collective-permute-start.5 = (bf16[128,256]{1,0:T(8,128)(2,1)S(1)}, bf16[128,256]{1,0:T(8,128)(2,1)S(1)}, u32[]{:S(2)}, u32[]{:S(2)}) collective-permute-start(bf16[128,256]{1,0:T(8,128)(2,1)S(1)} %get-tuple-element.28), channel_id=1, source_target_pairs={{0,4},{1,5},{2,6},{3,7},{4,0},{5,1},{6,2},{7,3},{8,12},{9,13},{10,... | collective-permute-start | bytes 196616 | tf_op jit(solution)/shard_map/ppermute | solution.py:188
  105.0 0.8 shard_map.129
  105.9 5.8 %collective-permute-done.5.came = bf16[128,256]{1,0:T(8,128)(2,1)S(1)} collective-permute-done((bf16[128,256]{1,0:T(8,128)(2,1)S(1)}, bf16[128,256]{1,0:T(8,128)(2,1)S(1)}, u32[]{:S(2)}, u32[]{:S(2)}) %collective-permute-start.5) | collective-permute-done | bytes 65568 | tf_op jit(solution)/shard_map/ppermute | solution.py:188
  111.7 0.9 shard_map.126
  112.6 0.0 all-to-all-done.3
  112.6 0.8 shard_map.132
  (10 shorter events, 0.0 us)
Async XLA Ops:
  0.6 0.7 copy-start.8
  1.3 0.8 copy-start.2
  3.0 7.8 %copy-start.1 = (bf16[128,256]{1,0:T(8,128)(2,1)S(1)}, bf16[128,256]{1,0:T(8,128)(2,1)}, u32[]{:S(2)}) copy-start(bf16[128,256]{1,0:T(8,128)(2,1)} %features.3) | copy-start | bytes 196612
  3.0 29.0 %copy-start = (bf16[1,1,16,128,128]{4,3,2,1,0:T(8,128)(2,1)S(1)}, bf16[1,1,16,128,128]{4,3,2,1,0:T(8,128)(2,1)}, u32[]{:S(2)}) copy-start(bf16[1,1,16,128,128]{4,3,2,1,0:T(8,128)(2,1)} %param.12) | copy-start | bytes 1572868
  3.1 30.8 %all-to-all-start = ((bf16[8,128,256]{2,1,0:T(8,128)(2,1)}), bf16[8,128,256]{2,1,0:T(8,128)(2,1)S(1)}, u32[]{:S(2)}, u32[]{:S(2)}) async-start(bf16[8,128,256]{2,1,0:T(8,128)(2,1)} %bitcast.9), calls=%async_computation | async-start | bytes 1048576 | tf_op jit(solution)/shard_map/all_to_all | solution.py:192
  10.8 5.4 %collective-permute-start.1 = (bf16[128,256]{1,0:T(8,128)(2,1)S(1)}, bf16[128,256]{1,0:T(8,128)(2,1)S(1)}, u32[]{:S(2)}, u32[]{:S(2)}) collective-permute-start(bf16[128,256]{1,0:T(8,128)(2,1)S(1)} %copy-done.1), channel_id=1, source_target_pairs={{16,0},{24,8},{32,16},{40,24},{48,32},{56,40},{64,48},{72,56},{80,... | collective-permute-start | bytes 196616 | tf_op jit(solution)/shard_map/ppermute | solution.py:184
  12.1 5.3 %collective-permute-start = (bf16[128,256]{1,0:T(8,128)(2,1)S(1)}, bf16[128,256]{1,0:T(8,128)(2,1)S(1)}, u32[]{:S(2)}, u32[]{:S(2)}) collective-permute-start(bf16[128,256]{1,0:T(8,128)(2,1)S(1)} %copy-done.1), channel_id=1, source_target_pairs={{0,16},{8,24},{16,32},{24,40},{32,48},{40,56},{48,64},{56,72},{64,... | collective-permute-start | bytes 196616 | tf_op jit(solution)/shard_map/ppermute | solution.py:184
  18.0 14.0 %collective-permute-start.2 = (bf16[256,256]{1,0:T(8,128)(2,1)S(1)}, bf16[256,256]{1,0:T(8,128)(2,1)S(1)}, u32[]{:S(2)}, u32[]{:S(2)}) collective-permute-start(bf16[256,256]{1,0:T(8,128)(2,1)S(1)} %shard_map.120), channel_id=1, source_target_pairs={{0,8},{8,0},{1,9},{9,1},{2,10},{10,2},{3,11},{11,3},{4,12},{12,4},... | collective-permute-start | bytes 393224 | tf_op jit(solution)/shard_map/ppermute | solution.py:188
  32.0 0.7 copy-start.6
  32.0 0.7 copy-start.7
  32.7 1.1 %copy-start.3 = (bf16[128,256]{1,0:T(8,128)(2,1)S(1)}, bf16[128,256]{1,0:T(8,128)(2,1)}, u32[]{:S(2)}) copy-start(bf16[128,256]{1,0:T(8,128)(2,1)} %cotangent.5) | copy-start | bytes 196612
  34.9 13.3 %copy-start.4 = (bf16[256,256]{1,0:T(8,128)(2,1)S(1)}, bf16[256,256]{1,0:T(8,128)(2,1)}, u32[]{:S(2)}) copy-start(bf16[256,256]{1,0:T(8,128)(2,1)} %weight.1) | copy-start | bytes 393220
  34.9 23.2 %all-to-all-start.1 = ((bf16[64,16,128]{2,1,0:T(8,128)(2,1)}), bf16[64,16,128]{2,1,0:T(8,128)(2,1)S(1)}, u32[]{:S(2)}, u32[]{:S(2)}) async-start(bf16[64,16,128]{2,1,0:T(8,128)(2,1)} %bitcast.11), calls=%async_computation.1 | async-start | bytes 524288 | tf_op jit(solution)/shard_map/all_to_all | solution.py:192
  44.9 13.2 %collective-permute-start.3 = (bf16[512,256]{1,0:T(8,128)(2,1)S(1)}, bf16[512,256]{1,0:T(8,128)(2,1)S(1)}, u32[]{:S(2)}, u32[]{:S(2)}) collective-permute-start(bf16[512,256]{1,0:T(8,128)(2,1)S(1)} %get-tuple-element.24), channel_id=1, source_target_pairs={{0,1},{1,0},{2,3},{3,2},{4,5},{5,4},{6,7},{7,6},{8,9},{9,8},{10,11... | collective-permute-start | bytes 786440 | tf_op jit(solution)/shard_map/ppermute | solution.py:188
  49.6 3.5 %collective-permute-start.6 = (bf16[256,256]{1,0:T(8,128)(2,1)S(1)}, bf16[256,256]{1,0:T(8,128)(2,1)S(1)}, u32[]{:S(2)}, u32[]{:S(2)}) collective-permute-start(bf16[256,256]{1,0:T(8,128)(2,1)S(1)} %get-tuple-element.31), channel_id=1, source_target_pairs={{0,8},{8,0},{1,9},{9,1},{2,10},{10,2},{3,11},{11,3},{4,12},{12,4},... | collective-permute-start | bytes 393224 | tf_op jit(solution)/shard_map/ppermute | solution.py:188
  58.9 26.0 %all-to-all-start.2 = ((bf16[16,16,128]{2,1,0:T(8,128)(2,1)}), bf16[16,16,128]{2,1,0:T(8,128)(2,1)S(1)}, u32[]{:S(2)}, u32[]{:S(2)}) async-start(bf16[16,16,128]{2,1,0:T(8,128)(2,1)} %bitcast.13), calls=%async_computation.2 | async-start | bytes 131072 | tf_op jit(solution)/shard_map/all_to_all | solution.py:192
  73.7 11.2 %collective-permute-start.4 = (bf16[256,256]{1,0:T(8,128)(2,1)S(1)}, bf16[256,256]{1,0:T(8,128)(2,1)S(1)}, u32[]{:S(2)}, u32[]{:S(2)}) collective-permute-start(bf16[256,256]{1,0:T(8,128)(2,1)S(1)} %get-tuple-element.26), channel_id=1, source_target_pairs={{0,2},{1,3},{2,0},{3,1},{4,6},{5,7},{6,4},{7,5},{8,10},{9,11},{10,... | collective-permute-start | bytes 393224 | tf_op jit(solution)/shard_map/ppermute | solution.py:188
  78.3 5.3 %collective-permute-start.7 = (bf16[128,256]{1,0:T(8,128)(2,1)S(1)}, bf16[128,256]{1,0:T(8,128)(2,1)S(1)}, u32[]{:S(2)}, u32[]{:S(2)}) collective-permute-start(bf16[128,256]{1,0:T(8,128)(2,1)S(1)} %get-tuple-element.35), channel_id=1, source_target_pairs={{16,0},{24,8},{32,16},{40,24},{48,32},{56,40},{64,48},{72,56},{80,... | collective-permute-start | bytes 196616 | tf_op jit(solution)/shard_map/ppermute | solution.py:184
  79.6 5.3 %collective-permute-start.8 = (bf16[128,256]{1,0:T(8,128)(2,1)S(1)}, bf16[128,256]{1,0:T(8,128)(2,1)S(1)}, u32[]{:S(2)}, u32[]{:S(2)}) collective-permute-start(bf16[128,256]{1,0:T(8,128)(2,1)S(1)} %get-tuple-element.36), channel_id=1, source_target_pairs={{0,16},{8,24},{16,32},{24,40},{32,48},{40,56},{48,64},{56,72},{64,... | collective-permute-start | bytes 196616 | tf_op jit(solution)/shard_map/ppermute | solution.py:184
  85.6 26.9 %all-to-all-start.3 = ((bf16[64,16,128]{2,1,0:T(8,128)(2,1)}), bf16[64,16,128]{2,1,0:T(8,128)(2,1)S(1)}, u32[]{:S(2)}, u32[]{:S(2)}) async-start(bf16[64,16,128]{2,1,0:T(8,128)(2,1)} %bitcast.15), calls=%async_computation.3 | async-start | bytes 524288 | tf_op jit(solution)/shard_map/all_to_all | solution.py:192
  97.2 7.8 %copy-start.5 = (bf16[256,256]{1,0:T(8,128)(2,1)S(1)}, bf16[256,256]{1,0:T(8,128)(2,1)}, u32[]{:S(2)}) copy-start(bf16[256,256]{1,0:T(8,128)(2,1)} %self_weight.3) | copy-start | bytes 393220
  97.8 13.9 %collective-permute-start.5 = (bf16[128,256]{1,0:T(8,128)(2,1)S(1)}, bf16[128,256]{1,0:T(8,128)(2,1)S(1)}, u32[]{:S(2)}, u32[]{:S(2)}) collective-permute-start(bf16[128,256]{1,0:T(8,128)(2,1)S(1)} %get-tuple-element.28), channel_id=1, source_target_pairs={{0,4},{1,5},{2,6},{3,7},{4,0},{5,1},{6,2},{7,3},{8,12},{9,13},{10,... | collective-permute-start | bytes 196616 | tf_op jit(solution)/shard_map/ppermute | solution.py:188

commit v2 on v1

--- a/solution.py
+++ b/solution.py
@@ -21,14 +21,13 @@
 HB = pl.BlockSpec(memory_space=pl.ANY)
 
 
-def call(body, outs, in_specs, out_specs=None, scratch=(), aliases=None, cost=None):
+def call(body, outs, in_specs, scratch=(), cost=None):
     return pl.pallas_call(
         body,
         out_shape=outs,
         in_specs=in_specs,
-        out_specs=out_specs if out_specs is not None else jax.tree.map(lambda _: VM, outs),
+        out_specs=[VM] * len(outs) if isinstance(outs, list) else VM,
         scratch_shapes=list(scratch),
-        input_output_aliases=aliases or {},
         cost_estimate=cost,
         compiler_params=pltpu.CompilerParams(vmem_limit_bytes=LIMIT),
     )
@@ -56,21 +55,23 @@
     out[blk:, :] = jnp.where(spot[0] == 0, above[...], below[...])
 
 
-def forward_body(rows, bands, count, spot, tiles, f0, near, f4, own, out, sent, kept, window, total):
+def lay_out(window, spot, f0, pair, own, f4):
+    blk = own.shape[0]
+    core = spot[0]
+    window[0] = f0[...]
+    window[1 + 2 * (1 - core)] = pair[:blk, :]
+    window[2] = own[...]
+    window[1 + 2 * core] = pair[blk:, :]
+    window[4] = f4[...]
+
+
+def forward_body(rows, bands, count, spot, tiles, window, after, sent, kept, total):
     slots, blk = tiles.shape[0], tiles.shape[1]
     ncol = total.shape[0] - 1
-    core = spot[0]
-    window[0] = f0[...]
-    window[1] = near[pl.ds(pl.multiple_of((1 - core) * blk, blk), blk), :]
-    window[2] = own[...]
-    window[3] = near[pl.ds(pl.multiple_of(core * blk, blk), blk), :]
-    window[4] = f4[...]
     total[...] = jnp.zeros_like(total)
     for slot in range(slots):
         place = jnp.where(slot < count[0], rows[slot], ncol)
         total[place] += dot(tiles[slot], window[bands[slot]], 1, 0)
-    for at in range(ncol):
-        out[at * blk : (at + 1) * blk, :] = total[at].astype(jnp.bfloat16)
     bit = spot[1]
     for at in range(ncol // 2):
         sent[at * blk : (at + 1) * blk, :] = total[2 * at + 1 - bit].astype(jnp.bfloat16)
@@ -78,7 +79,8 @@
 
 
 def halve_body(blk, which):
-    def body(spot, came, held, sent, kept):
+    def body(spot, came, held, *rest):
+        sent, kept = rest[-2:]
         bit = spot[which]
         for at in range(sent.shape[0] // blk):
             for out, side in ((sent, 1 - bit), (kept, bit)):
@@ -103,26 +105,30 @@
         out[at * blk : (at + 1) * blk, :] = share
 
 
-def grads_body(features, cotangent, partial, shares, sent, out, passed):
+def grads_body(spot, cotangent, f0, pair, features, f4, landing, out, window):
+    lay_out(window, spot, f0, pair, features, f4)
     own = dot(features[...], cotangent[...], 0, 0).astype(jnp.bfloat16)
-    neigh = dot(partial[...], shares[...], 0, 0).astype(jnp.bfloat16)
+    neigh = dot(window[0], landing[0], 0, 0)
+    for at in range(1, WIDE):
+        neigh = neigh + dot(window[at], landing[at], 0, 0)
+    neigh = neigh.astype(jnp.bfloat16)
     height, lanes = own.shape[0], out.shape[1]
     for at in range(2):
         out[at * height : (at + 1) * height, :] = own[:, at * lanes : (at + 1) * lanes]
         out[(at + 2) * height : (at + 3) * height, :] = neigh[:, at * lanes : (at + 1) * lanes]
 
 
-def backward_body(rows, bands, count, tiles, shares, weight, after, far0, near, own, far1, total):
+def backward_body(rows, bands, count, tiles, shares, weight, out, far0, near, own, far1, total):
     slots, blk = tiles.shape[0], tiles.shape[1]
     total[...] = jnp.zeros_like(total)
     for slot in range(slots):
         place = jnp.where(slot < count[0], bands[slot], WIDE)
         start = pl.multiple_of(rows[slot] * blk, blk)
         total[place] += dot(tiles[slot], shares[pl.ds(start, blk), :], 0, 0)
-    landed = [
-        dot(total[at].astype(jnp.bfloat16), weight[...], 1, 1).astype(jnp.bfloat16)
-        for at in range(WIDE)
-    ]
+    landed = []
+    for at in range(WIDE):
+        out[at] = total[at].astype(jnp.bfloat16)
+        landed.append(dot(out[at], weight[...], 1, 1).astype(jnp.bfloat16))
     far0[...], own[...], far1[...] = landed[0], landed[2], landed[4]
     near[:blk, :], near[blk:, :] = landed[1], landed[3]
 
@@ -205,70 +211,66 @@
     core, at_col = lax.axis_index("core"), lax.axis_index("y")
     spot = jnp.stack([core, at_col % 2, at_col // 2 % 2, at_col // 4]).astype(jnp.int32)
     degree = degree[None, :]
-    work = 2 * slots * blk * blk * width
     factor = 1.0 / math.sqrt(lax.axis_size(ROW) * ncol * blk)
 
+    below, above = passed_along(features, 2), passed_along(features, -2)
     copies = call(share_body, half(ncol * blk, width), [VM] * 2)(degree, cotangent)
     shares = exchange(copies, "y")
-    below, above = passed_along(features, 2), passed_along(features, -2)
     pair = call(pair_body, half(2 * blk, width), [SM] + [VM] * 3)(spot, features, below, above)
-    near_blocks = crossed(pair, "core", 1)
-    partial, sent, kept = call(
+    pair = crossed(pair, "core", 1)
+    landing, far0, near_landed, own, far1 = call(
+        backward_body,
+        [half(WIDE, blk, width), half(blk, width), half(2 * blk, width)] + [half(blk, width)] * 2,
+        [SM] * 3 + [VM] * 3,
+        scratch=[pltpu.VMEM((WIDE + 1, blk, width), jnp.float32)],
+        cost=cost(5 * 10**9, tile_set.size * 2 + 13 * features.size * 2),
+    )(rows, bands, count, tile_set, shares, neigh_weight)
+
+    grads, window = call(
+        grads_body,
+        [half(4 * width, lanes), half(WIDE, blk, width)],
+        [SM] + [VM] * 6,
+        cost=cost(2 * (WIDE + 1) * blk * width * width, 18 * features.size * 2),
+    )(spot, cotangent, below, pair, features, above, landing)
+    scattered = exchange(grads, NEAR)
+
+    sent, kept = call(
         forward_body,
-        [half(ncol * blk, width)] + [half(ncol // 2 * blk, width)] * 2,
-        [SM] * 4 + [VM] * 5,
-        scratch=[
-            pltpu.VMEM((WIDE, blk, width), jnp.bfloat16),
-            pltpu.VMEM((ncol + 1, blk, width), jnp.float32),
-        ],
-        cost=cost(work, tile_set.size * 2 + 21 * features.size * 2),
-    )(rows, bands, count, spot, tile_set, below, near_blocks, above, features)
-
-    grads, sent = call(
-        grads_body,
-        [half(4 * width, lanes), half(*sent.shape)],
-        [VM] * 4 + [HB],
-        [VM, HB],
-        aliases={4: 1},
-        cost=cost(2 * (ncol + 1) * blk * width * width, 18 * features.size * 2),
-    )(features, cotangent, partial, shares, sent)
-    scattered = exchange(grads, NEAR)
-
-    far0, near_landed, own, far1 = call(
-        backward_body,
-        [half(blk, width), half(2 * blk, width), half(blk, width), half(blk, width)],
-        [SM] * 3 + [VM] * 3 + [HB],
-        scratch=[pltpu.VMEM((WIDE + 1, blk, width), jnp.float32)],
-        cost=cost(work, tile_set.size * 2 + 13 * features.size * 2),
-    )(rows, bands, count, tile_set, shares, neigh_weight, grads)
+        [half(ncol // 2 * blk, width)] * 2,
+        [SM] * 4 + [VM] * 2 + [HB],
+        scratch=[pltpu.VMEM((ncol + 1, blk, width), jnp.float32)],
+        cost=cost(5 * 10**9, tile_set.size * 2 + 13 * features.size * 2),
+    )(rows, bands, count, spot, tile_set, window, grads)
+    came = crossed(sent, "y", 1)
     near_landed = crossed(near_landed, "core", 1)
-    came = crossed(sent, "y", 1)
-
-    joined = fold_spread(scattered, near, far, after=[near_landed, came])
-    joined = exchange(joined, "z")
-
-    low, high, mid = call(
-        merge_body, [half(blk, width)] * 2 + [full(blk, width)], [SM] + [VM] * 4
-    )(spot, near_landed, far0, far1, own)
-    low, high = passed_along(low, -2), passed_along(high, 2)
     sent, kept = call(
         halve_body(blk, 2),
         [half(ncol // 4 * blk, width), full(ncol // 4 * blk, width)],
         [SM] + [VM] * 2,
     )(spot, came, kept)
+    low, high, mid = call(
+        merge_body, [half(blk, width)] * 2 + [full(blk, width)], [SM] + [VM] * 4
+    )(spot, near_landed, far0, far1, own)
+
+    joined = fold_spread(scattered, near, far, after=[low])
+    joined = exchange(joined, "z")
+
     came = crossed(sent, "y", 2)
-
-    grads = fold_spread(joined, far, near, after=[low, high, came])
+    low, high = passed_along(low, -2), passed_along(high, 2)
+    grads = fold_spread(joined, far, near, after=[sent])
     gathered = exchange(grads, NEAR)
 
-    feature_grad = call(feature_body, half(blk, width), [VM] * 5)(
+    sent, kept = call(
+        halve_body(blk, 3),
+        [half(blk, width), full(blk, width)],
+        [SM] + [VM] * 2 + [HB],
+        cost=cost(2 * 10**9, 0),
+    )(spot, came, kept, grads)
+    feature_grad = call(feature_body, half(blk, width), [VM] * 5, cost=cost(4 * 10**9, 0))(
         low, high, mid, cotangent, self_weight
     )
-    sent, kept = call(halve_body(blk, 3), [half(blk, width), full(blk, width)], [SM] + [VM] * 2)(
-        spot, came, kept
-    )
     came = crossed(sent, "y", 4)
-    output = call(output_body, half(blk, width), [VM] * 6)(
+    output = call(output_body, half(blk, width), [VM] * 6, cost=cost(2 * 10**9, 0))(
         came, kept, degree, features, self_weight, neigh_weight
     )
     self_grad, neigh_grad = call(

time: 114 us -> 109 us (0.956)
  starting transfers between devices: 84.2 us -> 77.6 us
  waiting for transfers between devices: 14.7 us -> 15.9 us
    all_to_all x4, waiting for transfers between devices: 0.01 us -> 6.16 us  [exchange(): return lax.all_to_all(value, axes, 0, 0, tiled=True)]
    ppermute x5, waiting for transfers between devices: 12.1 us -> 6.77 us  [crossed(): lax.ppermute(value, axis, [(at, at ^ flip) for at in range(lax.axis_size(...]
    all_to_all x4, starting transfers between devices: 43.5 us -> 40.4 us  [exchange(): return lax.all_to_all(value, axes, 0, 0, tiled=True)]
    ppermute x5, starting transfers between devices: 30.1 us -> 27.5 us  [crossed(): lax.ppermute(value, axis, [(at, at ^ flip) for at in range(lax.axis_size(...]
  transfers between devices with their start and end apart: 13 -> 13, of which waited for: 6 -> 5; matrix products, arithmetic and copies ran while one was open for 0% -> 0% of each run, Pallas kernels for 6% -> 7%
where the time goes in v2:
time: 109 us
  starting transfers between devices  77.6 us (71%)
  waiting for transfers between devices  15.9 us (15%)
  Pallas kernels  11.3 us (10%)
  local copies, waits for them, and re-layouts  2.15 us (2%)
  between operations  1.58 us (1%)
    all_to_all x4, starting transfers between devices, exchange(): return lax.all_to_all(value, axes, 0, 0, tiled=True)  40.4 us
    ppermute x5, starting transfers between devices, crossed(): lax.ppermute(value, axis, [(at, at ^ flip) for at in range(lax.axis_size(...  27.5 us
    ppermute x4, starting transfers between devices, passed_along(): lax.ppermute(value, ROW, [(source, source + steps) for source in range(le...  9.69 us
    ppermute x5, waiting for transfers between devices, crossed(): lax.ppermute(value, axis, [(at, at ^ flip) for at in range(lax.axis_size(...  6.77 us
    all_to_all x4, waiting for transfers between devices, exchange(): return lax.all_to_all(value, axes, 0, 0, tiled=True)  6.16 us
    ppermute x4, waiting for transfers between devices, passed_along(): lax.ppermute(value, ROW, [(source, source + steps) for source in range(le...  2.95 us
  transfers between devices with their start and end apart: 13, of which 5 were waited for; matrix products, arithmetic and copies ran while one was open for 0% of the time, Pallas kernels for 7%

profile of v2, /device:TPU:1, one launch (start us, length us, event | category | flops | bytes accessed | tf_op | source)
XLA Modules:
  0.0 108.6 jit_solution(17390243800335841497)
XLA Ops:
  0.6 0.0 copy-start.3
  0.6 0.6 copy-done.3
  1.3 0.8 copy-done.1
  2.1 0.9 shard_map.121
  3.1 7.8 %all-to-all-start = ((bf16[8,128,256]{2,1,0:T(8,128)(2,1)}), bf16[8,128,256]{2,1,0:T(8,128)(2,1)S(1)}, u32[]{:S(2)}, u32[]{:S(2)}) async-start(bf16[8,128,256]{2,1,0:T(8,128)(2,1)} %bitcast.9), calls=%async_computation | async-start | bytes 1048576 | tf_op jit(solution)/shard_map/all_to_all | solution.py:198
  10.8 3.1 %collective-permute-start = (bf16[128,256]{1,0:T(8,128)(2,1)S(1)}, bf16[128,256]{1,0:T(8,128)(2,1)S(1)}, u32[]{:S(2)}, u32[]{:S(2)}) collective-permute-start(bf16[128,256]{1,0:T(8,128)(2,1)S(1)} %copy-done), channel_id=1, source_target_pairs={{0,16},{8,24},{16,32},{24,40},{32,48},{40,56},{48,64},{56,72},{64,... | collective-permute-start | bytes 196616 | tf_op jit(solution)/shard_map/ppermute | solution.py:190
  14.0 1.3 %collective-permute-start.1 = (bf16[128,256]{1,0:T(8,128)(2,1)S(1)}, bf16[128,256]{1,0:T(8,128)(2,1)S(1)}, u32[]{:S(2)}, u32[]{:S(2)}) collective-permute-start(bf16[128,256]{1,0:T(8,128)(2,1)S(1)} %copy-done), channel_id=1, source_target_pairs={{16,0},{24,8},{32,16},{40,24},{48,32},{56,40},{64,48},{72,56},{80,... | collective-permute-start | bytes 196616 | tf_op jit(solution)/shard_map/ppermute | solution.py:190
  16.0 0.1 pad_add_fusion.spot
  16.0 0.0 collective-permute-done.below.f0
  16.0 2.9 %collective-permute-done.1.above.f4 = bf16[128,256]{1,0:T(8,128)(2,1)S(1)} collective-permute-done((bf16[128,256]{1,0:T(8,128)(2,1)S(1)}, bf16[128,256]{1,0:T(8,128)(2,1)S(1)}, u32[]{:S(2)}, u32[]{:S(2)}) %collective-permute-start.1) | collective-permute-done | bytes 65568 | tf_op jit(solution)/shard_map/ppermute | solution.py:190
  19.0 0.6 shard_map.120
  19.5 11.2 %collective-permute-start.2 = (bf16[256,256]{1,0:T(8,128)(2,1)S(1)}, bf16[256,256]{1,0:T(8,128)(2,1)S(1)}, u32[]{:S(2)}, u32[]{:S(2)}) collective-permute-start(bf16[256,256]{1,0:T(8,128)(2,1)S(1)} %shard_map.120), channel_id=1, source_target_pairs={{0,8},{8,0},{1,9},{9,1},{2,10},{10,2},{3,11},{11,3},{4,12},{12,4},... | collective-permute-start | bytes 393224 | tf_op jit(solution)/shard_map/ppermute | solution.py:194
  30.8 0.0 all-to-all-done
  30.8 0.0 copy-start.7
  30.8 0.0 copy-start.8
  30.8 0.6 copy-done.7
  31.5 0.0 copy-done.8
  31.5 1.4 %shard_map.122 = (bf16[5,128,256]{2,1,0:T(8,128)(2,1)S(1)}, bf16[128,256]{1,0:T(8,128)(2,1)S(1)}, bf16[256,256]{1,0:T(8,128)(2,1)S(1)}, bf16[128,256]{1,0:T(8,128)(2,1)S(1)}, bf16[128,256]{1,0:T(8,128)(2,1)S(1)}) custom-call(s32[16]{0:T(128)S(1)} %bitcast.27, s32[16]{0:T(128)S(1)} %bitcast.29, s32[1]{0:T(128)} %bitcast.17.count, ...), custom_call_target="tpu_custom_call" | custom-call | flops 5000000000 | bytes 1376256 | tf_op jit(solution)/shard_map/pallas_call | solution.py:221
  32.9 0.0 collective-permute-done.2.pair
  32.9 1.7 %shard_map.123 = (bf16[1024,128]{1,0:T(8,128)(2,1)}, bf16[5,128,256]{2,1,0:T(8,128)(2,1)S(1)}) custom-call(s32[4]{0:T(128)S(1)} %pad_add_fusion.spot, bf16[128,256]{1,0:T(8,128)(2,1)S(1)} %copy-done.2, bf16[128,256]{1,0:T(8,128)(2,1)S(1)} %collective-permute-done.below.f0, bf16[256,256]{1,0:T(8,128)(2,1)S(1)} %collective-permute-done.2.pair, ...), custom_call_target="tpu_custom_call" | custom-call | flops 100663296 | bytes 1179648 | tf_op jit(solution)/shard_map/pallas_call | solution.py:229
  34.5 7.8 %all-to-all-start.1 = ((bf16[64,16,128]{2,1,0:T(8,128)(2,1)}), bf16[64,16,128]{2,1,0:T(8,128)(2,1)S(1)}, u32[]{:S(2)}, u32[]{:S(2)}) async-start(bf16[64,16,128]{2,1,0:T(8,128)(2,1)} %bitcast.11), calls=%async_computation.1 | async-start | bytes 524288 | tf_op jit(solution)/shard_map/all_to_all | solution.py:198
  42.3 1.1 shard_map.124
  43.4 3.3 %collective-permute-start.3 = (bf16[512,256]{1,0:T(8,128)(2,1)S(1)}, bf16[512,256]{1,0:T(8,128)(2,1)S(1)}, u32[]{:S(2)}, u32[]{:S(2)}) collective-permute-start(bf16[512,256]{1,0:T(8,128)(2,1)S(1)} %get-tuple-element.25), channel_id=1, source_target_pairs={{0,1},{1,0},{2,3},{3,2},{4,5},{5,4},{6,7},{7,6},{8,9},{9,8},{10,11... | collective-permute-start | bytes 786440 | tf_op jit(solution)/shard_map/ppermute | solution.py:194
  46.7 2.6 %collective-permute-start.5 = (bf16[256,256]{1,0:T(8,128)(2,1)S(1)}, bf16[256,256]{1,0:T(8,128)(2,1)S(1)}, u32[]{:S(2)}, u32[]{:S(2)}) collective-permute-start(bf16[256,256]{1,0:T(8,128)(2,1)S(1)} %get-tuple-element.29), channel_id=1, source_target_pairs={{0,8},{8,0},{1,9},{9,1},{2,10},{10,2},{3,11},{11,3},{4,12},{12,4},... | collective-permute-start | bytes 393224 | tf_op jit(solution)/shard_map/ppermute | solution.py:194
  49.2 1.0 collective-permute-done.5.came
  50.2 0.6 shard_map.126
  50.8 3.7 %all-to-all-done.1 = bf16[64,16,128]{2,1,0:T(8,128)(2,1)S(1)} async-done(((bf16[64,16,128]{2,1,0:T(8,128)(2,1)}), bf16[64,16,128]{2,1,0:T(8,128)(2,1)S(1)}, u32[]{:S(2)}, u32[]{:S(2)}) %all-to-all-start.1) | async-done | bytes 262176 | tf_op jit(solution)/shard_map/all_to_all | solution.py:198
  54.6 0.7 shard_map.127
  55.3 17.1 %all-to-all-start.2 = ((bf16[16,16,128]{2,1,0:T(8,128)(2,1)}), bf16[16,16,128]{2,1,0:T(8,128)(2,1)S(1)}, u32[]{:S(2)}, u32[]{:S(2)}) async-start(bf16[16,16,128]{2,1,0:T(8,128)(2,1)} %bitcast.13), calls=%async_computation.2 | async-start | bytes 131072 | tf_op jit(solution)/shard_map/all_to_all | solution.py:198
  72.4 0.0 collective-permute-done.3.came
  72.4 0.6 shard_map.125
  73.0 3.2 %collective-permute-start.4 = (bf16[256,256]{1,0:T(8,128)(2,1)S(1)}, bf16[256,256]{1,0:T(8,128)(2,1)S(1)}, u32[]{:S(2)}, u32[]{:S(2)}) collective-permute-start(bf16[256,256]{1,0:T(8,128)(2,1)S(1)} %get-tuple-element.27.refs_1_), channel_id=1, source_target_pairs={{0,2},{1,3},{2,0},{3,1},{4,6},{5,7},{6,4},{7,5},{8,10},{9,11},{10,... | collective-permute-start | bytes 393224 | tf_op jit(solution)/shard_map/ppermute | solution.py:194
  76.3 1.3 %collective-permute-start.7 = (bf16[128,256]{1,0:T(8,128)(2,1)S(1)}, bf16[128,256]{1,0:T(8,128)(2,1)S(1)}, u32[]{:S(2)}, u32[]{:S(2)}) collective-permute-start(bf16[128,256]{1,0:T(8,128)(2,1)S(1)} %get-tuple-element.33.refs_1_), channel_id=1, source_target_pairs={{16,0},{24,8},{32,16},{40,24},{48,32},{56,40},{64,48},{72,56},{80,... | collective-permute-start | bytes 196616 | tf_op jit(solution)/shard_map/ppermute | solution.py:190
  77.6 4.0 %collective-permute-start.8 = (bf16[128,256]{1,0:T(8,128)(2,1)S(1)}, bf16[128,256]{1,0:T(8,128)(2,1)S(1)}, u32[]{:S(2)}, u32[]{:S(2)}) collective-permute-start(bf16[128,256]{1,0:T(8,128)(2,1)S(1)} %get-tuple-element.36), channel_id=1, source_target_pairs={{0,16},{8,24},{16,32},{24,40},{32,48},{40,56},{48,64},{56,72},{64,... | collective-permute-start | bytes 196616 | tf_op jit(solution)/shard_map/ppermute | solution.py:190
  81.6 2.4 %all-to-all-done.2 = bf16[16,16,128]{2,1,0:T(8,128)(2,1)S(1)} async-done(((bf16[16,16,128]{2,1,0:T(8,128)(2,1)}), bf16[16,16,128]{2,1,0:T(8,128)(2,1)S(1)}, u32[]{:S(2)}, u32[]{:S(2)}) %all-to-all-start.2) | async-done | bytes 65568 | tf_op jit(solution)/shard_map/all_to_all | solution.py:198
  84.0 0.7 shard_map.128.rest_0_
  84.7 7.7 %all-to-all-start.3 = ((bf16[64,16,128]{2,1,0:T(8,128)(2,1)}), bf16[64,16,128]{2,1,0:T(8,128)(2,1)S(1)}, u32[]{:S(2)}, u32[]{:S(2)}) async-start(bf16[64,16,128]{2,1,0:T(8,128)(2,1)} %bitcast.15), calls=%async_computation.3 | async-start | bytes 524288 | tf_op jit(solution)/shard_map/all_to_all | solution.py:198
  92.4 0.0 collective-permute-done.4.came
  92.4 0.0 copy-start.6
  92.4 0.6 shard_map.129
  93.0 7.2 %collective-permute-start.6 = (bf16[128,256]{1,0:T(8,128)(2,1)S(1)}, bf16[128,256]{1,0:T(8,128)(2,1)S(1)}, u32[]{:S(2)}, u32[]{:S(2)}) collective-permute-start(bf16[128,256]{1,0:T(8,128)(2,1)S(1)} %get-tuple-element.34), channel_id=1, source_target_pairs={{0,4},{1,5},{2,6},{3,7},{4,0},{5,1},{6,2},{7,3},{8,12},{9,13},{10,... | collective-permute-start | bytes 196616 | tf_op jit(solution)/shard_map/ppermute | solution.py:194
  100.2 0.0 collective-permute-done.7.low
  100.2 0.0 collective-permute-done.8.high
  100.3 0.8 shard_map.131
  101.1 5.8 %collective-permute-done.6.came = bf16[128,256]{1,0:T(8,128)(2,1)S(1)} collective-permute-done((bf16[128,256]{1,0:T(8,128)(2,1)S(1)}, bf16[128,256]{1,0:T(8,128)(2,1)S(1)}, u32[]{:S(2)}, u32[]{:S(2)}) %collective-permute-start.6) | collective-permute-done | bytes 65568 | tf_op jit(solution)/shard_map/ppermute | solution.py:194
  106.9 0.9 shard_map.130
  107.8 0.0 all-to-all-done.3
  107.8 0.8 shard_map.132
  (10 shorter events, 0.0 us)
Async XLA Ops:
  0.6 0.7 copy-start.3
  1.3 0.8 copy-start.1
  3.0 7.8 %copy-start = (bf16[128,256]{1,0:T(8,128)(2,1)S(1)}, bf16[128,256]{1,0:T(8,128)(2,1)}, u32[]{:S(2)}) copy-start(bf16[128,256]{1,0:T(8,128)(2,1)} %features.3) | copy-start | bytes 196612
  3.0 27.8 %copy-start.4 = (bf16[1,1,16,128,128]{4,3,2,1,0:T(8,128)(2,1)S(1)}, bf16[1,1,16,128,128]{4,3,2,1,0:T(8,128)(2,1)}, u32[]{:S(2)}) copy-start(bf16[1,1,16,128,128]{4,3,2,1,0:T(8,128)(2,1)} %param.12) | copy-start | bytes 1572868
  3.1 27.7 %all-to-all-start = ((bf16[8,128,256]{2,1,0:T(8,128)(2,1)}), bf16[8,128,256]{2,1,0:T(8,128)(2,1)S(1)}, u32[]{:S(2)}, u32[]{:S(2)}) async-start(bf16[8,128,256]{2,1,0:T(8,128)(2,1)} %bitcast.9), calls=%async_computation | async-start | bytes 1048576 | tf_op jit(solution)/shard_map/all_to_all | solution.py:198
  10.8 5.2 %collective-permute-start = (bf16[128,256]{1,0:T(8,128)(2,1)S(1)}, bf16[128,256]{1,0:T(8,128)(2,1)S(1)}, u32[]{:S(2)}, u32[]{:S(2)}) collective-permute-start(bf16[128,256]{1,0:T(8,128)(2,1)S(1)} %copy-done), channel_id=1, source_target_pairs={{0,16},{8,24},{16,32},{24,40},{32,48},{40,56},{48,64},{56,72},{64,... | collective-permute-start | bytes 196616 | tf_op jit(solution)/shard_map/ppermute | solution.py:190
  14.0 5.0 %collective-permute-start.1 = (bf16[128,256]{1,0:T(8,128)(2,1)S(1)}, bf16[128,256]{1,0:T(8,128)(2,1)S(1)}, u32[]{:S(2)}, u32[]{:S(2)}) collective-permute-start(bf16[128,256]{1,0:T(8,128)(2,1)S(1)} %copy-done), channel_id=1, source_target_pairs={{16,0},{24,8},{32,16},{40,24},{48,32},{56,40},{64,48},{72,56},{80,... | collective-permute-start | bytes 196616 | tf_op jit(solution)/shard_map/ppermute | solution.py:190
  16.0 14.8 %copy-start.5 = (bf16[256,256]{1,0:T(8,128)(2,1)S(1)}, bf16[256,256]{1,0:T(8,128)(2,1)}, u32[]{:S(2)}) copy-start(bf16[256,256]{1,0:T(8,128)(2,1)} %neigh_weight.1) | copy-start | bytes 393220
  19.5 13.3 %collective-permute-start.2 = (bf16[256,256]{1,0:T(8,128)(2,1)S(1)}, bf16[256,256]{1,0:T(8,128)(2,1)S(1)}, u32[]{:S(2)}, u32[]{:S(2)}) collective-permute-start(bf16[256,256]{1,0:T(8,128)(2,1)S(1)} %shard_map.120), channel_id=1, source_target_pairs={{0,8},{8,0},{1,9},{9,1},{2,10},{10,2},{3,11},{11,3},{4,12},{12,4},... | collective-permute-start | bytes 393224 | tf_op jit(solution)/shard_map/ppermute | solution.py:194
  30.8 0.7 copy-start.7
  30.8 0.7 copy-start.8
  31.5 1.4 %copy-start.2 = (bf16[128,256]{1,0:T(8,128)(2,1)S(1)}, bf16[128,256]{1,0:T(8,128)(2,1)}, u32[]{:S(2)}) copy-start(bf16[128,256]{1,0:T(8,128)(2,1)} %cotangent.5) | copy-start | bytes 196612
  34.5 20.0 %all-to-all-start.1 = ((bf16[64,16,128]{2,1,0:T(8,128)(2,1)}), bf16[64,16,128]{2,1,0:T(8,128)(2,1)S(1)}, u32[]{:S(2)}, u32[]{:S(2)}) async-start(bf16[64,16,128]{2,1,0:T(8,128)(2,1)} %bitcast.11), calls=%async_computation.1 | async-start | bytes 524288 | tf_op jit(solution)/shard_map/all_to_all | solution.py:198
  43.4 29.0 %collective-permute-start.3 = (bf16[512,256]{1,0:T(8,128)(2,1)S(1)}, bf16[512,256]{1,0:T(8,128)(2,1)S(1)}, u32[]{:S(2)}, u32[]{:S(2)}) collective-permute-start(bf16[512,256]{1,0:T(8,128)(2,1)S(1)} %get-tuple-element.25), channel_id=1, source_target_pairs={{0,1},{1,0},{2,3},{3,2},{4,5},{5,4},{6,7},{7,6},{8,9},{9,8},{10,11... | collective-permute-start | bytes 786440 | tf_op jit(solution)/shard_map/ppermute | solution.py:194
  46.7 3.5 %collective-permute-start.5 = (bf16[256,256]{1,0:T(8,128)(2,1)S(1)}, bf16[256,256]{1,0:T(8,128)(2,1)S(1)}, u32[]{:S(2)}, u32[]{:S(2)}) collective-permute-start(bf16[256,256]{1,0:T(8,128)(2,1)S(1)} %get-tuple-element.29), channel_id=1, source_target_pairs={{0,8},{8,0},{1,9},{9,1},{2,10},{10,2},{3,11},{11,3},{4,12},{12,4},... | collective-permute-start | bytes 393224 | tf_op jit(solution)/shard_map/ppermute | solution.py:194
  55.3 28.7 %all-to-all-start.2 = ((bf16[16,16,128]{2,1,0:T(8,128)(2,1)}), bf16[16,16,128]{2,1,0:T(8,128)(2,1)S(1)}, u32[]{:S(2)}, u32[]{:S(2)}) async-start(bf16[16,16,128]{2,1,0:T(8,128)(2,1)} %bitcast.13), calls=%async_computation.2 | async-start | bytes 131072 | tf_op jit(solution)/shard_map/all_to_all | solution.py:198
  73.0 19.4 %collective-permute-start.4 = (bf16[256,256]{1,0:T(8,128)(2,1)S(1)}, bf16[256,256]{1,0:T(8,128)(2,1)S(1)}, u32[]{:S(2)}, u32[]{:S(2)}) collective-permute-start(bf16[256,256]{1,0:T(8,128)(2,1)S(1)} %get-tuple-element.27.refs_1_), channel_id=1, source_target_pairs={{0,2},{1,3},{2,0},{3,1},{4,6},{5,7},{6,4},{7,5},{8,10},{9,11},{10,... | collective-permute-start | bytes 393224 | tf_op jit(solution)/shard_map/ppermute | solution.py:194
  76.3 24.0 %collective-permute-start.7 = (bf16[128,256]{1,0:T(8,128)(2,1)S(1)}, bf16[128,256]{1,0:T(8,128)(2,1)S(1)}, u32[]{:S(2)}, u32[]{:S(2)}) collective-permute-start(bf16[128,256]{1,0:T(8,128)(2,1)S(1)} %get-tuple-element.33.refs_1_), channel_id=1, source_target_pairs={{16,0},{24,8},{32,16},{40,24},{48,32},{56,40},{64,48},{72,56},{80,... | collective-permute-start | bytes 196616 | tf_op jit(solution)/shard_map/ppermute | solution.py:190
  77.6 22.7 %collective-permute-start.8 = (bf16[128,256]{1,0:T(8,128)(2,1)S(1)}, bf16[128,256]{1,0:T(8,128)(2,1)S(1)}, u32[]{:S(2)}, u32[]{:S(2)}) collective-permute-start(bf16[128,256]{1,0:T(8,128)(2,1)S(1)} %get-tuple-element.36), channel_id=1, source_target_pairs={{0,16},{8,24},{16,32},{24,40},{32,48},{40,56},{48,64},{56,72},{64,... | collective-permute-start | bytes 196616 | tf_op jit(solution)/shard_map/ppermute | solution.py:190
  84.7 23.1 %all-to-all-start.3 = ((bf16[64,16,128]{2,1,0:T(8,128)(2,1)}), bf16[64,16,128]{2,1,0:T(8,128)(2,1)S(1)}, u32[]{:S(2)}, u32[]{:S(2)}) async-start(bf16[64,16,128]{2,1,0:T(8,128)(2,1)} %bitcast.15), calls=%async_computation.3 | async-start | bytes 524288 | tf_op jit(solution)/shard_map/all_to_all | solution.py:198
  92.4 7.8 %copy-start.6 = (bf16[256,256]{1,0:T(8,128)(2,1)S(1)}, bf16[256,256]{1,0:T(8,128)(2,1)}, u32[]{:S(2)}) copy-start(bf16[256,256]{1,0:T(8,128)(2,1)} %self_weight.3) | copy-start | bytes 393220
  93.0 13.9 %collective-permute-start.6 = (bf16[128,256]{1,0:T(8,128)(2,1)S(1)}, bf16[128,256]{1,0:T(8,128)(2,1)S(1)}, u32[]{:S(2)}, u32[]{:S(2)}) collective-permute-start(bf16[128,256]{1,0:T(8,128)(2,1)S(1)} %get-tuple-element.34), channel_id=1, source_target_pairs={{0,4},{1,5},{2,6},{3,7},{4,0},{5,1},{6,2},{7,3},{8,12},{9,13},{10,... | collective-permute-start | bytes 196616 | tf_op jit(solution)/shard_map/ppermute | solution.py:194

commit v3 on v1

--- a/solution.py
+++ b/solution.py
@@ -21,15 +21,15 @@
 HB = pl.BlockSpec(memory_space=pl.ANY)
 
 
-def call(body, outs, in_specs, out_specs=None, scratch=(), aliases=None, cost=None):
+def call(body, outs, in_specs, scratch=(), cost=None, out_specs=None, aliases=None):
     return pl.pallas_call(
         body,
         out_shape=outs,
         in_specs=in_specs,
-        out_specs=out_specs if out_specs is not None else jax.tree.map(lambda _: VM, outs),
+        out_specs=out_specs or ([VM] * len(outs) if isinstance(outs, list) else VM),
         scratch_shapes=list(scratch),
+        cost_estimate=cost,
         input_output_aliases=aliases or {},
-        cost_estimate=cost,
         compiler_params=pltpu.CompilerParams(vmem_limit_bytes=LIMIT),
     )
 
@@ -50,20 +50,22 @@
     return pl.CostEstimate(flops=flops, bytes_accessed=moved, transcendentals=0)
 
 
-def pair_body(spot, own, below, above, out):
+def pair_body(spot, rows, bands, own, below, above, out):
     blk = own.shape[0]
     out[:blk, :] = own[...]
     out[blk:, :] = jnp.where(spot[0] == 0, above[...], below[...])
 
 
-def forward_body(rows, bands, count, spot, tiles, f0, near, f4, own, out, sent, kept, window, total):
+def forward_body(
+    rows, bands, count, spot, tiles, f0, pair, own, f4, out, sent, kept, window, total
+):
     slots, blk = tiles.shape[0], tiles.shape[1]
     ncol = total.shape[0] - 1
-    core = spot[0]
+    core, bit = spot[0], spot[1]
     window[0] = f0[...]
-    window[1] = near[pl.ds(pl.multiple_of((1 - core) * blk, blk), blk), :]
+    window[1 + 2 * (1 - core)] = pair[:blk, :]
     window[2] = own[...]
-    window[3] = near[pl.ds(pl.multiple_of(core * blk, blk), blk), :]
+    window[1 + 2 * core] = pair[blk:, :]
     window[4] = f4[...]
     total[...] = jnp.zeros_like(total)
     for slot in range(slots):
@@ -71,21 +73,19 @@
         total[place] += dot(tiles[slot], window[bands[slot]], 1, 0)
     for at in range(ncol):
         out[at * blk : (at + 1) * blk, :] = total[at].astype(jnp.bfloat16)
-    bit = spot[1]
     for at in range(ncol // 2):
         sent[at * blk : (at + 1) * blk, :] = total[2 * at + 1 - bit].astype(jnp.bfloat16)
         kept[at * blk : (at + 1) * blk, :] = total[2 * at + bit].astype(jnp.bfloat16)
 
 
 def halve_body(blk, which):
-    def body(spot, came, held, sent, kept):
-        bit = spot[which]
-        for at in range(sent.shape[0] // blk):
-            for out, side in ((sent, 1 - bit), (kept, bit)):
-                start = pl.multiple_of((2 * at + side) * blk, blk)
-                rows = pl.ds(start, blk)
-                total = came[rows, :].astype(jnp.float32) + held[rows, :].astype(jnp.float32)
-                out[at * blk : (at + 1) * blk, :] = total.astype(out.dtype)
+    def body(spot, came, held, *rest):
+        sent, kept = rest[-2:]
+        rows = sent.shape[0]
+        for out, side in ((sent, 1 - spot[which]), (kept, spot[which])):
+            part = pl.ds(pl.multiple_of(side * rows, blk), rows)
+            total = came[part, :].astype(jnp.float32) + held[part, :].astype(jnp.float32)
+            out[...] = total.astype(out.dtype)
 
     return body
 
@@ -96,11 +96,23 @@
     return jnp.concatenate([tall] * (width // blk), axis=1)
 
 
-def share_body(degree, cotangent, out):
-    blk, width = cotangent.shape
-    share = (cotangent[...].astype(jnp.float32) / column(degree, width)).astype(jnp.bfloat16)
-    for at in range(out.shape[0] // blk):
-        out[at * blk : (at + 1) * blk, :] = share
+def share_body(degree, cotangent, out, norm, block, share, sems):
+    blk, width = block.shape
+    first = pltpu.make_async_copy(degree, norm, sems.at[0])
+    second = pltpu.make_async_copy(cotangent, block, sems.at[1])
+    first.start()
+    second.start()
+    first.wait()
+    second.wait()
+    share[...] = (block[...].astype(jnp.float32) / column(norm, width)).astype(jnp.bfloat16)
+    copies = [
+        pltpu.make_async_copy(share, out.at[pl.ds(at * blk, blk), :], sems.at[2 + at])
+        for at in range(out.shape[0] // blk)
+    ]
+    for copy in copies:
+        copy.start()
+    for copy in copies:
+        copy.wait()
 
 
 def grads_body(features, cotangent, partial, shares, sent, out, passed):
@@ -203,16 +215,28 @@
     tile_set = tiles[0, 0]
     rows, bands, count = tile_rows[0, 0], tile_bands[0, 0], tile_count[0]
     core, at_col = lax.axis_index("core"), lax.axis_index("y")
-    spot = jnp.stack([core, at_col % 2, at_col // 2 % 2, at_col // 4]).astype(jnp.int32)
+    spot = jnp.stack([core, at_col & 1, at_col >> 2, (at_col >> 1) & 1]).astype(jnp.int32)
     degree = degree[None, :]
-    work = 2 * slots * blk * blk * width
     factor = 1.0 / math.sqrt(lax.axis_size(ROW) * ncol * blk)
 
-    copies = call(share_body, half(ncol * blk, width), [VM] * 2)(degree, cotangent)
+    below, above = passed_along(features, 2), passed_along(features, -2)
+    copies = call(
+        share_body,
+        half(ncol * blk, width),
+        [HB] * 2,
+        scratch=[
+            pltpu.VMEM((1, blk), jnp.int32),
+            pltpu.VMEM((blk, width), jnp.bfloat16),
+            pltpu.VMEM((blk, width), jnp.bfloat16),
+            pltpu.SemaphoreType.DMA((2 + ncol,)),
+        ],
+        out_specs=HB,
+    )(*(pltpu.with_memory_space_constraint(item, pltpu.HBM) for item in (degree, cotangent)))
     shares = exchange(copies, "y")
-    below, above = passed_along(features, 2), passed_along(features, -2)
-    pair = call(pair_body, half(2 * blk, width), [SM] + [VM] * 3)(spot, features, below, above)
-    near_blocks = crossed(pair, "core", 1)
+    pair = call(pair_body, half(2 * blk, width), [SM] * 3 + [VM] * 3)(
+        spot, rows, bands, features, below, above
+    )
+    pair = crossed(pair, "core", 1)
     partial, sent, kept = call(
         forward_body,
         [half(ncol * blk, width)] + [half(ncol // 2 * blk, width)] * 2,
@@ -221,54 +245,56 @@
             pltpu.VMEM((WIDE, blk, width), jnp.bfloat16),
             pltpu.VMEM((ncol + 1, blk, width), jnp.float32),
         ],
-        cost=cost(work, tile_set.size * 2 + 21 * features.size * 2),
-    )(rows, bands, count, spot, tile_set, below, near_blocks, above, features)
+        cost=cost(4 * 10**9, tile_set.size * 2 + 21 * features.size * 2),
+    )(rows, bands, count, spot, tile_set, below, pair, features, above)
 
     grads, sent = call(
         grads_body,
         [half(4 * width, lanes), half(*sent.shape)],
         [VM] * 4 + [HB],
-        [VM, HB],
+        out_specs=[VM, HB],
         aliases={4: 1},
         cost=cost(2 * (ncol + 1) * blk * width * width, 18 * features.size * 2),
     )(features, cotangent, partial, shares, sent)
     scattered = exchange(grads, NEAR)
+    came = crossed(sent, "y", 1)
 
     far0, near_landed, own, far1 = call(
         backward_body,
         [half(blk, width), half(2 * blk, width), half(blk, width), half(blk, width)],
         [SM] * 3 + [VM] * 3 + [HB],
         scratch=[pltpu.VMEM((WIDE + 1, blk, width), jnp.float32)],
-        cost=cost(work, tile_set.size * 2 + 13 * features.size * 2),
+        cost=cost(5 * 10**9, tile_set.size * 2 + 13 * features.size * 2),
     )(rows, bands, count, tile_set, shares, neigh_weight, grads)
     near_landed = crossed(near_landed, "core", 1)
-    came = crossed(sent, "y", 1)
-
-    joined = fold_spread(scattered, near, far, after=[near_landed, came])
-    joined = exchange(joined, "z")
-
-    low, high, mid = call(
-        merge_body, [half(blk, width)] * 2 + [full(blk, width)], [SM] + [VM] * 4
-    )(spot, near_landed, far0, far1, own)
-    low, high = passed_along(low, -2), passed_along(high, 2)
     sent, kept = call(
         halve_body(blk, 2),
         [half(ncol // 4 * blk, width), full(ncol // 4 * blk, width)],
         [SM] + [VM] * 2,
     )(spot, came, kept)
+    low, high, mid = call(
+        merge_body, [half(blk, width)] * 2 + [full(blk, width)], [SM] + [VM] * 4
+    )(spot, near_landed, far0, far1, own)
+
+    joined = fold_spread(scattered, near, far, after=[low])
+    joined = exchange(joined, "z")
+
+    came = crossed(sent, "y", 4)
+    low, high = passed_along(low, -2), passed_along(high, 2)
+    grads = fold_spread(joined, far, near, after=[sent])
+    gathered = exchange(grads, NEAR)
+
+    sent, kept = call(
+        halve_body(blk, 3),
+        [half(blk, width), full(blk, width)],
+        [SM] + [VM] * 2 + [HB],
+        cost=cost(2 * 10**9, 0),
+    )(spot, came, kept, grads)
+    feature_grad = call(feature_body, half(blk, width), [VM] * 5, cost=cost(4 * 10**9, 0))(
+        low, high, mid, cotangent, self_weight
+    )
     came = crossed(sent, "y", 2)
-
-    grads = fold_spread(joined, far, near, after=[low, high, came])
-    gathered = exchange(grads, NEAR)
-
-    feature_grad = call(feature_body, half(blk, width), [VM] * 5)(
-        low, high, mid, cotangent, self_weight
-    )
-    sent, kept = call(halve_body(blk, 3), [half(blk, width), full(blk, width)], [SM] + [VM] * 2)(
-        spot, came, kept
-    )
-    came = crossed(sent, "y", 4)
-    output = call(output_body, half(blk, width), [VM] * 6)(
+    output = call(output_body, half(blk, width), [VM] * 6, cost=cost(2 * 10**9, 0))(
         came, kept, degree, features, self_weight, neigh_weight
     )
     self_grad, neigh_grad = call(

time: 114 us -> 108 us (0.947)
  starting transfers between devices: 84.2 us -> 78.8 us
  local copies, waits for them, and re-layouts: 2.18 us -> 0.7 us
    all_to_all x4, waiting for transfers between devices: 0.01 us -> 6.34 us  [exchange(): return lax.all_to_all(value, axes, 0, 0, tiled=True)]
    ppermute x5, waiting for transfers between devices: 12.1 us -> 6.7 us  [crossed(): lax.ppermute(value, axis, [(at, at ^ flip) for at in range(lax.axis_size(...]
    ppermute x5, starting transfers between devices: 30.1 us -> 26.9 us  [crossed(): lax.ppermute(value, axis, [(at, at ^ flip) for at in range(lax.axis_size(...]
    all_to_all x4, starting transfers between devices: 43.5 us -> 41.4 us  [exchange(): return lax.all_to_all(value, axes, 0, 0, tiled=True)]
    unnamed x18 -> x16, local copies, waits for them, and re-layouts: 2.18 us -> 0.7 us
    ppermute x4, waiting for transfers between devices: 2.5 us -> 1.23 us  [passed_along(): lax.ppermute(value, ROW, [(source, source + steps) for source in range(le...]
  transfers between devices with their start and end apart: 13 -> 13, of which waited for: 6 -> 7; matrix products, arithmetic and copies ran while one was open for 0% -> 0% of each run, Pallas kernels for 6% -> 7%
where the time goes in v3:
time: 108 us; the launch traced here: 107 us
  starting transfers between devices  78.8 us (73%)
  waiting for transfers between devices  14.3 us (13%)
  Pallas kernels  11.7 us (11%)
  between operations  1.54 us (1%)
    all_to_all x4, starting transfers between devices, exchange(): return lax.all_to_all(value, axes, 0, 0, tiled=True)  41.4 us
    ppermute x5, starting transfers between devices, crossed(): lax.ppermute(value, axis, [(at, at ^ flip) for at in range(lax.axis_size(...  26.9 us
    ppermute x4, starting transfers between devices, passed_along(): lax.ppermute(value, ROW, [(source, source + steps) for source in range(le...  10.6 us
    ppermute x5, waiting for transfers between devices, crossed(): lax.ppermute(value, axis, [(at, at ^ flip) for at in range(lax.axis_size(...  6.7 us
    all_to_all x4, waiting for transfers between devices, exchange(): return lax.all_to_all(value, axes, 0, 0, tiled=True)  6.34 us
  transfers between devices with their start and end apart: 13, of which 7 were waited for; matrix products, arithmetic and copies ran while one was open for 0% of the time, Pallas kernels for 7%

profile of v3, /device:TPU:1, one launch (start us, length us, event | category | flops | bytes accessed | tf_op | source)
XLA Modules:
  0.0 107.1 jit_solution(17165171493697916875)
XLA Ops:
  0.6 1.9 %shard_map.122 = bf16[1024,256]{1,0:T(8,128)(2,1)} custom-call(s32[1,128]{1,0:T(1,128)} %bitcast.30, bf16[128,256]{1,0:T(8,128)(2,1)} %cotangent.5), custom_call_target="tpu_custom_call" | custom-call | tf_op jit(solution)/shard_map/pallas_call | solution.py:223
  2.5 0.0 copy-start
  2.5 0.0 copy-start.5
  2.5 7.8 %all-to-all-start = ((bf16[8,128,256]{2,1,0:T(8,128)(2,1)}), bf16[8,128,256]{2,1,0:T(8,128)(2,1)S(1)}, u32[]{:S(2)}, u32[]{:S(2)}) async-start(bf16[8,128,256]{2,1,0:T(8,128)(2,1)} %bitcast.9), calls=%async_computation | async-start | bytes 1048576 | tf_op jit(solution)/shard_map/all_to_all | solution.py:204
  10.3 0.0 copy-done
  10.3 1.3 %collective-permute-start.1 = (bf16[128,256]{1,0:T(8,128)(2,1)S(1)}, bf16[128,256]{1,0:T(8,128)(2,1)S(1)}, u32[]{:S(2)}, u32[]{:S(2)}) collective-permute-start(bf16[128,256]{1,0:T(8,128)(2,1)S(1)} %copy-done), channel_id=1, source_target_pairs={{16,0},{24,8},{32,16},{40,24},{48,32},{56,40},{64,48},{72,56},{80,... | collective-permute-start | bytes 196616 | tf_op jit(solution)/shard_map/ppermute | solution.py:196
  11.6 4.0 %collective-permute-start = (bf16[128,256]{1,0:T(8,128)(2,1)S(1)}, bf16[128,256]{1,0:T(8,128)(2,1)S(1)}, u32[]{:S(2)}, u32[]{:S(2)}) collective-permute-start(bf16[128,256]{1,0:T(8,128)(2,1)S(1)} %copy-done), channel_id=1, source_target_pairs={{0,16},{8,24},{16,32},{24,40},{32,48},{40,56},{48,64},{56,72},{64,... | collective-permute-start | bytes 196616 | tf_op jit(solution)/shard_map/ppermute | solution.py:196
  15.6 0.1 pad_add_fusion.spot
  15.7 0.0 collective-permute-done.1.above.f4
  15.7 1.2 %collective-permute-done.below.f0 = bf16[128,256]{1,0:T(8,128)(2,1)S(1)} collective-permute-done((bf16[128,256]{1,0:T(8,128)(2,1)S(1)}, bf16[128,256]{1,0:T(8,128)(2,1)S(1)}, u32[]{:S(2)}, u32[]{:S(2)}) %collective-permute-start) | collective-permute-done | bytes 65568 | tf_op jit(solution)/shard_map/ppermute | solution.py:196
  16.9 0.7 copy-done.2
  17.6 0.0 copy-done.3
  17.6 0.6 shard_map.120
  18.2 13.0 %collective-permute-start.2 = (bf16[256,256]{1,0:T(8,128)(2,1)S(1)}, bf16[256,256]{1,0:T(8,128)(2,1)S(1)}, u32[]{:S(2)}, u32[]{:S(2)}) collective-permute-start(bf16[256,256]{1,0:T(8,128)(2,1)S(1)} %shard_map.120), channel_id=1, source_target_pairs={{0,8},{8,0},{1,9},{9,1},{2,10},{10,2},{3,11},{11,3},{4,12},{12,4},... | collective-permute-start | bytes 393224 | tf_op jit(solution)/shard_map/ppermute | solution.py:200
  31.9 0.3 collective-permute-done.2.pair
  32.2 0.0 copy-done.5
  32.2 1.1 %shard_map.121 = (bf16[1024,256]{1,0:T(8,128)(2,1)S(1)}, bf16[512,256]{1,0:T(8,128)(2,1)S(1)}, bf16[512,256]{1,0:T(8,128)(2,1)S(1)}) custom-call(s32[16]{0:T(128)S(1)} %bitcast.25, s32[16]{0:T(128)S(1)} %bitcast.28, s32[1]{0:T(128)} %bitcast.17.count, s32[4]{0:T(128)S(1)} %pad_add_fusion.spot, bf16[16,128,128]{2,1,0:T(8,128)(2,1)S(1)} %bitcast.32, ...), custom_call_target="tpu_custom_call" | custom-call | flops 4000000000 | bytes 1900544 | tf_op jit(solution)/shard_map/pallas_call | solution.py:240
  33.3 0.0 all-to-all-done
  33.4 1.1 %shard_map.123 = (bf16[1024,128]{1,0:T(8,128)(2,1)}, bf16[512,256]{1,0:T(8,128)(2,1)S(1)}) custom-call(bf16[128,256]{1,0:T(8,128)(2,1)S(1)} %copy-done, bf16[128,256]{1,0:T(8,128)(2,1)S(1)} %copy-done.1, bf16[1024,256]{1,0:T(8,128)(2,1)S(1)} %get-tuple-element.22.partial, bf16[1024,256]{1,0:T(8,128)(2,1)S(1)} %bitcast.19, ...), custom_call_target="tpu_custom_call", output_to_operand_aliasing={{1}: (4, {})} | custom-call | flops 150994944 | bytes 1179648 | tf_op jit(solution)/shard_map/pallas_call | solution.py:251
  34.4 10.0 %all-to-all-start.1 = ((bf16[64,16,128]{2,1,0:T(8,128)(2,1)}), bf16[64,16,128]{2,1,0:T(8,128)(2,1)S(1)}, u32[]{:S(2)}, u32[]{:S(2)}) async-start(bf16[64,16,128]{2,1,0:T(8,128)(2,1)} %bitcast.11), calls=%async_computation.1 | async-start | bytes 524288 | tf_op jit(solution)/shard_map/all_to_all | solution.py:204
  44.4 3.3 %collective-permute-start.3 = (bf16[512,256]{1,0:T(8,128)(2,1)S(1)}, bf16[512,256]{1,0:T(8,128)(2,1)S(1)}, u32[]{:S(2)}, u32[]{:S(2)}) collective-permute-start(bf16[512,256]{1,0:T(8,128)(2,1)S(1)} %get-tuple-element.24), channel_id=1, source_target_pairs={{0,1},{1,0},{2,3},{3,2},{4,5},{5,4},{6,7},{7,6},{8,9},{9,8},{10,11... | collective-permute-start | bytes 786440 | tf_op jit(solution)/shard_map/ppermute | solution.py:200
  47.8 1.4 %shard_map.125 = (bf16[128,256]{1,0:T(8,128)(2,1)S(1)}, bf16[256,256]{1,0:T(8,128)(2,1)S(1)}, bf16[128,256]{1,0:T(8,128)(2,1)S(1)}, bf16[128,256]{1,0:T(8,128)(2,1)S(1)}) custom-call(s32[16]{0:T(128)S(1)} %bitcast.26, s32[16]{0:T(128)S(1)} %bitcast.29, s32[1]{0:T(128)} %bitcast.18.count, bf16[16,128,128]{2,1,0:T(8,128)(2,1)S(1)} %bitcast.33, ...), custom_call_target="tpu_custom_call" | custom-call | flops 5000000000 | bytes 1376256 | tf_op jit(solution)/shard_map/pallas_call | solution.py:262
  49.1 2.5 %collective-permute-start.5 = (bf16[256,256]{1,0:T(8,128)(2,1)S(1)}, bf16[256,256]{1,0:T(8,128)(2,1)S(1)}, u32[]{:S(2)}, u32[]{:S(2)}) collective-permute-start(bf16[256,256]{1,0:T(8,128)(2,1)S(1)} %get-tuple-element.29), channel_id=1, source_target_pairs={{0,8},{8,0},{1,9},{9,1},{2,10},{10,2},{3,11},{11,3},{4,12},{12,4},... | collective-permute-start | bytes 393224 | tf_op jit(solution)/shard_map/ppermute | solution.py:200
  51.7 1.0 collective-permute-done.5.came
  52.7 0.6 shard_map.126
  53.3 3.4 %all-to-all-done.1 = bf16[64,16,128]{2,1,0:T(8,128)(2,1)S(1)} async-done(((bf16[64,16,128]{2,1,0:T(8,128)(2,1)}), bf16[64,16,128]{2,1,0:T(8,128)(2,1)S(1)}, u32[]{:S(2)}, u32[]{:S(2)}) %all-to-all-start.1) | async-done | bytes 262176 | tf_op jit(solution)/shard_map/all_to_all | solution.py:204
  56.7 0.7 shard_map.127
  57.4 14.2 %all-to-all-start.2 = ((bf16[16,16,128]{2,1,0:T(8,128)(2,1)}), bf16[16,16,128]{2,1,0:T(8,128)(2,1)S(1)}, u32[]{:S(2)}, u32[]{:S(2)}) async-start(bf16[16,16,128]{2,1,0:T(8,128)(2,1)} %bitcast.13), calls=%async_computation.2 | async-start | bytes 131072 | tf_op jit(solution)/shard_map/all_to_all | solution.py:204
  71.6 0.0 collective-permute-done.3.came
  71.6 0.6 shard_map.124
  72.2 3.8 %collective-permute-start.4 = (bf16[256,256]{1,0:T(8,128)(2,1)S(1)}, bf16[256,256]{1,0:T(8,128)(2,1)S(1)}, u32[]{:S(2)}, u32[]{:S(2)}) collective-permute-start(bf16[256,256]{1,0:T(8,128)(2,1)S(1)} %get-tuple-element.26.refs_1_), channel_id=1, source_target_pairs={{0,4},{1,5},{2,6},{3,7},{4,0},{5,1},{6,2},{7,3},{8,12},{9,13},{10,... | collective-permute-start | bytes 393224 | tf_op jit(solution)/shard_map/ppermute | solution.py:200
  76.0 1.3 %collective-permute-start.7 = (bf16[128,256]{1,0:T(8,128)(2,1)S(1)}, bf16[128,256]{1,0:T(8,128)(2,1)S(1)}, u32[]{:S(2)}, u32[]{:S(2)}) collective-permute-start(bf16[128,256]{1,0:T(8,128)(2,1)S(1)} %get-tuple-element.33.refs_1_), channel_id=1, source_target_pairs={{16,0},{24,8},{32,16},{40,24},{48,32},{56,40},{64,48},{72,56},{80,... | collective-permute-start | bytes 196616 | tf_op jit(solution)/shard_map/ppermute | solution.py:196
  77.3 4.0 %collective-permute-start.8 = (bf16[128,256]{1,0:T(8,128)(2,1)S(1)}, bf16[128,256]{1,0:T(8,128)(2,1)S(1)}, u32[]{:S(2)}, u32[]{:S(2)}) collective-permute-start(bf16[128,256]{1,0:T(8,128)(2,1)S(1)} %get-tuple-element.36), channel_id=1, source_target_pairs={{0,16},{8,24},{16,32},{24,40},{32,48},{40,56},{48,64},{56,72},{64,... | collective-permute-start | bytes 196616 | tf_op jit(solution)/shard_map/ppermute | solution.py:196
  81.3 1.8 %all-to-all-done.2 = bf16[16,16,128]{2,1,0:T(8,128)(2,1)S(1)} async-done(((bf16[16,16,128]{2,1,0:T(8,128)(2,1)}), bf16[16,16,128]{2,1,0:T(8,128)(2,1)S(1)}, u32[]{:S(2)}, u32[]{:S(2)}) %all-to-all-start.2) | async-done | bytes 65568 | tf_op jit(solution)/shard_map/all_to_all | solution.py:204
  83.1 0.7 shard_map.128.rest_0_
  83.9 9.4 %all-to-all-start.3 = ((bf16[64,16,128]{2,1,0:T(8,128)(2,1)}), bf16[64,16,128]{2,1,0:T(8,128)(2,1)S(1)}, u32[]{:S(2)}, u32[]{:S(2)}) async-start(bf16[64,16,128]{2,1,0:T(8,128)(2,1)} %bitcast.15), calls=%async_computation.3 | async-start | bytes 524288 | tf_op jit(solution)/shard_map/all_to_all | solution.py:204
  93.3 0.0 collective-permute-done.4.came
  93.3 0.0 copy-start.7
  93.3 0.6 shard_map.129
  93.9 4.2 %collective-permute-start.6 = (bf16[128,256]{1,0:T(8,128)(2,1)S(1)}, bf16[128,256]{1,0:T(8,128)(2,1)S(1)}, u32[]{:S(2)}, u32[]{:S(2)}) collective-permute-start(bf16[128,256]{1,0:T(8,128)(2,1)S(1)} %get-tuple-element.34), channel_id=1, source_target_pairs={{0,2},{1,3},{2,0},{3,1},{4,6},{5,7},{6,4},{7,5},{8,10},{9,11},{10,... | collective-permute-start | bytes 196616 | tf_op jit(solution)/shard_map/ppermute | solution.py:200
  98.1 0.0 collective-permute-done.8.high
  98.1 0.0 collective-permute-done.7.low
  98.1 0.8 shard_map.131
  99.0 5.4 %collective-permute-done.6.came = bf16[128,256]{1,0:T(8,128)(2,1)S(1)} collective-permute-done((bf16[128,256]{1,0:T(8,128)(2,1)S(1)}, bf16[128,256]{1,0:T(8,128)(2,1)S(1)}, u32[]{:S(2)}, u32[]{:S(2)}) %collective-permute-start.6) | collective-permute-done | bytes 65568 | tf_op jit(solution)/shard_map/ppermute | solution.py:200
  104.4 0.0 copy-done.4
  104.4 0.9 shard_map.130
  105.2 1.1 %all-to-all-done.3 = bf16[64,16,128]{2,1,0:T(8,128)(2,1)S(1)} async-done(((bf16[64,16,128]{2,1,0:T(8,128)(2,1)}), bf16[64,16,128]{2,1,0:T(8,128)(2,1)S(1)}, u32[]{:S(2)}, u32[]{:S(2)}) %all-to-all-start.3) | async-done | bytes 262176 | tf_op jit(solution)/shard_map/all_to_all | solution.py:204
  106.3 0.8 shard_map.132
  (8 shorter events, 0.0 us)
Async XLA Ops:
  2.5 7.8 %copy-start = (bf16[128,256]{1,0:T(8,128)(2,1)S(1)}, bf16[128,256]{1,0:T(8,128)(2,1)}, u32[]{:S(2)}) copy-start(bf16[128,256]{1,0:T(8,128)(2,1)} %features.3) | copy-start | bytes 196612
  2.5 29.7 %copy-start.5 = (bf16[1,1,16,128,128]{4,3,2,1,0:T(8,128)(2,1)S(1)}, bf16[1,1,16,128,128]{4,3,2,1,0:T(8,128)(2,1)}, u32[]{:S(2)}) copy-start(bf16[1,1,16,128,128]{4,3,2,1,0:T(8,128)(2,1)} %param.12) | copy-start | bytes 1572868
  2.5 30.8 %all-to-all-start = ((bf16[8,128,256]{2,1,0:T(8,128)(2,1)}), bf16[8,128,256]{2,1,0:T(8,128)(2,1)S(1)}, u32[]{:S(2)}, u32[]{:S(2)}) async-start(bf16[8,128,256]{2,1,0:T(8,128)(2,1)} %bitcast.9), calls=%async_computation | async-start | bytes 1048576 | tf_op jit(solution)/shard_map/all_to_all | solution.py:204
  10.3 5.4 %collective-permute-start.1 = (bf16[128,256]{1,0:T(8,128)(2,1)S(1)}, bf16[128,256]{1,0:T(8,128)(2,1)S(1)}, u32[]{:S(2)}, u32[]{:S(2)}) collective-permute-start(bf16[128,256]{1,0:T(8,128)(2,1)S(1)} %copy-done), channel_id=1, source_target_pairs={{16,0},{24,8},{32,16},{40,24},{48,32},{56,40},{64,48},{72,56},{80,... | collective-permute-start | bytes 196616 | tf_op jit(solution)/shard_map/ppermute | solution.py:196
  11.6 5.3 %collective-permute-start = (bf16[128,256]{1,0:T(8,128)(2,1)S(1)}, bf16[128,256]{1,0:T(8,128)(2,1)S(1)}, u32[]{:S(2)}, u32[]{:S(2)}) collective-permute-start(bf16[128,256]{1,0:T(8,128)(2,1)S(1)} %copy-done), channel_id=1, source_target_pairs={{0,16},{8,24},{16,32},{24,40},{32,48},{40,56},{48,64},{56,72},{64,... | collective-permute-start | bytes 196616 | tf_op jit(solution)/shard_map/ppermute | solution.py:196
  16.9 0.7 copy-start.2
  16.9 0.7 copy-start.3
  18.2 14.0 %collective-permute-start.2 = (bf16[256,256]{1,0:T(8,128)(2,1)S(1)}, bf16[256,256]{1,0:T(8,128)(2,1)S(1)}, u32[]{:S(2)}, u32[]{:S(2)}) collective-permute-start(bf16[256,256]{1,0:T(8,128)(2,1)S(1)} %shard_map.120), channel_id=1, source_target_pairs={{0,8},{8,0},{1,9},{9,1},{2,10},{10,2},{3,11},{11,3},{4,12},{12,4},... | collective-permute-start | bytes 393224 | tf_op jit(solution)/shard_map/ppermute | solution.py:200
  32.2 1.1 %copy-start.1 = (bf16[128,256]{1,0:T(8,128)(2,1)S(1)}, bf16[128,256]{1,0:T(8,128)(2,1)}, u32[]{:S(2)}) copy-start(bf16[128,256]{1,0:T(8,128)(2,1)} %cotangent.5) | copy-start | bytes 196612
  34.4 13.3 %copy-start.6 = (bf16[256,256]{1,0:T(8,128)(2,1)S(1)}, bf16[256,256]{1,0:T(8,128)(2,1)}, u32[]{:S(2)}) copy-start(bf16[256,256]{1,0:T(8,128)(2,1)} %neigh_weight.1) | copy-start | bytes 393220
  34.4 22.3 %all-to-all-start.1 = ((bf16[64,16,128]{2,1,0:T(8,128)(2,1)}), bf16[64,16,128]{2,1,0:T(8,128)(2,1)S(1)}, u32[]{:S(2)}, u32[]{:S(2)}) async-start(bf16[64,16,128]{2,1,0:T(8,128)(2,1)} %bitcast.11), calls=%async_computation.1 | async-start | bytes 524288 | tf_op jit(solution)/shard_map/all_to_all | solution.py:204
  44.4 27.1 %collective-permute-start.3 = (bf16[512,256]{1,0:T(8,128)(2,1)S(1)}, bf16[512,256]{1,0:T(8,128)(2,1)S(1)}, u32[]{:S(2)}, u32[]{:S(2)}) collective-permute-start(bf16[512,256]{1,0:T(8,128)(2,1)S(1)} %get-tuple-element.24), channel_id=1, source_target_pairs={{0,1},{1,0},{2,3},{3,2},{4,5},{5,4},{6,7},{7,6},{8,9},{9,8},{10,11... | collective-permute-start | bytes 786440 | tf_op jit(solution)/shard_map/ppermute | solution.py:200
  49.1 3.5 %collective-permute-start.5 = (bf16[256,256]{1,0:T(8,128)(2,1)S(1)}, bf16[256,256]{1,0:T(8,128)(2,1)S(1)}, u32[]{:S(2)}, u32[]{:S(2)}) collective-permute-start(bf16[256,256]{1,0:T(8,128)(2,1)S(1)} %get-tuple-element.29), channel_id=1, source_target_pairs={{0,8},{8,0},{1,9},{9,1},{2,10},{10,2},{3,11},{11,3},{4,12},{12,4},... | collective-permute-start | bytes 393224 | tf_op jit(solution)/shard_map/ppermute | solution.py:200
  57.4 25.8 %all-to-all-start.2 = ((bf16[16,16,128]{2,1,0:T(8,128)(2,1)}), bf16[16,16,128]{2,1,0:T(8,128)(2,1)S(1)}, u32[]{:S(2)}, u32[]{:S(2)}) async-start(bf16[16,16,128]{2,1,0:T(8,128)(2,1)} %bitcast.13), calls=%async_computation.2 | async-start | bytes 131072 | tf_op jit(solution)/shard_map/all_to_all | solution.py:204
  72.2 21.1 %collective-permute-start.4 = (bf16[256,256]{1,0:T(8,128)(2,1)S(1)}, bf16[256,256]{1,0:T(8,128)(2,1)S(1)}, u32[]{:S(2)}, u32[]{:S(2)}) collective-permute-start(bf16[256,256]{1,0:T(8,128)(2,1)S(1)} %get-tuple-element.26.refs_1_), channel_id=1, source_target_pairs={{0,4},{1,5},{2,6},{3,7},{4,0},{5,1},{6,2},{7,3},{8,12},{9,13},{10,... | collective-permute-start | bytes 393224 | tf_op jit(solution)/shard_map/ppermute | solution.py:200
  76.0 22.1 %collective-permute-start.7 = (bf16[128,256]{1,0:T(8,128)(2,1)S(1)}, bf16[128,256]{1,0:T(8,128)(2,1)S(1)}, u32[]{:S(2)}, u32[]{:S(2)}) collective-permute-start(bf16[128,256]{1,0:T(8,128)(2,1)S(1)} %get-tuple-element.33.refs_1_), channel_id=1, source_target_pairs={{16,0},{24,8},{32,16},{40,24},{48,32},{56,40},{64,48},{72,56},{80,... | collective-permute-start | bytes 196616 | tf_op jit(solution)/shard_map/ppermute | solution.py:196
  77.3 20.8 %collective-permute-start.8 = (bf16[128,256]{1,0:T(8,128)(2,1)S(1)}, bf16[128,256]{1,0:T(8,128)(2,1)S(1)}, u32[]{:S(2)}, u32[]{:S(2)}) collective-permute-start(bf16[128,256]{1,0:T(8,128)(2,1)S(1)} %get-tuple-element.36), channel_id=1, source_target_pairs={{0,16},{8,24},{16,32},{24,40},{32,48},{40,56},{48,64},{56,72},{64,... | collective-permute-start | bytes 196616 | tf_op jit(solution)/shard_map/ppermute | solution.py:196
  83.9 22.4 %all-to-all-start.3 = ((bf16[64,16,128]{2,1,0:T(8,128)(2,1)}), bf16[64,16,128]{2,1,0:T(8,128)(2,1)S(1)}, u32[]{:S(2)}, u32[]{:S(2)}) async-start(bf16[64,16,128]{2,1,0:T(8,128)(2,1)} %bitcast.15), calls=%async_computation.3 | async-start | bytes 524288 | tf_op jit(solution)/shard_map/all_to_all | solution.py:204
  93.3 4.8 %copy-start.7 = (bf16[256,256]{1,0:T(8,128)(2,1)S(1)}, bf16[256,256]{1,0:T(8,128)(2,1)}, u32[]{:S(2)}) copy-start(bf16[256,256]{1,0:T(8,128)(2,1)} %self_weight.3) | copy-start | bytes 393220
  93.9 10.5 %collective-permute-start.6 = (bf16[128,256]{1,0:T(8,128)(2,1)S(1)}, bf16[128,256]{1,0:T(8,128)(2,1)S(1)}, u32[]{:S(2)}, u32[]{:S(2)}) collective-permute-start(bf16[128,256]{1,0:T(8,128)(2,1)S(1)} %get-tuple-element.34), channel_id=1, source_target_pairs={{0,2},{1,3},{2,0},{3,1},{4,6},{5,7},{6,4},{7,5},{8,10},{9,11},{10,... | collective-permute-start | bytes 196616 | tf_op jit(solution)/shard_map/ppermute | solution.py:200
  99.0 5.4 %copy-start.4 = (s32[128]{0:T(128)S(1)}, s32[128]{0:T(128)}, u32[]{:S(2)}) copy-start(s32[128]{0:T(128)} %param.16) | copy-start | bytes 1540

commit v4 on v3

--- a/solution.py
+++ b/solution.py
@@ -50,7 +50,7 @@
     return pl.CostEstimate(flops=flops, bytes_accessed=moved, transcendentals=0)
 
 
-def pair_body(spot, rows, bands, own, below, above, out):
+def pair_body(spot, own, below, above, out):
     blk = own.shape[0]
     out[:blk, :] = own[...]
     out[blk:, :] = jnp.where(spot[0] == 0, above[...], below[...])
@@ -96,26 +96,33 @@
     return jnp.concatenate([tall] * (width // blk), axis=1)
 
 
-def share_body(degree, cotangent, out, norm, block, share, sems):
+def share_body(degree, cotangent, rows, bands, out, rows_out, bands_out, norm, block, share, sems):
     blk, width = block.shape
     first = pltpu.make_async_copy(degree, norm, sems.at[0])
     second = pltpu.make_async_copy(cotangent, block, sems.at[1])
     first.start()
     second.start()
+    ncol = out.shape[0] // blk
+    tables = [
+        pltpu.make_async_copy(rows, rows_out, sems.at[2 + ncol]),
+        pltpu.make_async_copy(bands, bands_out, sems.at[3 + ncol]),
+    ]
+    for table in tables:
+        table.start()
     first.wait()
     second.wait()
     share[...] = (block[...].astype(jnp.float32) / column(norm, width)).astype(jnp.bfloat16)
     copies = [
         pltpu.make_async_copy(share, out.at[pl.ds(at * blk, blk), :], sems.at[2 + at])
-        for at in range(out.shape[0] // blk)
+        for at in range(ncol)
     ]
     for copy in copies:
         copy.start()
-    for copy in copies:
+    for copy in tables + copies:
         copy.wait()
 
 
-def grads_body(features, cotangent, partial, shares, sent, out, passed):
+def grads_body(features, cotangent, partial, shares, out):
     own = dot(features[...], cotangent[...], 0, 0).astype(jnp.bfloat16)
     neigh = dot(partial[...], shares[...], 0, 0).astype(jnp.bfloat16)
     height, lanes = own.shape[0], out.shape[1]
@@ -124,7 +131,9 @@
         out[(at + 2) * height : (at + 3) * height, :] = neigh[:, at * lanes : (at + 1) * lanes]
 
 
-def backward_body(rows, bands, count, tiles, shares, weight, after, far0, near, own, far1, total):
+def backward_body(
+    rows, bands, count, tiles, shares, weight, after, sent, far0, near, own, far1, passed, total
+):
     slots, blk = tiles.shape[0], tiles.shape[1]
     total[...] = jnp.zeros_like(total)
     for slot in range(slots):
@@ -220,22 +229,25 @@
     factor = 1.0 / math.sqrt(lax.axis_size(ROW) * ncol * blk)
 
     below, above = passed_along(features, 2), passed_along(features, -2)
-    copies = call(
+    table = jax.ShapeDtypeStruct((slots,), jnp.int32)
+    given = [
+        pltpu.with_memory_space_constraint(item, pltpu.HBM)
+        for item in (degree, cotangent, rows, bands)
+    ]
+    copies, rows, bands = call(
         share_body,
-        half(ncol * blk, width),
-        [HB] * 2,
+        [half(ncol * blk, width), table, table],
+        [HB] * 4,
         scratch=[
             pltpu.VMEM((1, blk), jnp.int32),
             pltpu.VMEM((blk, width), jnp.bfloat16),
             pltpu.VMEM((blk, width), jnp.bfloat16),
-            pltpu.SemaphoreType.DMA((2 + ncol,)),
+            pltpu.SemaphoreType.DMA((4 + ncol,)),
         ],
-        out_specs=HB,
-    )(*(pltpu.with_memory_space_constraint(item, pltpu.HBM) for item in (degree, cotangent)))
+        out_specs=[HB, VM, VM],
+    )(*given)
     shares = exchange(copies, "y")
-    pair = call(pair_body, half(2 * blk, width), [SM] * 3 + [VM] * 3)(
-        spot, rows, bands, features, below, above
-    )
+    pair = call(pair_body, half(2 * blk, width), [SM] + [VM] * 3)(spot, features, below, above)
     pair = crossed(pair, "core", 1)
     partial, sent, kept = call(
         forward_body,
@@ -248,24 +260,25 @@
         cost=cost(4 * 10**9, tile_set.size * 2 + 21 * features.size * 2),
     )(rows, bands, count, spot, tile_set, below, pair, features, above)
 
-    grads, sent = call(
+    grads = call(
         grads_body,
-        [half(4 * width, lanes), half(*sent.shape)],
-        [VM] * 4 + [HB],
-        out_specs=[VM, HB],
-        aliases={4: 1},
+        half(4 * width, lanes),
+        [VM] * 4,
         cost=cost(2 * (ncol + 1) * blk * width * width, 18 * features.size * 2),
-    )(features, cotangent, partial, shares, sent)
+    )(features, cotangent, partial, shares)
     scattered = exchange(grads, NEAR)
-    came = crossed(sent, "y", 1)
-
-    far0, near_landed, own, far1 = call(
+
+    far0, near_landed, own, far1, sent = call(
         backward_body,
-        [half(blk, width), half(2 * blk, width), half(blk, width), half(blk, width)],
-        [SM] * 3 + [VM] * 3 + [HB],
+        [half(blk, width), half(2 * blk, width), half(blk, width), half(blk, width)]
+        + [half(*sent.shape)],
+        [SM] * 3 + [VM] * 3 + [HB] * 2,
+        out_specs=[VM] * 4 + [HB],
+        aliases={7: 4},
         scratch=[pltpu.VMEM((WIDE + 1, blk, width), jnp.float32)],
         cost=cost(5 * 10**9, tile_set.size * 2 + 13 * features.size * 2),
-    )(rows, bands, count, tile_set, shares, neigh_weight, grads)
+    )(rows, bands, count, tile_set, shares, neigh_weight, grads, sent)
+    came = crossed(sent, "y", 1)
     near_landed = crossed(near_landed, "core", 1)
     sent, kept = call(
         halve_body(blk, 2),

time: 108 us -> 107 us (level)
  no operation moved by 1% of the time
where the time goes in v4:
time: 107 us; the launch traced here: 106 us
  starting transfers between devices  78.9 us (74%)
  waiting for transfers between devices  14.3 us (13%)
  Pallas kernels  11.7 us (11%)
  between operations  1.54 us (1%)
    all_to_all x4, starting transfers between devices, exchange(): return lax.all_to_all(value, axes, 0, 0, tiled=True)  41.4 us
    ppermute x5, starting transfers between devices, crossed(): lax.ppermute(value, axis, [(at, at ^ flip) for at in range(lax.axis_size(...  26.9 us
    ppermute x4, starting transfers between devices, passed_along(): lax.ppermute(value, ROW, [(source, source + steps) for source in range(le...  10.6 us
    ppermute x5, waiting for transfers between devices, crossed(): lax.ppermute(value, axis, [(at, at ^ flip) for at in range(lax.axis_size(...  6.7 us
    all_to_all x4, waiting for transfers between devices, exchange(): return lax.all_to_all(value, axes, 0, 0, tiled=True)  6.32 us
  transfers between devices with their start and end apart: 13, of which 7 were waited for; matrix products, arithmetic and copies ran while one was open for 0% of the time, Pallas kernels for 7%

profile of v4, /device:TPU:1, one launch (start us, length us, event | category | flops | bytes accessed | tf_op | source)
XLA Modules:
  0.0 106.5 jit_solution(573545181141866624)
XLA Ops:
  0.6 1.9 %shard_map.120 = (bf16[1024,256]{1,0:T(8,128)(2,1)}, s32[16]{0:T(128)S(1)}, s32[16]{0:T(128)S(1)}) custom-call(s32[1,128]{1,0:T(1,128)} %bitcast.24, bf16[128,256]{1,0:T(8,128)(2,1)} %cotangent.5, s32[16]{0:T(128)} %bitcast.28, s32[16]{0:T(128)} %bitcast.29), custom_call_target="tpu_custom_call" | custom-call | tf_op jit(solution)/shard_map/pallas_call | solution.py:237
  2.5 0.0 copy-start
  2.5 0.0 copy-start.3
  2.5 7.8 %all-to-all-start = ((bf16[8,128,256]{2,1,0:T(8,128)(2,1)}), bf16[8,128,256]{2,1,0:T(8,128)(2,1)S(1)}, u32[]{:S(2)}, u32[]{:S(2)}) async-start(bf16[8,128,256]{2,1,0:T(8,128)(2,1)} %bitcast.9), calls=%async_computation | async-start | bytes 1048576 | tf_op jit(solution)/shard_map/all_to_all | solution.py:213
  10.3 0.0 copy-done
  10.3 1.3 %collective-permute-start.1 = (bf16[128,256]{1,0:T(8,128)(2,1)S(1)}, bf16[128,256]{1,0:T(8,128)(2,1)S(1)}, u32[]{:S(2)}, u32[]{:S(2)}) collective-permute-start(bf16[128,256]{1,0:T(8,128)(2,1)S(1)} %copy-done), channel_id=1, source_target_pairs={{16,0},{24,8},{32,16},{40,24},{48,32},{56,40},{64,48},{72,56},{80,... | collective-permute-start | bytes 196616 | tf_op jit(solution)/shard_map/ppermute | solution.py:205
  11.6 4.0 %collective-permute-start = (bf16[128,256]{1,0:T(8,128)(2,1)S(1)}, bf16[128,256]{1,0:T(8,128)(2,1)S(1)}, u32[]{:S(2)}, u32[]{:S(2)}) collective-permute-start(bf16[128,256]{1,0:T(8,128)(2,1)S(1)} %copy-done), channel_id=1, source_target_pairs={{0,16},{8,24},{16,32},{24,40},{32,48},{40,56},{48,64},{56,72},{64,... | collective-permute-start | bytes 196616 | tf_op jit(solution)/shard_map/ppermute | solution.py:205
  15.6 0.1 pad_add_fusion.spot
  15.7 0.0 collective-permute-done.1.above.f4
  15.7 1.2 %collective-permute-done.below.f0 = bf16[128,256]{1,0:T(8,128)(2,1)S(1)} collective-permute-done((bf16[128,256]{1,0:T(8,128)(2,1)S(1)}, bf16[128,256]{1,0:T(8,128)(2,1)S(1)}, u32[]{:S(2)}, u32[]{:S(2)}) %collective-permute-start) | collective-permute-done | bytes 65568 | tf_op jit(solution)/shard_map/ppermute | solution.py:205
  17.0 0.6 shard_map.121
  17.5 13.0 %collective-permute-start.2 = (bf16[256,256]{1,0:T(8,128)(2,1)S(1)}, bf16[256,256]{1,0:T(8,128)(2,1)S(1)}, u32[]{:S(2)}, u32[]{:S(2)}) collective-permute-start(bf16[256,256]{1,0:T(8,128)(2,1)S(1)} %shard_map.121), channel_id=1, source_target_pairs={{0,8},{8,0},{1,9},{9,1},{2,10},{10,2},{3,11},{11,3},{4,12},{12,4},... | collective-permute-start | bytes 393224 | tf_op jit(solution)/shard_map/ppermute | solution.py:209
  31.2 0.3 collective-permute-done.2.pair
  31.5 0.0 copy-done.3
  31.5 1.1 %shard_map.122 = (bf16[1024,256]{1,0:T(8,128)(2,1)S(1)}, bf16[512,256]{1,0:T(8,128)(2,1)S(1)}, bf16[512,256]{1,0:T(8,128)(2,1)S(1)}) custom-call(s32[16]{0:T(128)S(1)} %get-tuple-element.24.rows, s32[16]{0:T(128)S(1)} %get-tuple-element.25.bands, s32[1]{0:T(128)} %bitcast.17.count, s32[4]{0:T(128)S(1)} %pad_add_fusion.spot, ...), custom_call_target="tpu_custom_call" | custom-call | flops 4000000000 | bytes 1900544 | tf_op jit(solution)/shard_map/pallas_call | solution.py:252
  32.7 0.0 all-to-all-done
  32.7 0.0 copy-done.1
  32.7 1.1 %shard_map.123.after = bf16[1024,128]{1,0:T(8,128)(2,1)} custom-call(bf16[128,256]{1,0:T(8,128)(2,1)S(1)} %copy-done, bf16[128,256]{1,0:T(8,128)(2,1)S(1)} %copy-done.1, bf16[1024,256]{1,0:T(8,128)(2,1)S(1)} %get-tuple-element.27.partial, bf16[1024,256]{1,0:T(8,128)(2,1)S(1)} %bitcast.19), custom_call_target="tpu_custom_call" | custom-call | flops 150994944 | bytes 1179648 | tf_op jit(solution)/shard_map/pallas_call | solution.py:263
  33.8 10.0 %all-to-all-start.1 = ((bf16[64,16,128]{2,1,0:T(8,128)(2,1)}), bf16[64,16,128]{2,1,0:T(8,128)(2,1)S(1)}, u32[]{:S(2)}, u32[]{:S(2)}) async-start(bf16[64,16,128]{2,1,0:T(8,128)(2,1)} %bitcast.11), calls=%async_computation.1 | async-start | bytes 524288 | tf_op jit(solution)/shard_map/all_to_all | solution.py:213
  43.8 0.0 copy-done.4
  43.8 1.4 %shard_map.124 = (bf16[128,256]{1,0:T(8,128)(2,1)S(1)}, bf16[256,256]{1,0:T(8,128)(2,1)S(1)}, bf16[128,256]{1,0:T(8,128)(2,1)S(1)}, bf16[128,256]{1,0:T(8,128)(2,1)S(1)}, bf16[512,256]{1,0:T(8,128)(2,1)S(1)}) custom-call(s32[16]{0:T(128)S(1)} %get-tuple-element.24.rows, s32[16]{0:T(128)S(1)} %get-tuple-element.25.bands, ...), custom_call_target="tpu_custom_call", output_to_operand_aliasing={{4}: (7, {})} | custom-call | flops 5000000000 | bytes 1376256 | tf_op jit(solution)/shard_map/pallas_call | solution.py:271
  45.2 3.3 %collective-permute-start.3 = (bf16[512,256]{1,0:T(8,128)(2,1)S(1)}, bf16[512,256]{1,0:T(8,128)(2,1)S(1)}, u32[]{:S(2)}, u32[]{:S(2)}) collective-permute-start(bf16[512,256]{1,0:T(8,128)(2,1)S(1)} %get-tuple-element.29), channel_id=1, source_target_pairs={{0,1},{1,0},{2,3},{3,2},{4,5},{5,4},{6,7},{7,6},{8,9},{9,8},{10,11... | collective-permute-start | bytes 786440 | tf_op jit(solution)/shard_map/ppermute | solution.py:209
  48.5 2.6 %collective-permute-start.5 = (bf16[256,256]{1,0:T(8,128)(2,1)S(1)}, bf16[256,256]{1,0:T(8,128)(2,1)S(1)}, u32[]{:S(2)}, u32[]{:S(2)}) collective-permute-start(bf16[256,256]{1,0:T(8,128)(2,1)S(1)} %get-tuple-element.33), channel_id=1, source_target_pairs={{0,8},{8,0},{1,9},{9,1},{2,10},{10,2},{3,11},{11,3},{4,12},{12,4},... | collective-permute-start | bytes 393224 | tf_op jit(solution)/shard_map/ppermute | solution.py:209
  51.0 1.0 collective-permute-done.5.came
  52.0 0.6 shard_map.126
  52.6 3.4 %all-to-all-done.1 = bf16[64,16,128]{2,1,0:T(8,128)(2,1)S(1)} async-done(((bf16[64,16,128]{2,1,0:T(8,128)(2,1)}), bf16[64,16,128]{2,1,0:T(8,128)(2,1)S(1)}, u32[]{:S(2)}, u32[]{:S(2)}) %all-to-all-start.1) | async-done | bytes 262176 | tf_op jit(solution)/shard_map/all_to_all | solution.py:213
  56.0 0.7 shard_map.127
  56.7 14.2 %all-to-all-start.2 = ((bf16[16,16,128]{2,1,0:T(8,128)(2,1)}), bf16[16,16,128]{2,1,0:T(8,128)(2,1)S(1)}, u32[]{:S(2)}, u32[]{:S(2)}) async-start(bf16[16,16,128]{2,1,0:T(8,128)(2,1)} %bitcast.13), calls=%async_computation.2 | async-start | bytes 131072 | tf_op jit(solution)/shard_map/all_to_all | solution.py:213
  70.9 0.0 collective-permute-done.3.came
  70.9 0.6 shard_map.125
  71.5 3.8 %collective-permute-start.4 = (bf16[256,256]{1,0:T(8,128)(2,1)S(1)}, bf16[256,256]{1,0:T(8,128)(2,1)S(1)}, u32[]{:S(2)}, u32[]{:S(2)}) collective-permute-start(bf16[256,256]{1,0:T(8,128)(2,1)S(1)} %get-tuple-element.31.refs_1_), channel_id=1, source_target_pairs={{0,4},{1,5},{2,6},{3,7},{4,0},{5,1},{6,2},{7,3},{8,12},{9,13},{10,... | collective-permute-start | bytes 393224 | tf_op jit(solution)/shard_map/ppermute | solution.py:209
  75.4 1.3 %collective-permute-start.7 = (bf16[128,256]{1,0:T(8,128)(2,1)S(1)}, bf16[128,256]{1,0:T(8,128)(2,1)S(1)}, u32[]{:S(2)}, u32[]{:S(2)}) collective-permute-start(bf16[128,256]{1,0:T(8,128)(2,1)S(1)} %get-tuple-element.37.refs_1_), channel_id=1, source_target_pairs={{16,0},{24,8},{32,16},{40,24},{48,32},{56,40},{64,48},{72,56},{80,... | collective-permute-start | bytes 196616 | tf_op jit(solution)/shard_map/ppermute | solution.py:205
  76.7 4.0 %collective-permute-start.8 = (bf16[128,256]{1,0:T(8,128)(2,1)S(1)}, bf16[128,256]{1,0:T(8,128)(2,1)S(1)}, u32[]{:S(2)}, u32[]{:S(2)}) collective-permute-start(bf16[128,256]{1,0:T(8,128)(2,1)S(1)} %get-tuple-element.40), channel_id=1, source_target_pairs={{0,16},{8,24},{16,32},{24,40},{32,48},{40,56},{48,64},{56,72},{64,... | collective-permute-start | bytes 196616 | tf_op jit(solution)/shard_map/ppermute | solution.py:205
  80.7 1.8 %all-to-all-done.2 = bf16[16,16,128]{2,1,0:T(8,128)(2,1)S(1)} async-done(((bf16[16,16,128]{2,1,0:T(8,128)(2,1)}), bf16[16,16,128]{2,1,0:T(8,128)(2,1)S(1)}, u32[]{:S(2)}, u32[]{:S(2)}) %all-to-all-start.2) | async-done | bytes 65568 | tf_op jit(solution)/shard_map/all_to_all | solution.py:213
  82.5 0.7 shard_map.128.rest_0_
  83.2 9.4 %all-to-all-start.3 = ((bf16[64,16,128]{2,1,0:T(8,128)(2,1)}), bf16[64,16,128]{2,1,0:T(8,128)(2,1)S(1)}, u32[]{:S(2)}, u32[]{:S(2)}) async-start(bf16[64,16,128]{2,1,0:T(8,128)(2,1)} %bitcast.15), calls=%async_computation.3 | async-start | bytes 524288 | tf_op jit(solution)/shard_map/all_to_all | solution.py:213
  92.6 0.0 collective-permute-done.4.came
  92.6 0.0 copy-start.5
  92.7 0.6 shard_map.129
  93.2 4.2 %collective-permute-start.6 = (bf16[128,256]{1,0:T(8,128)(2,1)S(1)}, bf16[128,256]{1,0:T(8,128)(2,1)S(1)}, u32[]{:S(2)}, u32[]{:S(2)}) collective-permute-start(bf16[128,256]{1,0:T(8,128)(2,1)S(1)} %get-tuple-element.38), channel_id=1, source_target_pairs={{0,2},{1,3},{2,0},{3,1},{4,6},{5,7},{6,4},{7,5},{8,10},{9,11},{10,... | collective-permute-start | bytes 196616 | tf_op jit(solution)/shard_map/ppermute | solution.py:209
  97.4 0.0 collective-permute-done.8.high
  97.4 0.0 collective-permute-done.7.low
  97.5 0.0 copy-done.5
  97.5 0.8 shard_map.131
  98.3 5.4 %collective-permute-done.6.came = bf16[128,256]{1,0:T(8,128)(2,1)S(1)} collective-permute-done((bf16[128,256]{1,0:T(8,128)(2,1)S(1)}, bf16[128,256]{1,0:T(8,128)(2,1)S(1)}, u32[]{:S(2)}, u32[]{:S(2)}) %collective-permute-start.6) | collective-permute-done | bytes 65568 | tf_op jit(solution)/shard_map/ppermute | solution.py:209
  103.7 0.9 shard_map.130
  104.6 1.1 %all-to-all-done.3 = bf16[64,16,128]{2,1,0:T(8,128)(2,1)S(1)} async-done(((bf16[64,16,128]{2,1,0:T(8,128)(2,1)}), bf16[64,16,128]{2,1,0:T(8,128)(2,1)S(1)}, u32[]{:S(2)}, u32[]{:S(2)}) %all-to-all-start.3) | async-done | bytes 262176 | tf_op jit(solution)/shard_map/all_to_all | solution.py:213
  105.7 0.8 shard_map.132
  (4 shorter events, 0.0 us)
Async XLA Ops:
  2.5 7.8 %copy-start = (bf16[128,256]{1,0:T(8,128)(2,1)S(1)}, bf16[128,256]{1,0:T(8,128)(2,1)}, u32[]{:S(2)}) copy-start(bf16[128,256]{1,0:T(8,128)(2,1)} %features.3) | copy-start | bytes 196612
  2.5 29.0 %copy-start.3 = (bf16[1,1,16,128,128]{4,3,2,1,0:T(8,128)(2,1)S(1)}, bf16[1,1,16,128,128]{4,3,2,1,0:T(8,128)(2,1)}, u32[]{:S(2)}) copy-start(bf16[1,1,16,128,128]{4,3,2,1,0:T(8,128)(2,1)} %param.12) | copy-start | bytes 1572868
  2.5 30.1 %all-to-all-start = ((bf16[8,128,256]{2,1,0:T(8,128)(2,1)}), bf16[8,128,256]{2,1,0:T(8,128)(2,1)S(1)}, u32[]{:S(2)}, u32[]{:S(2)}) async-start(bf16[8,128,256]{2,1,0:T(8,128)(2,1)} %bitcast.9), calls=%async_computation | async-start | bytes 1048576 | tf_op jit(solution)/shard_map/all_to_all | solution.py:213
  10.3 5.4 %collective-permute-start.1 = (bf16[128,256]{1,0:T(8,128)(2,1)S(1)}, bf16[128,256]{1,0:T(8,128)(2,1)S(1)}, u32[]{:S(2)}, u32[]{:S(2)}) collective-permute-start(bf16[128,256]{1,0:T(8,128)(2,1)S(1)} %copy-done), channel_id=1, source_target_pairs={{16,0},{24,8},{32,16},{40,24},{48,32},{56,40},{64,48},{72,56},{80,... | collective-permute-start | bytes 196616 | tf_op jit(solution)/shard_map/ppermute | solution.py:205
  11.6 5.3 %collective-permute-start = (bf16[128,256]{1,0:T(8,128)(2,1)S(1)}, bf16[128,256]{1,0:T(8,128)(2,1)S(1)}, u32[]{:S(2)}, u32[]{:S(2)}) collective-permute-start(bf16[128,256]{1,0:T(8,128)(2,1)S(1)} %copy-done), channel_id=1, source_target_pairs={{0,16},{8,24},{16,32},{24,40},{32,48},{40,56},{48,64},{56,72},{64,... | collective-permute-start | bytes 196616 | tf_op jit(solution)/shard_map/ppermute | solution.py:205
  17.5 14.0 %collective-permute-start.2 = (bf16[256,256]{1,0:T(8,128)(2,1)S(1)}, bf16[256,256]{1,0:T(8,128)(2,1)S(1)}, u32[]{:S(2)}, u32[]{:S(2)}) collective-permute-start(bf16[256,256]{1,0:T(8,128)(2,1)S(1)} %shard_map.121), channel_id=1, source_target_pairs={{0,8},{8,0},{1,9},{9,1},{2,10},{10,2},{3,11},{11,3},{4,12},{12,4},... | collective-permute-start | bytes 393224 | tf_op jit(solution)/shard_map/ppermute | solution.py:209
  31.5 1.1 %copy-start.1 = (bf16[128,256]{1,0:T(8,128)(2,1)S(1)}, bf16[128,256]{1,0:T(8,128)(2,1)}, u32[]{:S(2)}) copy-start(bf16[128,256]{1,0:T(8,128)(2,1)} %cotangent.5) | copy-start | bytes 196612
  33.8 10.0 %copy-start.4 = (bf16[256,256]{1,0:T(8,128)(2,1)S(1)}, bf16[256,256]{1,0:T(8,128)(2,1)}, u32[]{:S(2)}) copy-start(bf16[256,256]{1,0:T(8,128)(2,1)} %neigh_weight.1) | copy-start | bytes 393220
  33.8 22.2 %all-to-all-start.1 = ((bf16[64,16,128]{2,1,0:T(8,128)(2,1)}), bf16[64,16,128]{2,1,0:T(8,128)(2,1)S(1)}, u32[]{:S(2)}, u32[]{:S(2)}) async-start(bf16[64,16,128]{2,1,0:T(8,128)(2,1)} %bitcast.11), calls=%async_computation.1 | async-start | bytes 524288 | tf_op jit(solution)/shard_map/all_to_all | solution.py:213
  45.2 25.8 %collective-permute-start.3 = (bf16[512,256]{1,0:T(8,128)(2,1)S(1)}, bf16[512,256]{1,0:T(8,128)(2,1)S(1)}, u32[]{:S(2)}, u32[]{:S(2)}) collective-permute-start(bf16[512,256]{1,0:T(8,128)(2,1)S(1)} %get-tuple-element.29), channel_id=1, source_target_pairs={{0,1},{1,0},{2,3},{3,2},{4,5},{5,4},{6,7},{7,6},{8,9},{9,8},{10,11... | collective-permute-start | bytes 786440 | tf_op jit(solution)/shard_map/ppermute | solution.py:209
  48.5 3.5 %collective-permute-start.5 = (bf16[256,256]{1,0:T(8,128)(2,1)S(1)}, bf16[256,256]{1,0:T(8,128)(2,1)S(1)}, u32[]{:S(2)}, u32[]{:S(2)}) collective-permute-start(bf16[256,256]{1,0:T(8,128)(2,1)S(1)} %get-tuple-element.33), channel_id=1, source_target_pairs={{0,8},{8,0},{1,9},{9,1},{2,10},{10,2},{3,11},{11,3},{4,12},{12,4},... | collective-permute-start | bytes 393224 | tf_op jit(solution)/shard_map/ppermute | solution.py:209
  56.7 25.8 %all-to-all-start.2 = ((bf16[16,16,128]{2,1,0:T(8,128)(2,1)}), bf16[16,16,128]{2,1,0:T(8,128)(2,1)S(1)}, u32[]{:S(2)}, u32[]{:S(2)}) async-start(bf16[16,16,128]{2,1,0:T(8,128)(2,1)} %bitcast.13), calls=%async_computation.2 | async-start | bytes 131072 | tf_op jit(solution)/shard_map/all_to_all | solution.py:213
  71.5 21.1 %collective-permute-start.4 = (bf16[256,256]{1,0:T(8,128)(2,1)S(1)}, bf16[256,256]{1,0:T(8,128)(2,1)S(1)}, u32[]{:S(2)}, u32[]{:S(2)}) collective-permute-start(bf16[256,256]{1,0:T(8,128)(2,1)S(1)} %get-tuple-element.31.refs_1_), channel_id=1, source_target_pairs={{0,4},{1,5},{2,6},{3,7},{4,0},{5,1},{6,2},{7,3},{8,12},{9,13},{10,... | collective-permute-start | bytes 393224 | tf_op jit(solution)/shard_map/ppermute | solution.py:209
  75.4 22.1 %collective-permute-start.7 = (bf16[128,256]{1,0:T(8,128)(2,1)S(1)}, bf16[128,256]{1,0:T(8,128)(2,1)S(1)}, u32[]{:S(2)}, u32[]{:S(2)}) collective-permute-start(bf16[128,256]{1,0:T(8,128)(2,1)S(1)} %get-tuple-element.37.refs_1_), channel_id=1, source_target_pairs={{16,0},{24,8},{32,16},{40,24},{48,32},{56,40},{64,48},{72,56},{80,... | collective-permute-start | bytes 196616 | tf_op jit(solution)/shard_map/ppermute | solution.py:205
  76.7 20.8 %collective-permute-start.8 = (bf16[128,256]{1,0:T(8,128)(2,1)S(1)}, bf16[128,256]{1,0:T(8,128)(2,1)S(1)}, u32[]{:S(2)}, u32[]{:S(2)}) collective-permute-start(bf16[128,256]{1,0:T(8,128)(2,1)S(1)} %get-tuple-element.40), channel_id=1, source_target_pairs={{0,16},{8,24},{16,32},{24,40},{32,48},{40,56},{48,64},{56,72},{64,... | collective-permute-start | bytes 196616 | tf_op jit(solution)/shard_map/ppermute | solution.py:205
  83.2 22.4 %all-to-all-start.3 = ((bf16[64,16,128]{2,1,0:T(8,128)(2,1)}), bf16[64,16,128]{2,1,0:T(8,128)(2,1)S(1)}, u32[]{:S(2)}, u32[]{:S(2)}) async-start(bf16[64,16,128]{2,1,0:T(8,128)(2,1)} %bitcast.15), calls=%async_computation.3 | async-start | bytes 524288 | tf_op jit(solution)/shard_map/all_to_all | solution.py:213
  92.6 4.8 %copy-start.5 = (bf16[256,256]{1,0:T(8,128)(2,1)S(1)}, bf16[256,256]{1,0:T(8,128)(2,1)}, u32[]{:S(2)}) copy-start(bf16[256,256]{1,0:T(8,128)(2,1)} %self_weight.3) | copy-start | bytes 393220
  93.2 10.5 %collective-permute-start.6 = (bf16[128,256]{1,0:T(8,128)(2,1)S(1)}, bf16[128,256]{1,0:T(8,128)(2,1)S(1)}, u32[]{:S(2)}, u32[]{:S(2)}) collective-permute-start(bf16[128,256]{1,0:T(8,128)(2,1)S(1)} %get-tuple-element.38), channel_id=1, source_target_pairs={{0,2},{1,3},{2,0},{3,1},{4,6},{5,7},{6,4},{7,5},{8,10},{9,11},{10,... | collective-permute-start | bytes 196616 | tf_op jit(solution)/shard_map/ppermute | solution.py:209
  98.3 5.4 %copy-start.2 = (s32[128]{0:T(128)S(1)}, s32[128]{0:T(128)}, u32[]{:S(2)}) copy-start(s32[128]{0:T(128)} %param.16) | copy-start | bytes 1540

commit v5 on v4

--- a/solution.py
+++ b/solution.py
@@ -166,7 +166,7 @@
     return total
 
 
-def fold_spread(value, members, copies, after=()):
+def fold_spread(value, members, copies, after=(), weight=0):
     rows, lanes = value.shape[0] // members, value.shape[1]
 
     def body(*refs):
@@ -174,7 +174,9 @@
         for at in range(copies):
             refs[-1][at * rows : (at + 1) * rows, :] = total
 
-    return call(body, half(copies * rows, lanes), [VM] + [HB] * len(after))(value, *after)
+    return call(
+        body, half(copies * rows, lanes), [VM] + [HB] * len(after), cost=cost(weight, 0)
+    )(value, *after)
 
 
 def finish_body(factor, source, own, neigh):
@@ -280,16 +282,16 @@
     )(rows, bands, count, tile_set, shares, neigh_weight, grads, sent)
     came = crossed(sent, "y", 1)
     near_landed = crossed(near_landed, "core", 1)
+    low, high, mid = call(
+        merge_body, [half(blk, width)] * 2 + [full(blk, width)], [SM] + [VM] * 4
+    )(spot, near_landed, far0, far1, own)
     sent, kept = call(
         halve_body(blk, 2),
         [half(ncol // 4 * blk, width), full(ncol // 4 * blk, width)],
-        [SM] + [VM] * 2,
-    )(spot, came, kept)
-    low, high, mid = call(
-        merge_body, [half(blk, width)] * 2 + [full(blk, width)], [SM] + [VM] * 4
-    )(spot, near_landed, far0, far1, own)
-
-    joined = fold_spread(scattered, near, far, after=[low])
+        [SM] + [VM] * 2 + [HB],
+    )(spot, came, kept, low)
+
+    joined = fold_spread(scattered, near, far, after=[far0], weight=5 * 10**9)
     joined = exchange(joined, "z")
 
     came = crossed(sent, "y", 4)

time: 107 us -> 107 us (level)
  transfers between devices with their start and end apart: 13 -> 13, of which waited for: 7 -> 6; matrix products, arithmetic and copies ran while one was open for 0% -> 0% of each run, Pallas kernels for 7% -> 7%
where the time goes in v5:
time: 107 us
  starting transfers between devices  79.3 us (74%)
  waiting for transfers between devices  14.1 us (13%)
  Pallas kernels  11.7 us (11%)
  between operations  1.54 us (1%)
    all_to_all x4, starting transfers between devices, exchange(): return lax.all_to_all(value, axes, 0, 0, tiled=True)  41.9 us
    ppermute x5, starting transfers between devices, crossed(): lax.ppermute(value, axis, [(at, at ^ flip) for at in range(lax.axis_size(...  26.8 us
    ppermute x4, starting transfers between devices, passed_along(): lax.ppermute(value, ROW, [(source, source + steps) for source in range(le...  10.6 us
    all_to_all x4, waiting for transfers between devices, exchange(): return lax.all_to_all(value, axes, 0, 0, tiled=True)  7.12 us
    ppermute x5, waiting for transfers between devices, crossed(): lax.ppermute(value, axis, [(at, at ^ flip) for at in range(lax.axis_size(...  5.74 us
  transfers between devices with their start and end apart: 13, of which 6 were waited for; matrix products, arithmetic and copies ran while one was open for 0% of the time, Pallas kernels for 7%

profile of v5, /device:TPU:1, one launch (start us, length us, event | category | flops | bytes accessed | tf_op | source)
XLA Modules:
  0.0 106.7 jit_solution(14363437336086331728)
XLA Ops:
  0.6 1.9 %shard_map.120 = (bf16[1024,256]{1,0:T(8,128)(2,1)}, s32[16]{0:T(128)S(1)}, s32[16]{0:T(128)S(1)}) custom-call(s32[1,128]{1,0:T(1,128)} %bitcast.24, bf16[128,256]{1,0:T(8,128)(2,1)} %cotangent.5, s32[16]{0:T(128)} %bitcast.28, s32[16]{0:T(128)} %bitcast.29), custom_call_target="tpu_custom_call" | custom-call | tf_op jit(solution)/shard_map/pallas_call | solution.py:239
  2.5 0.0 copy-start
  2.5 0.0 copy-start.3
  2.5 7.8 %all-to-all-start = ((bf16[8,128,256]{2,1,0:T(8,128)(2,1)}), bf16[8,128,256]{2,1,0:T(8,128)(2,1)S(1)}, u32[]{:S(2)}, u32[]{:S(2)}) async-start(bf16[8,128,256]{2,1,0:T(8,128)(2,1)} %bitcast.9), calls=%async_computation | async-start | bytes 1048576 | tf_op jit(solution)/shard_map/all_to_all | solution.py:215
  10.3 0.0 copy-done
  10.3 1.3 %collective-permute-start.1 = (bf16[128,256]{1,0:T(8,128)(2,1)S(1)}, bf16[128,256]{1,0:T(8,128)(2,1)S(1)}, u32[]{:S(2)}, u32[]{:S(2)}) collective-permute-start(bf16[128,256]{1,0:T(8,128)(2,1)S(1)} %copy-done), channel_id=1, source_target_pairs={{16,0},{24,8},{32,16},{40,24},{48,32},{56,40},{64,48},{72,56},{80,... | collective-permute-start | bytes 196616 | tf_op jit(solution)/shard_map/ppermute | solution.py:207
  11.6 4.0 %collective-permute-start = (bf16[128,256]{1,0:T(8,128)(2,1)S(1)}, bf16[128,256]{1,0:T(8,128)(2,1)S(1)}, u32[]{:S(2)}, u32[]{:S(2)}) collective-permute-start(bf16[128,256]{1,0:T(8,128)(2,1)S(1)} %copy-done), channel_id=1, source_target_pairs={{0,16},{8,24},{16,32},{24,40},{32,48},{40,56},{48,64},{56,72},{64,... | collective-permute-start | bytes 196616 | tf_op jit(solution)/shard_map/ppermute | solution.py:207
  15.6 0.1 pad_add_fusion.spot
  15.7 0.0 collective-permute-done.1.above.f4
  15.7 1.2 %collective-permute-done.below.f0 = bf16[128,256]{1,0:T(8,128)(2,1)S(1)} collective-permute-done((bf16[128,256]{1,0:T(8,128)(2,1)S(1)}, bf16[128,256]{1,0:T(8,128)(2,1)S(1)}, u32[]{:S(2)}, u32[]{:S(2)}) %collective-permute-start) | collective-permute-done | bytes 65568 | tf_op jit(solution)/shard_map/ppermute | solution.py:207
  17.0 0.6 shard_map.121
  17.5 13.0 %collective-permute-start.2 = (bf16[256,256]{1,0:T(8,128)(2,1)S(1)}, bf16[256,256]{1,0:T(8,128)(2,1)S(1)}, u32[]{:S(2)}, u32[]{:S(2)}) collective-permute-start(bf16[256,256]{1,0:T(8,128)(2,1)S(1)} %shard_map.121), channel_id=1, source_target_pairs={{0,8},{8,0},{1,9},{9,1},{2,10},{10,2},{3,11},{11,3},{4,12},{12,4},... | collective-permute-start | bytes 393224 | tf_op jit(solution)/shard_map/ppermute | solution.py:211
  31.2 0.3 collective-permute-done.2.pair
  31.5 0.0 copy-done.3
  31.5 1.1 %shard_map.122 = (bf16[1024,256]{1,0:T(8,128)(2,1)S(1)}, bf16[512,256]{1,0:T(8,128)(2,1)S(1)}, bf16[512,256]{1,0:T(8,128)(2,1)S(1)}) custom-call(s32[16]{0:T(128)S(1)} %get-tuple-element.24.rows, s32[16]{0:T(128)S(1)} %get-tuple-element.25.bands, s32[1]{0:T(128)} %bitcast.17.count, s32[4]{0:T(128)S(1)} %pad_add_fusion.spot, ...), custom_call_target="tpu_custom_call" | custom-call | flops 4000000000 | bytes 1900544 | tf_op jit(solution)/shard_map/pallas_call | solution.py:254
  32.7 0.0 all-to-all-done
  32.7 0.0 copy-done.1
  32.7 1.1 %shard_map.123.after = bf16[1024,128]{1,0:T(8,128)(2,1)} custom-call(bf16[128,256]{1,0:T(8,128)(2,1)S(1)} %copy-done, bf16[128,256]{1,0:T(8,128)(2,1)S(1)} %copy-done.1, bf16[1024,256]{1,0:T(8,128)(2,1)S(1)} %get-tuple-element.27.partial, bf16[1024,256]{1,0:T(8,128)(2,1)S(1)} %bitcast.19), custom_call_target="tpu_custom_call" | custom-call | flops 150994944 | bytes 1179648 | tf_op jit(solution)/shard_map/pallas_call | solution.py:265
  33.8 10.0 %all-to-all-start.1 = ((bf16[64,16,128]{2,1,0:T(8,128)(2,1)}), bf16[64,16,128]{2,1,0:T(8,128)(2,1)S(1)}, u32[]{:S(2)}, u32[]{:S(2)}) async-start(bf16[64,16,128]{2,1,0:T(8,128)(2,1)} %bitcast.11), calls=%async_computation.1 | async-start | bytes 524288 | tf_op jit(solution)/shard_map/all_to_all | solution.py:215
  43.8 0.0 copy-done.4
  43.8 1.4 %shard_map.124 = (bf16[128,256]{1,0:T(8,128)(2,1)S(1)}, bf16[256,256]{1,0:T(8,128)(2,1)S(1)}, bf16[128,256]{1,0:T(8,128)(2,1)S(1)}, bf16[128,256]{1,0:T(8,128)(2,1)S(1)}, bf16[512,256]{1,0:T(8,128)(2,1)S(1)}) custom-call(s32[16]{0:T(128)S(1)} %get-tuple-element.24.rows, s32[16]{0:T(128)S(1)} %get-tuple-element.25.bands, ...), custom_call_target="tpu_custom_call", output_to_operand_aliasing={{4}: (7, {})} | custom-call | flops 5000000000 | bytes 1376256 | tf_op jit(solution)/shard_map/pallas_call | solution.py:273
  45.2 2.4 %collective-permute-start.4 = (bf16[256,256]{1,0:T(8,128)(2,1)S(1)}, bf16[256,256]{1,0:T(8,128)(2,1)S(1)}, u32[]{:S(2)}, u32[]{:S(2)}) collective-permute-start(bf16[256,256]{1,0:T(8,128)(2,1)S(1)} %get-tuple-element.31), channel_id=1, source_target_pairs={{0,8},{8,0},{1,9},{9,1},{2,10},{10,2},{3,11},{11,3},{4,12},{12,4},... | collective-permute-start | bytes 393224 | tf_op jit(solution)/shard_map/ppermute | solution.py:211
  47.5 3.2 %collective-permute-start.3 = (bf16[512,256]{1,0:T(8,128)(2,1)S(1)}, bf16[512,256]{1,0:T(8,128)(2,1)S(1)}, u32[]{:S(2)}, u32[]{:S(2)}) collective-permute-start(bf16[512,256]{1,0:T(8,128)(2,1)S(1)} %get-tuple-element.29), channel_id=1, source_target_pairs={{0,1},{1,0},{2,3},{3,2},{4,5},{5,4},{6,7},{7,6},{8,9},{9,8},{10,11... | collective-permute-start | bytes 786440 | tf_op jit(solution)/shard_map/ppermute | solution.py:211
  50.8 5.1 %all-to-all-done.1 = bf16[64,16,128]{2,1,0:T(8,128)(2,1)S(1)} async-done(((bf16[64,16,128]{2,1,0:T(8,128)(2,1)}), bf16[64,16,128]{2,1,0:T(8,128)(2,1)S(1)}, u32[]{:S(2)}, u32[]{:S(2)}) %all-to-all-start.1) | async-done | bytes 262176 | tf_op jit(solution)/shard_map/all_to_all | solution.py:215
  55.8 0.7 shard_map.127
  56.5 14.2 %all-to-all-start.2 = ((bf16[16,16,128]{2,1,0:T(8,128)(2,1)}), bf16[16,16,128]{2,1,0:T(8,128)(2,1)S(1)}, u32[]{:S(2)}, u32[]{:S(2)}) async-start(bf16[16,16,128]{2,1,0:T(8,128)(2,1)} %bitcast.13), calls=%async_computation.2 | async-start | bytes 131072 | tf_op jit(solution)/shard_map/all_to_all | solution.py:215
  70.7 0.0 collective-permute-done.4.came
  70.7 0.6 shard_map.125
  71.3 0.0 collective-permute-done.3.came
  71.3 0.6 shard_map.126
  72.0 4.0 %collective-permute-start.5 = (bf16[256,256]{1,0:T(8,128)(2,1)S(1)}, bf16[256,256]{1,0:T(8,128)(2,1)S(1)}, u32[]{:S(2)}, u32[]{:S(2)}) collective-permute-start(bf16[256,256]{1,0:T(8,128)(2,1)S(1)} %get-tuple-element.36.refs_1_), channel_id=1, source_target_pairs={{0,4},{1,5},{2,6},{3,7},{4,0},{5,1},{6,2},{7,3},{8,12},{9,13},{10,... | collective-permute-start | bytes 393224 | tf_op jit(solution)/shard_map/ppermute | solution.py:211
  76.0 1.3 %collective-permute-start.7 = (bf16[128,256]{1,0:T(8,128)(2,1)S(1)}, bf16[128,256]{1,0:T(8,128)(2,1)S(1)}, u32[]{:S(2)}, u32[]{:S(2)}) collective-permute-start(bf16[128,256]{1,0:T(8,128)(2,1)S(1)} %get-tuple-element.35.rest_0_), channel_id=1, source_target_pairs={{16,0},{24,8},{32,16},{40,24},{48,32},{56,40},{64,48},{72,56},{80,... | collective-permute-start | bytes 196616 | tf_op jit(solution)/shard_map/ppermute | solution.py:207
  77.3 4.0 %collective-permute-start.8 = (bf16[128,256]{1,0:T(8,128)(2,1)S(1)}, bf16[128,256]{1,0:T(8,128)(2,1)S(1)}, u32[]{:S(2)}, u32[]{:S(2)}) collective-permute-start(bf16[128,256]{1,0:T(8,128)(2,1)S(1)} %get-tuple-element.40), channel_id=1, source_target_pairs={{0,16},{8,24},{16,32},{24,40},{32,48},{40,56},{48,64},{56,72},{64,... | collective-permute-start | bytes 196616 | tf_op jit(solution)/shard_map/ppermute | solution.py:207
  81.3 1.0 all-to-all-done.2
  82.3 0.7 shard_map.128.rest_0_
  83.0 9.9 %all-to-all-start.3 = ((bf16[64,16,128]{2,1,0:T(8,128)(2,1)}), bf16[64,16,128]{2,1,0:T(8,128)(2,1)S(1)}, u32[]{:S(2)}, u32[]{:S(2)}) async-start(bf16[64,16,128]{2,1,0:T(8,128)(2,1)} %bitcast.15), calls=%async_computation.3 | async-start | bytes 524288 | tf_op jit(solution)/shard_map/all_to_all | solution.py:215
  92.9 0.0 collective-permute-done.5.came
  92.9 0.0 copy-start.5
  92.9 0.6 shard_map.129
  93.5 4.2 %collective-permute-start.6 = (bf16[128,256]{1,0:T(8,128)(2,1)S(1)}, bf16[128,256]{1,0:T(8,128)(2,1)S(1)}, u32[]{:S(2)}, u32[]{:S(2)}) collective-permute-start(bf16[128,256]{1,0:T(8,128)(2,1)S(1)} %get-tuple-element.38), channel_id=1, source_target_pairs={{0,2},{1,3},{2,0},{3,1},{4,6},{5,7},{6,4},{7,5},{8,10},{9,11},{10,... | collective-permute-start | bytes 196616 | tf_op jit(solution)/shard_map/ppermute | solution.py:211
  97.7 0.0 collective-permute-done.8.high
  97.7 0.0 collective-permute-done.7.low
  97.7 0.8 shard_map.131
  98.6 5.4 %collective-permute-done.6.came = bf16[128,256]{1,0:T(8,128)(2,1)S(1)} collective-permute-done((bf16[128,256]{1,0:T(8,128)(2,1)S(1)}, bf16[128,256]{1,0:T(8,128)(2,1)S(1)}, u32[]{:S(2)}, u32[]{:S(2)}) %collective-permute-start.6) | collective-permute-done | bytes 65568 | tf_op jit(solution)/shard_map/ppermute | solution.py:211
  104.0 0.0 copy-done.2
  104.0 0.9 shard_map.130
  104.8 1.1 %all-to-all-done.3 = bf16[64,16,128]{2,1,0:T(8,128)(2,1)S(1)} async-done(((bf16[64,16,128]{2,1,0:T(8,128)(2,1)}), bf16[64,16,128]{2,1,0:T(8,128)(2,1)S(1)}, u32[]{:S(2)}, u32[]{:S(2)}) %all-to-all-start.3) | async-done | bytes 262176 | tf_op jit(solution)/shard_map/all_to_all | solution.py:215
  105.9 0.8 shard_map.132
  (4 shorter events, 0.0 us)
Async XLA Ops:
  2.5 7.8 %copy-start = (bf16[128,256]{1,0:T(8,128)(2,1)S(1)}, bf16[128,256]{1,0:T(8,128)(2,1)}, u32[]{:S(2)}) copy-start(bf16[128,256]{1,0:T(8,128)(2,1)} %features.3) | copy-start | bytes 196612
  2.5 29.0 %copy-start.3 = (bf16[1,1,16,128,128]{4,3,2,1,0:T(8,128)(2,1)S(1)}, bf16[1,1,16,128,128]{4,3,2,1,0:T(8,128)(2,1)}, u32[]{:S(2)}) copy-start(bf16[1,1,16,128,128]{4,3,2,1,0:T(8,128)(2,1)} %param.12) | copy-start | bytes 1572868
  2.5 30.1 %all-to-all-start = ((bf16[8,128,256]{2,1,0:T(8,128)(2,1)}), bf16[8,128,256]{2,1,0:T(8,128)(2,1)S(1)}, u32[]{:S(2)}, u32[]{:S(2)}) async-start(bf16[8,128,256]{2,1,0:T(8,128)(2,1)} %bitcast.9), calls=%async_computation | async-start | bytes 1048576 | tf_op jit(solution)/shard_map/all_to_all | solution.py:215
  10.3 5.4 %collective-permute-start.1 = (bf16[128,256]{1,0:T(8,128)(2,1)S(1)}, bf16[128,256]{1,0:T(8,128)(2,1)S(1)}, u32[]{:S(2)}, u32[]{:S(2)}) collective-permute-start(bf16[128,256]{1,0:T(8,128)(2,1)S(1)} %copy-done), channel_id=1, source_target_pairs={{16,0},{24,8},{32,16},{40,24},{48,32},{56,40},{64,48},{72,56},{80,... | collective-permute-start | bytes 196616 | tf_op jit(solution)/shard_map/ppermute | solution.py:207
  11.6 5.3 %collective-permute-start = (bf16[128,256]{1,0:T(8,128)(2,1)S(1)}, bf16[128,256]{1,0:T(8,128)(2,1)S(1)}, u32[]{:S(2)}, u32[]{:S(2)}) collective-permute-start(bf16[128,256]{1,0:T(8,128)(2,1)S(1)} %copy-done), channel_id=1, source_target_pairs={{0,16},{8,24},{16,32},{24,40},{32,48},{40,56},{48,64},{56,72},{64,... | collective-permute-start | bytes 196616 | tf_op jit(solution)/shard_map/ppermute | solution.py:207
  17.5 14.0 %collective-permute-start.2 = (bf16[256,256]{1,0:T(8,128)(2,1)S(1)}, bf16[256,256]{1,0:T(8,128)(2,1)S(1)}, u32[]{:S(2)}, u32[]{:S(2)}) collective-permute-start(bf16[256,256]{1,0:T(8,128)(2,1)S(1)} %shard_map.121), channel_id=1, source_target_pairs={{0,8},{8,0},{1,9},{9,1},{2,10},{10,2},{3,11},{11,3},{4,12},{12,4},... | collective-permute-start | bytes 393224 | tf_op jit(solution)/shard_map/ppermute | solution.py:211
  31.5 1.2 %copy-start.1 = (bf16[128,256]{1,0:T(8,128)(2,1)S(1)}, bf16[128,256]{1,0:T(8,128)(2,1)}, u32[]{:S(2)}) copy-start(bf16[128,256]{1,0:T(8,128)(2,1)} %cotangent.5) | copy-start | bytes 196612
  33.8 10.0 %copy-start.4 = (bf16[256,256]{1,0:T(8,128)(2,1)S(1)}, bf16[256,256]{1,0:T(8,128)(2,1)}, u32[]{:S(2)}) copy-start(bf16[256,256]{1,0:T(8,128)(2,1)} %neigh_weight.1) | copy-start | bytes 393220
  33.8 22.0 %all-to-all-start.1 = ((bf16[64,16,128]{2,1,0:T(8,128)(2,1)}), bf16[64,16,128]{2,1,0:T(8,128)(2,1)S(1)}, u32[]{:S(2)}, u32[]{:S(2)}) async-start(bf16[64,16,128]{2,1,0:T(8,128)(2,1)} %bitcast.11), calls=%async_computation.1 | async-start | bytes 524288 | tf_op jit(solution)/shard_map/all_to_all | solution.py:215
  45.2 25.5 %collective-permute-start.4 = (bf16[256,256]{1,0:T(8,128)(2,1)S(1)}, bf16[256,256]{1,0:T(8,128)(2,1)S(1)}, u32[]{:S(2)}, u32[]{:S(2)}) collective-permute-start(bf16[256,256]{1,0:T(8,128)(2,1)S(1)} %get-tuple-element.31), channel_id=1, source_target_pairs={{0,8},{8,0},{1,9},{9,1},{2,10},{10,2},{3,11},{11,3},{4,12},{12,4},... | collective-permute-start | bytes 393224 | tf_op jit(solution)/shard_map/ppermute | solution.py:211
  47.5 23.8 %collective-permute-start.3 = (bf16[512,256]{1,0:T(8,128)(2,1)S(1)}, bf16[512,256]{1,0:T(8,128)(2,1)S(1)}, u32[]{:S(2)}, u32[]{:S(2)}) collective-permute-start(bf16[512,256]{1,0:T(8,128)(2,1)S(1)} %get-tuple-element.29), channel_id=1, source_target_pairs={{0,1},{1,0},{2,3},{3,2},{4,5},{5,4},{6,7},{7,6},{8,9},{9,8},{10,11... | collective-permute-start | bytes 786440 | tf_op jit(solution)/shard_map/ppermute | solution.py:211
  56.5 25.8 %all-to-all-start.2 = ((bf16[16,16,128]{2,1,0:T(8,128)(2,1)}), bf16[16,16,128]{2,1,0:T(8,128)(2,1)S(1)}, u32[]{:S(2)}, u32[]{:S(2)}) async-start(bf16[16,16,128]{2,1,0:T(8,128)(2,1)} %bitcast.13), calls=%async_computation.2 | async-start | bytes 131072 | tf_op jit(solution)/shard_map/all_to_all | solution.py:215
  72.0 20.9 %collective-permute-start.5 = (bf16[256,256]{1,0:T(8,128)(2,1)S(1)}, bf16[256,256]{1,0:T(8,128)(2,1)S(1)}, u32[]{:S(2)}, u32[]{:S(2)}) collective-permute-start(bf16[256,256]{1,0:T(8,128)(2,1)S(1)} %get-tuple-element.36.refs_1_), channel_id=1, source_target_pairs={{0,4},{1,5},{2,6},{3,7},{4,0},{5,1},{6,2},{7,3},{8,12},{9,13},{10,... | collective-permute-start | bytes 393224 | tf_op jit(solution)/shard_map/ppermute | solution.py:211
  76.0 21.7 %collective-permute-start.7 = (bf16[128,256]{1,0:T(8,128)(2,1)S(1)}, bf16[128,256]{1,0:T(8,128)(2,1)S(1)}, u32[]{:S(2)}, u32[]{:S(2)}) collective-permute-start(bf16[128,256]{1,0:T(8,128)(2,1)S(1)} %get-tuple-element.35.rest_0_), channel_id=1, source_target_pairs={{16,0},{24,8},{32,16},{40,24},{48,32},{56,40},{64,48},{72,56},{80,... | collective-permute-start | bytes 196616 | tf_op jit(solution)/shard_map/ppermute | solution.py:207
  77.3 20.4 %collective-permute-start.8 = (bf16[128,256]{1,0:T(8,128)(2,1)S(1)}, bf16[128,256]{1,0:T(8,128)(2,1)S(1)}, u32[]{:S(2)}, u32[]{:S(2)}) collective-permute-start(bf16[128,256]{1,0:T(8,128)(2,1)S(1)} %get-tuple-element.40), channel_id=1, source_target_pairs={{0,16},{8,24},{16,32},{24,40},{32,48},{40,56},{48,64},{56,72},{64,... | collective-permute-start | bytes 196616 | tf_op jit(solution)/shard_map/ppermute | solution.py:207
  83.0 22.9 %all-to-all-start.3 = ((bf16[64,16,128]{2,1,0:T(8,128)(2,1)}), bf16[64,16,128]{2,1,0:T(8,128)(2,1)S(1)}, u32[]{:S(2)}, u32[]{:S(2)}) async-start(bf16[64,16,128]{2,1,0:T(8,128)(2,1)} %bitcast.15), calls=%async_computation.3 | async-start | bytes 524288 | tf_op jit(solution)/shard_map/all_to_all | solution.py:215
  92.9 4.8 %copy-start.5 = (bf16[256,256]{1,0:T(8,128)(2,1)S(1)}, bf16[256,256]{1,0:T(8,128)(2,1)}, u32[]{:S(2)}) copy-start(bf16[256,256]{1,0:T(8,128)(2,1)} %self_weight.3) | copy-start | bytes 393220
  93.5 10.5 %collective-permute-start.6 = (bf16[128,256]{1,0:T(8,128)(2,1)S(1)}, bf16[128,256]{1,0:T(8,128)(2,1)S(1)}, u32[]{:S(2)}, u32[]{:S(2)}) collective-permute-start(bf16[128,256]{1,0:T(8,128)(2,1)S(1)} %get-tuple-element.38), channel_id=1, source_target_pairs={{0,2},{1,3},{2,0},{3,1},{4,6},{5,7},{6,4},{7,5},{8,10},{9,11},{10,... | collective-permute-start | bytes 196616 | tf_op jit(solution)/shard_map/ppermute | solution.py:211
  98.6 5.4 %copy-start.2 = (s32[128]{0:T(128)S(1)}, s32[128]{0:T(128)}, u32[]{:S(2)}) copy-start(s32[128]{0:T(128)} %param.16) | copy-start | bytes 1540

commit v6 on v4

--- a/solution.py
+++ b/solution.py
@@ -13,7 +13,8 @@
 HALO = 2
 WIDE = 2 * HALO + 1
 ROW = ("z", "x", "core")
-NEAR = ("x", "core", "y")
+NEAR = ("core", "x", "y")
+PLANE = ("x", "y")
 LIMIT = 48 * 1024 * 1024
 
 VM = pl.BlockSpec(memory_space=pltpu.VMEM)
@@ -177,13 +178,14 @@
     return call(body, half(copies * rows, lanes), [VM] + [HB] * len(after))(value, *after)
 
 
-def finish_body(factor, source, own, neigh):
-    height, lanes = own.shape[0], source.shape[1]
+def finish_body(factor, spot, mine, other, own, neigh):
+    height, lanes = own.shape[0], mine.shape[1]
     for at in range(2):
-        for first, grad in ((at, own), (at + 2, neigh)):
-            grad[:, at * lanes : (at + 1) * lanes] = (
-                source[first * height : (first + 1) * height, :].astype(jnp.float32) * factor
-            )
+        rows, columns = slice(at * height, (at + 1) * height), slice(at * lanes, (at + 1) * lanes)
+        first = mine[rows, :].astype(jnp.float32) * factor
+        second = other[rows, :].astype(jnp.float32) * factor
+        own[:, columns] = jnp.where(spot[0] == 0, first, second)
+        neigh[:, columns] = jnp.where(spot[0] == 0, second, first)
 
 
 def output_body(came, held, degree, features, self_weight, neigh_weight, out):
@@ -294,8 +296,9 @@
 
     came = crossed(sent, "y", 4)
     low, high = passed_along(low, -2), passed_along(high, 2)
-    grads = fold_spread(joined, far, near, after=[sent])
-    gathered = exchange(grads, NEAR)
+    grads = fold_spread(joined, far, near // 2, after=[sent])
+    mine = exchange(grads, PLANE)
+    other = crossed(mine, "core", 1)
 
     sent, kept = call(
         halve_body(blk, 3),
@@ -311,8 +314,8 @@
         came, kept, degree, features, self_weight, neigh_weight
     )
     self_grad, neigh_grad = call(
-        functools.partial(finish_body, factor), [full(width, width)] * 2, [VM]
-    )(gathered)
+        functools.partial(finish_body, factor), [full(width, width)] * 2, [SM] + [VM] * 2
+    )(spot, mine, other)
     return (output, feature_grad, self_grad, neigh_grad)
 
 

time: 107 us -> 108 us (level)
    ppermute x5 -> x6, waiting for transfers between devices: 6.7 us -> 1.37 us  [crossed(): lax.ppermute(value, axis, [(at, at ^ flip) for at in range(lax.axis_size(...]
    all_to_all x4, waiting for transfers between devices: 6.32 us -> 11.1 us  [exchange(): return lax.all_to_all(value, axes, 0, 0, tiled=True)]
    ppermute x5 -> x6, starting transfers between devices: 26.9 us -> 30.4 us  [crossed(): lax.ppermute(value, axis, [(at, at ^ flip) for at in range(lax.axis_size(...]
    all_to_all x4, starting transfers between devices: 41.4 us -> 38.8 us  [exchange(): return lax.all_to_all(value, axes, 0, 0, tiled=True)]
  transfers between devices with their start and end apart: 13 -> 14, of which waited for: 7 -> 7; matrix products, arithmetic and copies ran while one was open for 0% -> 0% of each run, Pallas kernels for 7% -> 7%
where the time goes in v6:
time: 108 us; the launch traced here: 107 us
  starting transfers between devices  79.8 us (74%)
  waiting for transfers between devices  13.7 us (13%)
  Pallas kernels  12.2 us (11%)
  between operations  1.56 us (1%)
    all_to_all x4, starting transfers between devices, exchange(): return lax.all_to_all(value, axes, 0, 0, tiled=True)  38.8 us
    ppermute x6, starting transfers between devices, crossed(): lax.ppermute(value, axis, [(at, at ^ flip) for at in range(lax.axis_size(...  30.4 us
    all_to_all x4, waiting for transfers between devices, exchange(): return lax.all_to_all(value, axes, 0, 0, tiled=True)  11.1 us
    ppermute x4, starting transfers between devices, passed_along(): lax.ppermute(value, ROW, [(source, source + steps) for source in range(le...  10.6 us
  transfers between devices with their start and end apart: 14, of which 7 were waited for; matrix products, arithmetic and copies ran while one was open for 0% of the time, Pallas kernels for 7%

profile of v6, /device:TPU:1, one launch (start us, length us, event | category | flops | bytes accessed | tf_op | source)
XLA Modules:
  0.0 107.4 jit_solution(11386295279703893998)
XLA Ops:
  0.6 1.9 %shard_map.120 = (bf16[1024,256]{1,0:T(8,128)(2,1)}, s32[16]{0:T(128)S(1)}, s32[16]{0:T(128)S(1)}) custom-call(s32[1,128]{1,0:T(1,128)} %bitcast.25, bf16[128,256]{1,0:T(8,128)(2,1)} %cotangent.5, s32[16]{0:T(128)} %bitcast.29, s32[16]{0:T(128)} %bitcast.30), custom_call_target="tpu_custom_call" | custom-call | tf_op jit(solution)/shard_map/pallas_call | solution.py:239
  2.5 0.0 copy-start
  2.5 0.0 copy-start.3
  2.6 7.8 %all-to-all-start = ((bf16[8,128,256]{2,1,0:T(8,128)(2,1)}), bf16[8,128,256]{2,1,0:T(8,128)(2,1)S(1)}, u32[]{:S(2)}, u32[]{:S(2)}) async-start(bf16[8,128,256]{2,1,0:T(8,128)(2,1)} %bitcast.9), calls=%async_computation | async-start | bytes 1048576 | tf_op jit(solution)/shard_map/all_to_all | solution.py:215
  10.4 0.0 copy-done
  10.4 1.3 %collective-permute-start.1 = (bf16[128,256]{1,0:T(8,128)(2,1)S(1)}, bf16[128,256]{1,0:T(8,128)(2,1)S(1)}, u32[]{:S(2)}, u32[]{:S(2)}) collective-permute-start(bf16[128,256]{1,0:T(8,128)(2,1)S(1)} %copy-done), channel_id=1, source_target_pairs={{16,0},{24,8},{32,16},{40,24},{48,32},{56,40},{64,48},{72,56},{80,... | collective-permute-start | bytes 196616 | tf_op jit(solution)/shard_map/ppermute | solution.py:207
  11.7 4.0 %collective-permute-start = (bf16[128,256]{1,0:T(8,128)(2,1)S(1)}, bf16[128,256]{1,0:T(8,128)(2,1)S(1)}, u32[]{:S(2)}, u32[]{:S(2)}) collective-permute-start(bf16[128,256]{1,0:T(8,128)(2,1)S(1)} %copy-done), channel_id=1, source_target_pairs={{0,16},{8,24},{16,32},{24,40},{32,48},{40,56},{48,64},{56,72},{64,... | collective-permute-start | bytes 196616 | tf_op jit(solution)/shard_map/ppermute | solution.py:207
  15.7 0.1 pad_add_fusion.spot
  15.7 0.0 collective-permute-done.1.above.f4
  15.7 1.2 %collective-permute-done.below.f0 = bf16[128,256]{1,0:T(8,128)(2,1)S(1)} collective-permute-done((bf16[128,256]{1,0:T(8,128)(2,1)S(1)}, bf16[128,256]{1,0:T(8,128)(2,1)S(1)}, u32[]{:S(2)}, u32[]{:S(2)}) %collective-permute-start) | collective-permute-done | bytes 65568 | tf_op jit(solution)/shard_map/ppermute | solution.py:207
  17.0 0.6 shard_map.121
  17.5 13.0 %collective-permute-start.2 = (bf16[256,256]{1,0:T(8,128)(2,1)S(1)}, bf16[256,256]{1,0:T(8,128)(2,1)S(1)}, u32[]{:S(2)}, u32[]{:S(2)}) collective-permute-start(bf16[256,256]{1,0:T(8,128)(2,1)S(1)} %shard_map.121), channel_id=1, source_target_pairs={{0,8},{8,0},{1,9},{9,1},{2,10},{10,2},{3,11},{11,3},{4,12},{12,4},... | collective-permute-start | bytes 393224 | tf_op jit(solution)/shard_map/ppermute | solution.py:211
  31.2 0.3 collective-permute-done.2.pair
  31.6 0.0 copy-done.3
  31.6 1.1 %shard_map.122 = (bf16[1024,256]{1,0:T(8,128)(2,1)S(1)}, bf16[512,256]{1,0:T(8,128)(2,1)S(1)}, bf16[512,256]{1,0:T(8,128)(2,1)S(1)}) custom-call(s32[16]{0:T(128)S(1)} %get-tuple-element.24.rows, s32[16]{0:T(128)S(1)} %get-tuple-element.25.bands, s32[1]{0:T(128)} %bitcast.17.count, s32[4]{0:T(128)S(1)} %pad_add_fusion.spot, ...), custom_call_target="tpu_custom_call" | custom-call | flops 4000000000 | bytes 1900544 | tf_op jit(solution)/shard_map/pallas_call | solution.py:254
  32.7 0.0 all-to-all-done
  32.7 0.0 copy-done.1
  32.7 1.1 %shard_map.123.after = bf16[1024,128]{1,0:T(8,128)(2,1)} custom-call(bf16[128,256]{1,0:T(8,128)(2,1)S(1)} %copy-done, bf16[128,256]{1,0:T(8,128)(2,1)S(1)} %copy-done.1, bf16[1024,256]{1,0:T(8,128)(2,1)S(1)} %get-tuple-element.27.partial, bf16[1024,256]{1,0:T(8,128)(2,1)S(1)} %bitcast.19), custom_call_target="tpu_custom_call" | custom-call | flops 150994944 | bytes 1179648 | tf_op jit(solution)/shard_map/pallas_call | solution.py:265
  33.8 10.1 %all-to-all-start.1 = ((bf16[64,16,128]{2,1,0:T(8,128)(2,1)}), bf16[64,16,128]{2,1,0:T(8,128)(2,1)S(1)}, u32[]{:S(2)}, u32[]{:S(2)}) async-start(bf16[64,16,128]{2,1,0:T(8,128)(2,1)} %bitcast.11), calls=%async_computation.1 | async-start | bytes 524288 | tf_op jit(solution)/shard_map/all_to_all | solution.py:215
  43.9 1.4 %shard_map.124 = (bf16[128,256]{1,0:T(8,128)(2,1)S(1)}, bf16[256,256]{1,0:T(8,128)(2,1)S(1)}, bf16[128,256]{1,0:T(8,128)(2,1)S(1)}, bf16[128,256]{1,0:T(8,128)(2,1)S(1)}, bf16[512,256]{1,0:T(8,128)(2,1)S(1)}) custom-call(s32[16]{0:T(128)S(1)} %get-tuple-element.24.rows, s32[16]{0:T(128)S(1)} %get-tuple-element.25.bands, ...), custom_call_target="tpu_custom_call", output_to_operand_aliasing={{4}: (7, {})} | custom-call | flops 5000000000 | bytes 1376256 | tf_op jit(solution)/shard_map/pallas_call | solution.py:273
  45.3 3.3 %collective-permute-start.3 = (bf16[512,256]{1,0:T(8,128)(2,1)S(1)}, bf16[512,256]{1,0:T(8,128)(2,1)S(1)}, u32[]{:S(2)}, u32[]{:S(2)}) collective-permute-start(bf16[512,256]{1,0:T(8,128)(2,1)S(1)} %get-tuple-element.29), channel_id=1, source_target_pairs={{0,1},{1,0},{2,3},{3,2},{4,5},{5,4},{6,7},{7,6},{8,9},{9,8},{10,11... | collective-permute-start | bytes 786440 | tf_op jit(solution)/shard_map/ppermute | solution.py:211
  48.6 2.5 %collective-permute-start.5 = (bf16[256,256]{1,0:T(8,128)(2,1)S(1)}, bf16[256,256]{1,0:T(8,128)(2,1)S(1)}, u32[]{:S(2)}, u32[]{:S(2)}) collective-permute-start(bf16[256,256]{1,0:T(8,128)(2,1)S(1)} %get-tuple-element.33), channel_id=1, source_target_pairs={{0,8},{8,0},{1,9},{9,1},{2,10},{10,2},{3,11},{11,3},{4,12},{12,4},... | collective-permute-start | bytes 393224 | tf_op jit(solution)/shard_map/ppermute | solution.py:211
  51.0 1.0 collective-permute-done.5.came
  52.0 0.6 shard_map.126
  52.6 4.7 %all-to-all-done.1 = bf16[64,16,128]{2,1,0:T(8,128)(2,1)S(1)} async-done(((bf16[64,16,128]{2,1,0:T(8,128)(2,1)}), bf16[64,16,128]{2,1,0:T(8,128)(2,1)S(1)}, u32[]{:S(2)}, u32[]{:S(2)}) %all-to-all-start.1) | async-done | bytes 262176 | tf_op jit(solution)/shard_map/all_to_all | solution.py:215
  57.3 0.7 shard_map.127
  58.0 14.2 %all-to-all-start.2 = ((bf16[16,16,128]{2,1,0:T(8,128)(2,1)}), bf16[16,16,128]{2,1,0:T(8,128)(2,1)S(1)}, u32[]{:S(2)}, u32[]{:S(2)}) async-start(bf16[16,16,128]{2,1,0:T(8,128)(2,1)} %bitcast.13), calls=%async_computation.2 | async-start | bytes 131072 | tf_op jit(solution)/shard_map/all_to_all | solution.py:215
  72.2 0.0 collective-permute-done.3.came
  72.2 0.6 shard_map.125
  72.8 2.9 %collective-permute-start.4 = (bf16[256,256]{1,0:T(8,128)(2,1)S(1)}, bf16[256,256]{1,0:T(8,128)(2,1)S(1)}, u32[]{:S(2)}, u32[]{:S(2)}) collective-permute-start(bf16[256,256]{1,0:T(8,128)(2,1)S(1)} %get-tuple-element.31.refs_1_), channel_id=1, source_target_pairs={{0,4},{1,5},{2,6},{3,7},{4,0},{5,1},{6,2},{7,3},{8,12},{9,13},{10,... | collective-permute-start | bytes 393224 | tf_op jit(solution)/shard_map/ppermute | solution.py:211
  75.7 1.3 %collective-permute-start.7 = (bf16[128,256]{1,0:T(8,128)(2,1)S(1)}, bf16[128,256]{1,0:T(8,128)(2,1)S(1)}, u32[]{:S(2)}, u32[]{:S(2)}) collective-permute-start(bf16[128,256]{1,0:T(8,128)(2,1)S(1)} %get-tuple-element.37.refs_1_), channel_id=1, source_target_pairs={{16,0},{24,8},{32,16},{40,24},{48,32},{56,40},{64,48},{72,56},{80,... | collective-permute-start | bytes 196616 | tf_op jit(solution)/shard_map/ppermute | solution.py:207
  77.0 4.0 %collective-permute-start.8 = (bf16[128,256]{1,0:T(8,128)(2,1)S(1)}, bf16[128,256]{1,0:T(8,128)(2,1)S(1)}, u32[]{:S(2)}, u32[]{:S(2)}) collective-permute-start(bf16[128,256]{1,0:T(8,128)(2,1)S(1)} %get-tuple-element.40), channel_id=1, source_target_pairs={{0,16},{8,24},{16,32},{24,40},{32,48},{40,56},{48,64},{56,72},{64,... | collective-permute-start | bytes 196616 | tf_op jit(solution)/shard_map/ppermute | solution.py:207
  81.0 2.8 %all-to-all-done.2 = bf16[16,16,128]{2,1,0:T(8,128)(2,1)S(1)} async-done(((bf16[16,16,128]{2,1,0:T(8,128)(2,1)}), bf16[16,16,128]{2,1,0:T(8,128)(2,1)S(1)}, u32[]{:S(2)}, u32[]{:S(2)}) %all-to-all-start.2) | async-done | bytes 65568 | tf_op jit(solution)/shard_map/all_to_all | solution.py:215
  83.8 0.7 shard_map.128.rest_0_
  84.4 6.7 %all-to-all-start.3 = ((bf16[32,16,128]{2,1,0:T(8,128)(2,1)}), bf16[32,16,128]{2,1,0:T(8,128)(2,1)S(1)}, u32[]{:S(2)}, u32[]{:S(2)}) async-start(bf16[32,16,128]{2,1,0:T(8,128)(2,1)} %bitcast.15), calls=%async_computation.3 | async-start | bytes 262144 | tf_op jit(solution)/shard_map/all_to_all | solution.py:215
  91.2 0.0 collective-permute-done.4.came
  91.2 0.0 copy-start.5
  91.2 0.6 shard_map.129
  91.8 4.0 %collective-permute-start.6 = (bf16[128,256]{1,0:T(8,128)(2,1)S(1)}, bf16[128,256]{1,0:T(8,128)(2,1)S(1)}, u32[]{:S(2)}, u32[]{:S(2)}) collective-permute-start(bf16[128,256]{1,0:T(8,128)(2,1)S(1)} %get-tuple-element.38), channel_id=1, source_target_pairs={{0,2},{1,3},{2,0},{3,1},{4,6},{5,7},{6,4},{7,5},{8,10},{9,11},{10,... | collective-permute-start | bytes 196616 | tf_op jit(solution)/shard_map/ppermute | solution.py:211
  95.8 0.0 collective-permute-done.8.high
  95.8 0.0 collective-permute-done.7.low
  95.9 0.8 shard_map.131
  96.7 3.6 %all-to-all-done.3 = bf16[32,16,128]{2,1,0:T(8,128)(2,1)S(1)} async-done(((bf16[32,16,128]{2,1,0:T(8,128)(2,1)}), bf16[32,16,128]{2,1,0:T(8,128)(2,1)S(1)}, u32[]{:S(2)}, u32[]{:S(2)}) %all-to-all-start.3) | async-done | bytes 131104 | tf_op jit(solution)/shard_map/all_to_all | solution.py:215
  100.3 4.7 %collective-permute-start.9 = (bf16[512,128]{1,0:T(8,128)(2,1)S(1)}, bf16[512,128]{1,0:T(8,128)(2,1)S(1)}, u32[]{:S(2)}, u32[]{:S(2)}) collective-permute-start(bf16[512,128]{1,0:T(8,128)(2,1)S(1)} %bitcast.22), channel_id=1, source_target_pairs={{0,8},{8,0},{1,9},{9,1},{2,10},{10,2},{3,11},{11,3},{4,12},{12,4},... | collective-permute-start | bytes 393224 | tf_op jit(solution)/shard_map/ppermute | solution.py:211
  105.1 0.0 collective-permute-done.6.came
  105.1 0.9 shard_map.130
  105.9 0.1 collective-permute-done.9.other
  106.0 1.4 %shard_map.132 = (f32[256,256]{1,0:T(8,128)}, f32[256,256]{1,0:T(8,128)}) custom-call(s32[4]{0:T(128)S(1)} %pad_add_fusion.spot, bf16[512,128]{1,0:T(8,128)(2,1)S(1)} %bitcast.23, bf16[512,128]{1,0:T(8,128)(2,1)S(1)} %collective-permute-done.9.other), custom_call_target="tpu_custom_call" | custom-call | tf_op jit(solution)/shard_map/pallas_call | solution.py:316
  (6 shorter events, 0.0 us)
Async XLA Ops:
  2.5 7.8 %copy-start = (bf16[128,256]{1,0:T(8,128)(2,1)S(1)}, bf16[128,256]{1,0:T(8,128)(2,1)}, u32[]{:S(2)}) copy-start(bf16[128,256]{1,0:T(8,128)(2,1)} %features.3) | copy-start | bytes 196612
  2.5 29.0 %copy-start.3 = (bf16[1,1,16,128,128]{4,3,2,1,0:T(8,128)(2,1)S(1)}, bf16[1,1,16,128,128]{4,3,2,1,0:T(8,128)(2,1)}, u32[]{:S(2)}) copy-start(bf16[1,1,16,128,128]{4,3,2,1,0:T(8,128)(2,1)} %param.12) | copy-start | bytes 1572868
  2.6 30.1 %all-to-all-start = ((bf16[8,128,256]{2,1,0:T(8,128)(2,1)}), bf16[8,128,256]{2,1,0:T(8,128)(2,1)S(1)}, u32[]{:S(2)}, u32[]{:S(2)}) async-start(bf16[8,128,256]{2,1,0:T(8,128)(2,1)} %bitcast.9), calls=%async_computation | async-start | bytes 1048576 | tf_op jit(solution)/shard_map/all_to_all | solution.py:215
  10.4 5.4 %collective-permute-start.1 = (bf16[128,256]{1,0:T(8,128)(2,1)S(1)}, bf16[128,256]{1,0:T(8,128)(2,1)S(1)}, u32[]{:S(2)}, u32[]{:S(2)}) collective-permute-start(bf16[128,256]{1,0:T(8,128)(2,1)S(1)} %copy-done), channel_id=1, source_target_pairs={{16,0},{24,8},{32,16},{40,24},{48,32},{56,40},{64,48},{72,56},{80,... | collective-permute-start | bytes 196616 | tf_op jit(solution)/shard_map/ppermute | solution.py:207
  11.7 5.3 %collective-permute-start = (bf16[128,256]{1,0:T(8,128)(2,1)S(1)}, bf16[128,256]{1,0:T(8,128)(2,1)S(1)}, u32[]{:S(2)}, u32[]{:S(2)}) collective-permute-start(bf16[128,256]{1,0:T(8,128)(2,1)S(1)} %copy-done), channel_id=1, source_target_pairs={{0,16},{8,24},{16,32},{24,40},{32,48},{40,56},{48,64},{56,72},{64,... | collective-permute-start | bytes 196616 | tf_op jit(solution)/shard_map/ppermute | solution.py:207
  17.5 14.0 %collective-permute-start.2 = (bf16[256,256]{1,0:T(8,128)(2,1)S(1)}, bf16[256,256]{1,0:T(8,128)(2,1)S(1)}, u32[]{:S(2)}, u32[]{:S(2)}) collective-permute-start(bf16[256,256]{1,0:T(8,128)(2,1)S(1)} %shard_map.121), channel_id=1, source_target_pairs={{0,8},{8,0},{1,9},{9,1},{2,10},{10,2},{3,11},{11,3},{4,12},{12,4},... | collective-permute-start | bytes 393224 | tf_op jit(solution)/shard_map/ppermute | solution.py:211
  31.6 1.2 %copy-start.1 = (bf16[128,256]{1,0:T(8,128)(2,1)S(1)}, bf16[128,256]{1,0:T(8,128)(2,1)}, u32[]{:S(2)}) copy-start(bf16[128,256]{1,0:T(8,128)(2,1)} %cotangent.5) | copy-start | bytes 196612
  33.8 10.1 %copy-start.4 = (bf16[256,256]{1,0:T(8,128)(2,1)S(1)}, bf16[256,256]{1,0:T(8,128)(2,1)}, u32[]{:S(2)}) copy-start(bf16[256,256]{1,0:T(8,128)(2,1)} %neigh_weight.1) | copy-start | bytes 393220
  33.8 23.5 %all-to-all-start.1 = ((bf16[64,16,128]{2,1,0:T(8,128)(2,1)}), bf16[64,16,128]{2,1,0:T(8,128)(2,1)S(1)}, u32[]{:S(2)}, u32[]{:S(2)}) async-start(bf16[64,16,128]{2,1,0:T(8,128)(2,1)} %bitcast.11), calls=%async_computation.1 | async-start | bytes 524288 | tf_op jit(solution)/shard_map/all_to_all | solution.py:215
  45.3 26.9 %collective-permute-start.3 = (bf16[512,256]{1,0:T(8,128)(2,1)S(1)}, bf16[512,256]{1,0:T(8,128)(2,1)S(1)}, u32[]{:S(2)}, u32[]{:S(2)}) collective-permute-start(bf16[512,256]{1,0:T(8,128)(2,1)S(1)} %get-tuple-element.29), channel_id=1, source_target_pairs={{0,1},{1,0},{2,3},{3,2},{4,5},{5,4},{6,7},{7,6},{8,9},{9,8},{10,11... | collective-permute-start | bytes 786440 | tf_op jit(solution)/shard_map/ppermute | solution.py:211
  48.6 3.5 %collective-permute-start.5 = (bf16[256,256]{1,0:T(8,128)(2,1)S(1)}, bf16[256,256]{1,0:T(8,128)(2,1)S(1)}, u32[]{:S(2)}, u32[]{:S(2)}) collective-permute-start(bf16[256,256]{1,0:T(8,128)(2,1)S(1)} %get-tuple-element.33), channel_id=1, source_target_pairs={{0,8},{8,0},{1,9},{9,1},{2,10},{10,2},{3,11},{11,3},{4,12},{12,4},... | collective-permute-start | bytes 393224 | tf_op jit(solution)/shard_map/ppermute | solution.py:211
  58.0 25.8 %all-to-all-start.2 = ((bf16[16,16,128]{2,1,0:T(8,128)(2,1)}), bf16[16,16,128]{2,1,0:T(8,128)(2,1)S(1)}, u32[]{:S(2)}, u32[]{:S(2)}) async-start(bf16[16,16,128]{2,1,0:T(8,128)(2,1)} %bitcast.13), calls=%async_computation.2 | async-start | bytes 131072 | tf_op jit(solution)/shard_map/all_to_all | solution.py:215
  72.8 18.4 %collective-permute-start.4 = (bf16[256,256]{1,0:T(8,128)(2,1)S(1)}, bf16[256,256]{1,0:T(8,128)(2,1)S(1)}, u32[]{:S(2)}, u32[]{:S(2)}) collective-permute-start(bf16[256,256]{1,0:T(8,128)(2,1)S(1)} %get-tuple-element.31.refs_1_), channel_id=1, source_target_pairs={{0,4},{1,5},{2,6},{3,7},{4,0},{5,1},{6,2},{7,3},{8,12},{9,13},{10,... | collective-permute-start | bytes 393224 | tf_op jit(solution)/shard_map/ppermute | solution.py:211
  75.7 20.2 %collective-permute-start.7 = (bf16[128,256]{1,0:T(8,128)(2,1)S(1)}, bf16[128,256]{1,0:T(8,128)(2,1)S(1)}, u32[]{:S(2)}, u32[]{:S(2)}) collective-permute-start(bf16[128,256]{1,0:T(8,128)(2,1)S(1)} %get-tuple-element.37.refs_1_), channel_id=1, source_target_pairs={{16,0},{24,8},{32,16},{40,24},{48,32},{56,40},{64,48},{72,56},{80,... | collective-permute-start | bytes 196616 | tf_op jit(solution)/shard_map/ppermute | solution.py:207
  77.0 18.8 %collective-permute-start.8 = (bf16[128,256]{1,0:T(8,128)(2,1)S(1)}, bf16[128,256]{1,0:T(8,128)(2,1)S(1)}, u32[]{:S(2)}, u32[]{:S(2)}) collective-permute-start(bf16[128,256]{1,0:T(8,128)(2,1)S(1)} %get-tuple-element.40), channel_id=1, source_target_pairs={{0,16},{8,24},{16,32},{24,40},{32,48},{40,56},{48,64},{56,72},{64,... | collective-permute-start | bytes 196616 | tf_op jit(solution)/shard_map/ppermute | solution.py:207
  84.4 15.9 %all-to-all-start.3 = ((bf16[32,16,128]{2,1,0:T(8,128)(2,1)}), bf16[32,16,128]{2,1,0:T(8,128)(2,1)S(1)}, u32[]{:S(2)}, u32[]{:S(2)}) async-start(bf16[32,16,128]{2,1,0:T(8,128)(2,1)} %bitcast.15), calls=%async_computation.3 | async-start | bytes 262144 | tf_op jit(solution)/shard_map/all_to_all | solution.py:215
  91.2 4.7 %copy-start.5 = (bf16[256,256]{1,0:T(8,128)(2,1)S(1)}, bf16[256,256]{1,0:T(8,128)(2,1)}, u32[]{:S(2)}) copy-start(bf16[256,256]{1,0:T(8,128)(2,1)} %self_weight.3) | copy-start | bytes 393220
  91.8 13.3 %collective-permute-start.6 = (bf16[128,256]{1,0:T(8,128)(2,1)S(1)}, bf16[128,256]{1,0:T(8,128)(2,1)S(1)}, u32[]{:S(2)}, u32[]{:S(2)}) collective-permute-start(bf16[128,256]{1,0:T(8,128)(2,1)S(1)} %get-tuple-element.38), channel_id=1, source_target_pairs={{0,2},{1,3},{2,0},{3,1},{4,6},{5,7},{6,4},{7,5},{8,10},{9,11},{10,... | collective-permute-start | bytes 196616 | tf_op jit(solution)/shard_map/ppermute | solution.py:211
  100.3 4.7 %copy-start.2 = (s32[128]{0:T(128)S(1)}, s32[128]{0:T(128)}, u32[]{:S(2)}) copy-start(s32[128]{0:T(128)} %param.16) | copy-start | bytes 1540
  100.3 5.7 %collective-permute-start.9 = (bf16[512,128]{1,0:T(8,128)(2,1)S(1)}, bf16[512,128]{1,0:T(8,128)(2,1)S(1)}, u32[]{:S(2)}, u32[]{:S(2)}) collective-permute-start(bf16[512,128]{1,0:T(8,128)(2,1)S(1)} %bitcast.22), channel_id=1, source_target_pairs={{0,8},{8,0},{1,9},{9,1},{2,10},{10,2},{3,11},{11,3},{4,12},{12,4},... | collective-permute-start | bytes 393224 | tf_op jit(solution)/shard_map/ppermute | solution.py:211
